TPU v7x, 128 devices: a whole 4x4x4 slice. The times are simulated.
128 devices in a mesh: seq: 16 (over x_hi, z, core), fsdp: 8 (over y, x_lo).
Axes of the slice: x: 4 (x_hi: 2, x_lo: 2; x = x_hi * 2 + x_lo), y: 4, z: 4, core: 2. Of those that a mesh axis runs over, the one named last changes fastest.
Arguments:
- inputs: bfloat16 [16, 1024, 1024], P('seq', 'fsdp'), may hold values from -6 to 6
- doc_ids: int32 [16, 1024], replicated, may hold values from 0 to 1, as said below
- positions: int32 [16, 1024], P('seq', 'fsdp'), may hold values from 0 to 1023, as said below
- attn_gain: bfloat16 [1024], P('fsdp'), may hold values from 0.5 to 1.5
- query_weight: bfloat16 [1024, 1024], P('fsdp'), may hold values from -0.1875 to 0.1875
- key_weight: bfloat16 [1024, 1024], P('fsdp'), may hold values from -0.1875 to 0.1875
- value_weight: bfloat16 [1024, 1024], P('fsdp'), may hold values from -0.1875 to 0.1875
- query_bias: bfloat16 [1024], P('fsdp'), may hold values from -3 to 3
- key_bias: bfloat16 [1024], P('fsdp'), may hold values from -3 to 3
- value_bias: bfloat16 [1024], P('fsdp'), may hold values from -3 to 3
- out_weight: bfloat16 [1024, 1024], P('fsdp'), may hold values from -0.75 to 0.75
- mlp_gain: bfloat16 [1024], P('fsdp'), may hold values from 0.5 to 1.5
- gate_weight: bfloat16 [1024, 2816], P('fsdp'), may hold values from -0.1875 to 0.1875
- up_weight: bfloat16 [1024, 2816], P('fsdp'), may hold values from -0.1875 to 0.1875
- down_weight: bfloat16 [2816, 1024], P(None, 'fsdp'), may hold values from -0.109375 to 0.109375
- cotangent: bfloat16 [16, 1024, 1024], P('seq', 'fsdp'), may hold values from -6 to 6
Outputs:
- layer_out: bfloat16 [16, 1024, 1024], P('seq', 'fsdp')
- input_grad: float32 [16, 1024, 1024], P('seq', 'fsdp')
- attn_gain_grad: float32 [1024], P('fsdp')
- query_weight_grad: float32 [1024, 1024], P('fsdp')
- key_weight_grad: float32 [1024, 1024], P('fsdp')
- value_weight_grad: float32 [1024, 1024], P('fsdp')
- query_bias_grad: float32 [1024], P('fsdp')
- key_bias_grad: float32 [1024], P('fsdp')
- value_bias_grad: float32 [1024], P('fsdp')
- out_weight_grad: float32 [1024, 1024], P('fsdp')
- mlp_gain_grad: float32 [1024], P('fsdp')
- gate_weight_grad: float32 [1024, 2816], P('fsdp')
- up_weight_grad: float32 [1024, 2816], P('fsdp')
- down_weight_grad: float32 [2816, 1024], P(None, 'fsdp')
Inputs may be any that keep to these rules, and one draw needn't show every extreme that they name: `doc_ids`: in each sequence the document number is 0 on a leading run of positions and 1 on the rest; in some sequences the run covers the whole sequence. Within a document the positions rise by one from token to token; the first document of each sequence starts at 0, the second at a position below the first's length.
All inputs are finite; a program needn't handle non-finite values.
Results may differ from a plain program's by a relative error of at most 0.023.
Values may be sent and summed in bfloat16 or wider, within the bound.
A program may use at most 256 MiB of HBM per device.

v0:
```python
import math

import jax
import jax.numpy as jnp
from jax import lax
from jax.sharding import PartitionSpec as P

HEADS = 16
HEAD_DIM = 64


EPS = 1e-06
THETA = 1000000.0
NEG = -1000000000.0


def rms_scale(tensor):
    return lax.rsqrt(jnp.mean(tensor * tensor, axis=-1, keepdims=True) + EPS)


def turn_half(tensor):
    half_dim = tensor.shape[-1] // 2
    return jnp.concatenate([-tensor[..., half_dim:], tensor[..., :half_dim]], axis=-1)


def rotary_tables(positions):
    exponent = jnp.arange(HEAD_DIM // 2, dtype=jnp.float32) * (2.0 / HEAD_DIM)
    inverse = jnp.exp(-math.log(THETA) * exponent)
    angles = positions.astype(jnp.float32)[..., None] * inverse
    angles = jnp.concatenate([angles, angles], axis=-1)
    return (jnp.cos(angles)[..., None, :], jnp.sin(angles)[..., None, :])


def matmul_t(left_op, right_op):
    return lax.dot_general(
        left_op, right_op, (((1,), (1,)), ((), ())), preferred_element_type=jnp.float32
    )


def inner_rows(left_op, right_op):
    return lax.dot_general(
        left_op, right_op, (((0,), (0,)), ((), ())), preferred_element_type=jnp.float32
    )


def norm_back(gradient, tensor, scale_vec, gain_vec):
    scaled = gradient * gain_vec
    back_part = scale_vec * scaled - tensor * scale_vec**3 * jnp.mean(
        scaled * tensor, axis=-1, keepdims=True
    )
    return (back_part, jnp.sum(gradient * tensor * scale_vec, axis=0))


def block_scores(query_rows, key_rows, same_doc):
    logit_scores = jnp.einsum(
        "bqhd,bkhd->bhqk", query_rows, key_rows, preferred_element_type=jnp.float32
    ) * (1.0 / math.sqrt(HEAD_DIM))
    return jnp.where(same_doc[:, None], logit_scores, NEG)


def attend_forward(block_in):
    query_rows, key_rows, value_rows, same_doc = block_in
    logit_scores = block_scores(query_rows, key_rows, same_doc)
    row_max = jnp.max(logit_scores, axis=-1, keepdims=True)
    weights = jnp.exp(logit_scores - row_max)
    row_sum = jnp.sum(weights, axis=-1, keepdims=True)
    attention_weights = (weights / row_sum).astype(jnp.bfloat16)
    mixed_out = jnp.einsum(
        "bhqk,bkhd->bqhd", attention_weights, value_rows, preferred_element_type=jnp.float32
    )
    return (mixed_out.astype(jnp.bfloat16), row_max + jnp.log(row_sum))


def attend_backward(block_in):
    query_rows, key_rows, value_rows, same_doc, log_total, grad_mixed = block_in
    logit_scores = block_scores(query_rows, key_rows, same_doc)
    attention_weights = jnp.exp(logit_scores - log_total)
    grad_values = jnp.einsum(
        "bhqk,bqhd->bkhd",
        attention_weights.astype(jnp.bfloat16),
        grad_mixed,
        preferred_element_type=jnp.float32,
    )
    grad_probs = jnp.einsum(
        "bqhd,bkhd->bhqk", grad_mixed, value_rows, preferred_element_type=jnp.float32
    )
    grad_scores = attention_weights * (
        grad_probs - jnp.sum(attention_weights * grad_probs, axis=-1, keepdims=True)
    )
    grad_scores = grad_scores.astype(jnp.bfloat16)
    scaling_factor = 1.0 / math.sqrt(HEAD_DIM)
    grad_queries = (
        jnp.einsum("bhqk,bkhd->bqhd", grad_scores, key_rows, preferred_element_type=jnp.float32)
        * scaling_factor
    )
    grad_keys = (
        jnp.einsum("bhqk,bqhd->bkhd", grad_scores, query_rows, preferred_element_type=jnp.float32)
        * scaling_factor
    )
    return (grad_queries.astype(jnp.bfloat16), grad_keys, grad_values)


def per_device(
    inputs,
    doc_ids,
    positions,
    attn_gain,
    query_weight,
    key_weight,
    value_weight,
    query_bias,
    key_bias,
    value_bias,
    out_weight,
    mlp_gain,
    gate_weight,
    up_weight,
    down_weight,
    cotangent,
):
    gathered = (
        lax.all_gather(attn_gain, "fsdp", axis=0, tiled=True),
        lax.all_gather(query_weight, "fsdp", axis=0, tiled=True),
        lax.all_gather(key_weight, "fsdp", axis=0, tiled=True),
        lax.all_gather(value_weight, "fsdp", axis=0, tiled=True),
        lax.all_gather(query_bias, "fsdp", axis=0, tiled=True),
        lax.all_gather(key_bias, "fsdp", axis=0, tiled=True),
        lax.all_gather(value_bias, "fsdp", axis=0, tiled=True),
        lax.all_gather(out_weight, "fsdp", axis=0, tiled=True),
        lax.all_gather(mlp_gain, "fsdp", axis=0, tiled=True),
        lax.all_gather(gate_weight, "fsdp", axis=0, tiled=True),
        lax.all_gather(up_weight, "fsdp", axis=0, tiled=True),
        lax.all_gather(down_weight, "fsdp", axis=1, tiled=True),
    )
    (
        gain_one,
        query_w,
        key_w,
        value_w,
        query_b,
        key_b,
        value_b,
        out_w,
        gain_two,
        gate_w,
        up_w,
        down_w,
    ) = gathered
    seqs_here, piece_len, model_width = inputs.shape
    seq_size = lax.axis_size("seq")
    fsdp_size = lax.axis_size("fsdp")
    fsdp_index = lax.axis_index("fsdp")
    heads_here = HEADS // seq_size
    tok_rows = seqs_here * piece_len
    flat_in = inputs.reshape(tok_rows, model_width).astype(jnp.float32)
    attn_scale = rms_scale(flat_in)
    gain_attn = gain_one.astype(jnp.float32)
    normed = (flat_in * attn_scale * gain_attn).astype(jnp.bfloat16)
    cos_table, sin_table = rotary_tables(positions.reshape(tok_rows))

    def project(matrix, bias_vec):
        linear = jnp.dot(normed, matrix, preferred_element_type=jnp.float32) + bias_vec.astype(
            jnp.float32
        )
        return linear.reshape(tok_rows, HEADS, HEAD_DIM)

    def rotated(matrix, bias_vec):
        unrotated = project(matrix, bias_vec)
        turned = unrotated * cos_table + turn_half(unrotated) * sin_table
        return turned.astype(jnp.bfloat16).reshape(seqs_here, piece_len, model_width)

    query_rows = rotated(query_w, query_b)
    key_rows = rotated(key_w, key_b)
    value_rows = (
        project(value_w, value_b).astype(jnp.bfloat16).reshape(seqs_here, piece_len, model_width)
    )
    query_heads, key_heads, value_heads = (
        lax.all_to_all(query_rows, "seq", split_axis=2, concat_axis=0, tiled=True),
        lax.all_to_all(key_rows, "seq", split_axis=2, concat_axis=0, tiled=True),
        lax.all_to_all(value_rows, "seq", split_axis=2, concat_axis=0, tiled=True),
    )
    keys_all, values_all = (
        lax.all_gather(key_heads, "fsdp", axis=1, tiled=True),
        lax.all_gather(value_heads, "fsdp", axis=1, tiled=True),
    )
    total_seqs = query_heads.shape[0]
    length = keys_all.shape[1]
    query_docs = lax.dynamic_slice_in_dim(doc_ids, fsdp_index * piece_len, piece_len, 1)
    query_place = fsdp_index * piece_len + jnp.arange(piece_len, dtype=jnp.int32)
    key_place = jnp.arange(length, dtype=jnp.int32)
    same_doc = (query_docs[:, :, None] == doc_ids[:, None, :]) & (
        key_place[None, None, :] <= query_place[None, :, None]
    )

    def split_heads(tensor):
        return tensor.reshape(tensor.shape[0], tensor.shape[1], heads_here, HEAD_DIM)

    def by_block(tensor):
        return tensor.reshape((seqs_here, seq_size) + tensor.shape[1:])

    query_blocks = by_block(split_heads(query_heads))
    key_blocks = by_block(split_heads(keys_all))
    value_blocks = by_block(split_heads(values_all))
    mask_blocks = by_block(same_doc)
    mixed_out, log_total = lax.map(
        attend_forward, (query_blocks, key_blocks, value_blocks, mask_blocks)
    )
    mixed_out = mixed_out.reshape(total_seqs, piece_len, heads_here * HEAD_DIM)
    mixed_tok = lax.all_to_all(mixed_out, "seq", split_axis=0, concat_axis=2, tiled=True)
    attn_rows = mixed_tok.reshape(tok_rows, model_width)
    hidden = flat_in + jnp.dot(attn_rows, out_w, preferred_element_type=jnp.float32)
    mlp_scale = rms_scale(hidden)
    gain_mlp = gain_two.astype(jnp.float32)
    normed_mlp = (hidden * mlp_scale * gain_mlp).astype(jnp.bfloat16)
    gate_val = jnp.dot(normed_mlp, gate_w, preferred_element_type=jnp.float32)
    up_val = jnp.dot(normed_mlp, up_w, preferred_element_type=jnp.float32)
    gate_sigmoid = jax.nn.sigmoid(gate_val)
    gate_silu = gate_val * gate_sigmoid
    active = (gate_silu * up_val).astype(jnp.bfloat16)
    result = hidden + jnp.dot(active, down_w, preferred_element_type=jnp.float32)
    layer_out = result.astype(jnp.bfloat16).reshape(inputs.shape)
    grad_out = cotangent.reshape(tok_rows, model_width)
    grad_active = matmul_t(grad_out, down_w)
    grad_gate = (
        grad_active * up_val * gate_sigmoid * (1.0 + gate_val * (1.0 - gate_sigmoid))
    ).astype(jnp.bfloat16)
    grad_up = (grad_active * gate_silu).astype(jnp.bfloat16)
    grad_mlp = matmul_t(grad_gate, gate_w) + matmul_t(grad_up, up_w)
    back_mlp, grad_gain_two = norm_back(grad_mlp, hidden, mlp_scale, gain_mlp)
    grad_hidden = grad_out.astype(jnp.float32) + back_mlp
    grad_branch = grad_hidden.astype(jnp.bfloat16)
    grad_attn_out = (
        matmul_t(grad_branch, out_w).astype(jnp.bfloat16).reshape(seqs_here, piece_len, model_width)
    )
    grad_mixed = lax.all_to_all(grad_attn_out, "seq", split_axis=2, concat_axis=0, tiled=True)
    grad_query_blk, grad_key_blk, grad_value_blk = lax.map(
        attend_backward,
        (
            query_blocks,
            key_blocks,
            value_blocks,
            mask_blocks,
            log_total,
            by_block(split_heads(grad_mixed)),
        ),
    )
    grad_keys_sum, grad_values_sum = (
        lax.psum_scatter(
            grad_key_blk.reshape(total_seqs, length, heads_here * HEAD_DIM),
            "fsdp",
            scatter_dimension=1,
            tiled=True,
        ),
        lax.psum_scatter(
            grad_value_blk.reshape(total_seqs, length, heads_here * HEAD_DIM),
            "fsdp",
            scatter_dimension=1,
            tiled=True,
        ),
    )
    grad_query_heads = grad_query_blk.reshape(total_seqs, piece_len, heads_here * HEAD_DIM)
    back_query, back_key, back_value = (
        lax.all_to_all(grad_query_heads, "seq", split_axis=0, concat_axis=2, tiled=True),
        lax.all_to_all(
            grad_keys_sum.astype(jnp.bfloat16), "seq", split_axis=0, concat_axis=2, tiled=True
        ),
        lax.all_to_all(
            grad_values_sum.astype(jnp.bfloat16), "seq", split_axis=0, concat_axis=2, tiled=True
        ),
    )

    def unrotate(gradient):
        grad_heads = gradient.astype(jnp.float32).reshape(tok_rows, HEADS, HEAD_DIM)
        reverted = grad_heads * cos_table - turn_half(grad_heads) * sin_table
        return reverted.astype(jnp.bfloat16).reshape(tok_rows, model_width)

    pre_query = unrotate(back_query)
    pre_key = unrotate(back_key)
    pre_value = back_value.reshape(tok_rows, model_width)
    grad_normed = (
        matmul_t(pre_query, query_w) + matmul_t(pre_key, key_w) + matmul_t(pre_value, value_w)
    )
    back_attn, grad_gain_one = norm_back(grad_normed, flat_in, attn_scale, gain_attn)
    input_grad = (grad_hidden + back_attn).reshape(inputs.shape)
    vector_sums = lax.psum(
        (
            grad_gain_one,
            jnp.sum(pre_query.astype(jnp.float32), axis=0),
            jnp.sum(pre_key.astype(jnp.float32), axis=0),
            jnp.sum(pre_value.astype(jnp.float32), axis=0),
            grad_gain_two,
        ),
        ("seq", "fsdp"),
    )
    shard_len = model_width // fsdp_size

    def own_shard(tensor):
        return lax.dynamic_slice_in_dim(tensor, fsdp_index * shard_len, shard_len, 0)

    def permuted(left_op):
        row_count = left_op.shape[1] // (fsdp_size * seq_size)
        return (
            left_op.reshape(tok_rows, fsdp_size, seq_size, row_count)
            .transpose(0, 2, 1, 3)
            .reshape(tok_rows, left_op.shape[1])
        )

    left_ops = (permuted(normed), permuted(attn_rows), permuted(normed_mlp), permuted(grad_out))
    normed_left, attn_left, mlp_left, down_left = left_ops
    qkv_grads = jnp.concatenate([pre_query, pre_key, pre_value], axis=1)
    gate_pair = jnp.concatenate([grad_gate, grad_up], axis=1)
    first_part = inner_rows(normed_left, qkv_grads)
    second = inner_rows(attn_left, grad_branch)
    attn_part = lax.psum_scatter(
        jnp.concatenate([first_part, second], axis=1),
        ("seq", "fsdp"),
        scatter_dimension=0,
        tiled=True,
    )
    first_part = inner_rows(mlp_left, gate_pair)
    second = inner_rows(down_left, active)
    mlp_part = lax.psum_scatter(
        jnp.concatenate([first_part, second], axis=1),
        ("seq", "fsdp"),
        scatter_dimension=0,
        tiled=True,
    )
    attn_part, mlp_part = (
        lax.all_gather(attn_part.astype(jnp.bfloat16), "seq", axis=0, tiled=True).astype(
            attn_part.dtype
        ),
        lax.all_gather(mlp_part.astype(jnp.bfloat16), "seq", axis=0, tiled=True).astype(
            mlp_part.dtype
        ),
    )
    hidden_units = gate_w.shape[1]
    return (
        layer_out,
        input_grad,
        own_shard(vector_sums[0]),
        attn_part[:, :model_width],
        attn_part[:, model_width : 2 * model_width],
        attn_part[:, 2 * model_width : 3 * model_width],
        own_shard(vector_sums[1]),
        own_shard(vector_sums[2]),
        own_shard(vector_sums[3]),
        attn_part[:, 3 * model_width :],
        own_shard(vector_sums[4]),
        mlp_part[:, :hidden_units],
        mlp_part[:, hidden_units : 2 * hidden_units],
        mlp_part[:, 2 * hidden_units :].T,
    )


def solution(mesh):
    return jax.shard_map(
        per_device,
        mesh=mesh,
        in_specs=(
            P("seq", "fsdp", None),
            P(),
            P("seq", "fsdp"),
            P("fsdp"),
            P("fsdp", None),
            P("fsdp", None),
            P("fsdp", None),
            P("fsdp"),
            P("fsdp"),
            P("fsdp"),
            P("fsdp", None),
            P("fsdp"),
            P("fsdp", None),
            P("fsdp", None),
            P(None, "fsdp"),
            P("seq", "fsdp", None),
        ),
        out_specs=(
            P("seq", "fsdp", None),
            P("seq", "fsdp", None),
            P("fsdp"),
            P("fsdp", None),
            P("fsdp", None),
            P("fsdp", None),
            P("fsdp"),
            P("fsdp"),
            P("fsdp"),
            P("fsdp", None),
            P("fsdp"),
            P("fsdp", None),
            P("fsdp", None),
            P(None, "fsdp"),
        ),
        check_vma=False,
    )
```

profile of v0, /device:TPU:1, one launch (start us, length us, event | category | flops | bytes accessed | tf_op | source)
XLA Modules:
  0.0 2493.3 jit_solution(12493699912659709147)
XLA Ops:
  9.5 16.2 all-gather.2
  25.6 12.8 all-gather.4
  38.4 14.7 all-gather.5
  55.3 9.7 all-gather.21.cloned.1.call-done
  65.0 2.2 convolution_add_fusion.4
  67.4 50.6 %all-gather.23.cloned.1.call-done = bf16[1024,1024]{1,0:T(8,128)(2,1)} async-done(((bf16[128,1024]{1,0:T(8,128)(2,1)}), bf16[1024,1024]{1,0:T(8,128)(2,1)}) %all-gather.23.cloned.1.call-update) | async-done | bytes 2097168 | tf_op jit(solution)/shard_map/all_gather | solution.py:124
  118.0 2.1 convolution_add_fusion.3
  122.1 2.2 reduce.14
  124.4 18.8 all_to_all.114
  144.3 12.8 all-gather.3
  157.1 16.8 all-gather.19.cloned.1.call-done
  173.9 2.1 fusion.31
  176.5 2.2 reduce.15
  178.8 18.8 all_to_all.115
  201.9 2.2 reduce.13
  204.8 4.7 all-to-all-start.1
  209.8 11.4 all-to-all-done.1
  221.5 8.9 all-gather.39.cloned.1.call-done
  230.3 4.3 fusion.79
  234.7 3.3 copy-done
  238.0 1.9 fusion
  239.9 45.3 %all-gather.37.cloned.1.call-done = bf16[16,1,1024,64]{2,3,0,1:T(8,128)(2,1)} async-done(((bf16[16,1,128,64]{2,3,0,1:T(8,128)(2,1)}), bf16[16,1,1024,64]{2,3,0,1:T(8,128)(2,1)}) %all-gather.37.cloned.1.call-update) | async-done | bytes 2097168 | tf_op jit(solution)/shard_map/all_gather | solution.py:184
  285.2 6.5 fusion.37
  291.7 8.1 all-to-all-start.3
  299.9 17.7 all-gather.6
  317.6 25.6 %all-gather.25.cloned.1.call-done = bf16[1024,1024]{1,0:T(8,128)(2,1)} async-done(((bf16[128,1024]{1,0:T(8,128)(2,1)}), bf16[1024,1024]{1,0:T(8,128)(2,1)}) %all-gather.25.cloned.1.call-update) | async-done | bytes 2097168 | tf_op jit(solution)/shard_map/all_gather | solution.py:129
  343.2 2.2 multiply_reduce_fusion.3
  345.6 118.2 %all-gather.29.cloned.1.call-done = bf16[1024,2816]{1,0:T(8,128)(2,1)} async-done(((bf16[128,2816]{1,0:T(8,128)(2,1)}), bf16[1024,2816]{1,0:T(8,128)(2,1)}) %all-gather.29.cloned.1.call-update) | async-done | bytes 5767184 | tf_op jit(solution)/shard_map/all_gather | solution.py:132
  463.8 4.7 fusion.81
  468.5 117.2 %all-gather.27.cloned.1.call-done = bf16[1024,2816]{1,0:T(8,128)(2,1)} async-done(((bf16[128,2816]{1,0:T(8,128)(2,1)}), bf16[1024,2816]{1,0:T(8,128)(2,1)}) %all-gather.27.cloned.1.call-update) | async-done | bytes 5767184 | tf_op jit(solution)/shard_map/all_gather | solution.py:131
  585.7 4.7 fusion.80
  590.4 116.5 %all-gather.31.cloned.1.call-done = bf16[2816,1024]{1,0:T(8,128)(2,1)} async-done(((bf16[2816,128]{1,0:T(8,128)(2,1)}), bf16[2816,1024]{1,0:T(8,128)(2,1)}) %all-gather.31.cloned.1.call-update) | async-done | bytes 5767184 | tf_op jit(solution)/shard_map/all_gather | solution.py:133
  706.9 5.8 multiply_convert_fusion.1
  712.8 2.0 fusion.82
  714.8 4.9 multiply_reduce_fusion.1
  721.8 3.1 reduce.16
  725.7 7.2 all-to-all-start.4
  733.2 8.4 all-to-all-done.4
  743.7 6.6 multiply_reduce_fusion
  752.1 2.0 copy-done.2
  754.1 2.7 multiply_bitcast_fusion
  756.8 7.1 fusion.6
  767.7 5.1 fusion.33
  772.9 4.3 all-to-all-start.5
  777.2 3.6 fusion.65
  780.8 67.3 %reduce-scatter.5.cloned.1.call-done = f32[16,128,64]{1,2,0:T(8,128)} async-done(((f32[16,1024,64]{1,2,0:T(8,128)}), f32[16,128,64]{1,2,0:T(8,128)}) %reduce-scatter.5.cloned.1.call-update) | async-done | bytes 524304 | tf_op jit(solution)/shard_map/reduce_scatter | solution.py:248
  849.9 7.4 all-to-all-start.6
  858.9 82.8 %reduce-scatter.7.cloned.1.call-done = f32[16,128,64]{1,2,0:T(8,128)} async-done(((f32[16,1024,64]{1,2,0:T(8,128)}), f32[16,128,64]{1,2,0:T(8,128)}) %reduce-scatter.7.cloned.1.call-update) | async-done | bytes 524304 | tf_op jit(solution)/shard_map/reduce_scatter | solution.py:254
  943.5 7.4 all-to-all-start.7
  954.6 5.0 all-to-all-done.7
  959.6 3.1 fusion.40
  962.7 6.0 pad_maximum_fusion.1
  973.4 6.0 convolution_bitcast_fusion
  979.4 9.5 fusion.15
  988.9 23.2 pad_maximum_fusion
  1012.1 607.7 %reduce-scatter.9.cloned.1.call-done = f32[8,4096]{1,0:T(8,128)} async-done(((f32[1024,4096]{1,0:T(8,128)}), f32[8,4096]{1,0:T(8,128)}) %reduce-scatter.9.cloned.1.call-update) | async-done | bytes 131088 | tf_op jit(solution)/shard_map/reduce_scatter | solution.py:314
  1621.5 760.0 %reduce-scatter.11.cloned.1.call-done = f32[8,8448]{1,0:T(8,128)} async-done(((f32[1024,8448]{1,0:T(8,128)}), f32[8,8448]{1,0:T(8,128)}) %reduce-scatter.11.cloned.1.call-update) | async-done | bytes 270352 | tf_op jit(solution)/shard_map/reduce_scatter | solution.py:322
  2383.1 4.5 fusion.36
  2388.1 1.9 fusion.83
  2390.0 2.5 convolution_add_fusion.1
  2393.5 66.0 %all-reduce = (f32[1024]{0:T(1024)S(1)}, f32[1024]{0:T(1024)S(1)}, f32[1024]{0:T(1024)S(1)}, f32[1024]{0:T(1024)S(1)}, f32[1024]{0:T(1024)S(1)}) all-reduce(f32[1024]{0:T(1024)S(1)} %get-tuple-element.109, f32[1024]{0:T(1024)S(1)} %reduce_sum.115, f32[1024]{0:T(1024)S(1)} %reduce_sum.117, ...), channel_id=1, replica_groups=mesh['seq'=16,'fsdp'=8] {'seq','fsdp'}, use_global_device_ids=true, to_apply=%region_10.11 | all-reduce | flops 5120 | bytes 40960 | tf_op jit(solution)/shard_map/psum | solution.py:285
  2463.4 2.6 fusion.78
  2466.0 12.6 all-gather.35.cloned.1.call-done
  2481.7 2.9 copy.88
  (171 shorter events, 51.6 us)
Async XLA Ops:
  7.2 110.8 %copy-start.3 = (bf16[1,128,1024]{2,1,0:T(8,128)(2,1)S(1)}, bf16[1,128,1024]{2,1,0:T(8,128)(2,1)}, u32[]{:S(2)}) copy-start(bf16[1,128,1024]{2,1,0:T(8,128)(2,1)} %param.16) | copy-start | bytes 786436
  7.2 57.8 %all-gather.21.cloned.1.call-start = ((), (), s32[]{:S(2)}) async-start(), calls=%async_computation.13 | async-start | bytes 2359296 | tf_op jit(solution)/shard_map/all_gather | solution.py:123
  7.9 110.1 %all-gather.23.cloned.1.call-start = ((), (), s32[]{:S(2)}) async-start(), calls=%async_computation.14 | async-start | bytes 2359296 | tf_op jit(solution)/shard_map/all_gather | solution.py:124
  8.7 165.3 %all-gather.19.cloned.1.call-start = ((), (), s32[]{:S(2)}) async-start(), calls=%async_computation.12 | async-start | bytes 2359296 | tf_op jit(solution)/shard_map/all_gather | solution.py:125
  9.4 220.9 %all-gather.39.cloned.1.call-start = ((), (), s32[]{:S(2)}) async-start(), calls=%async_computation.26 | async-start | bytes 2359296 | tf_op jit(solution)/shard_map/all_gather | solution.py:183
  120.7 23.6 copy-start.24
  144.3 141.0 %all-gather.37.cloned.1.call-start = ((), (), s32[]{:S(2)}) async-start(), calls=%async_computation.25 | async-start | bytes 2359296 | tf_op jit(solution)/shard_map/all_gather | solution.py:184
  173.9 27.5 %copy-start.23 = (s32[16,1024]{1,0:T(8,128)S(1)}, s32[16,1024]{1,0:T(8,128)}, u32[]{:S(2)}) copy-start(s32[16,1024]{1,0:T(8,128)} %param.17) | copy-start | bytes 196612
  198.6 144.6 %all-gather.25.cloned.1.call-start = ((), (), s32[]{:S(2)}) async-start(), calls=%async_computation.15 | async-start | bytes 2359296 | tf_op jit(solution)/shard_map/all_gather | solution.py:129
  199.2 264.7 %all-gather.29.cloned.1.call-start = ((), (), s32[]{:S(2)}) async-start(), calls=%async_computation.17 | async-start | bytes 6488064 | tf_op jit(solution)/shard_map/all_gather | solution.py:132
  199.9 385.8 %all-gather.27.cloned.1.call-start = ((), (), s32[]{:S(2)}) async-start(), calls=%async_computation.16 | async-start | bytes 6488064 | tf_op jit(solution)/shard_map/all_gather | solution.py:131
  200.7 506.2 %all-gather.31.cloned.1.call-start = ((), (), s32[]{:S(2)}) async-start(), calls=%async_computation.18 | async-start | bytes 6488064 | tf_op jit(solution)/shard_map/all_gather | solution.py:133
  204.8 16.3 all-to-all-start.1
  221.4 13.2 copy-start.19
  234.7 3.3 copy-start
  239.9 60.0 %copy-start.25 = (bf16[128]{0:T(256)(128)(2,1)S(1)}, bf16[128]{0:T(256)(128)(2,1)}, u32[]{:S(2)}) copy-start(bf16[128]{0:T(256)(128)(2,1)} %param.27) | copy-start | bytes 772
  291.7 51.5 %all-to-all-start.3 = ((bf16[16,128,64]{1,2,0:T(8,128)(2,1)}), bf16[16,128,64]{1,2,0:T(8,128)(2,1)S(1)}, u32[]{:S(2)}, u32[]{:S(2)}) async-start(bf16[16,128,64]{1,2,0:T(8,128)(2,1)} %fusion.37), calls=%async_computation.3 | async-start | bytes 524288 | tf_op jit(solution)/shard_map/all_to_all | solution.py:209
  343.2 2.2 copy-start.16
  468.5 238.4 %copy-start.21 = (bf16[1,128,1024]{2,1,0:T(8,128)(2,1)S(1)}, bf16[1,128,1024]{2,1,0:T(8,128)(2,1)}, u32[]{:S(2)}) copy-start(bf16[1,128,1024]{2,1,0:T(8,128)(2,1)} %param.31) | copy-start | bytes 786436
  706.9 5.9 copy-start.1
  712.8 6.9 copy-start.13
  712.8 260.6 %copy-start.12 = (bf16[128,2816]{1,0:T(8,128)(2,1)}, bf16[128,2816]{1,0:T(8,128)(2,1)S(1)}, u32[]{:S(2)}) copy-start(bf16[128,2816]{1,0:T(8,128)(2,1)S(1)} %get-tuple-element.122) | copy-start | bytes 2162692
  714.8 5.1 copy-start.8
  725.7 15.9 all-to-all-start.4
  732.9 115.1 %reduce-scatter.5.cloned.1.call-start = ((), (), s32[]{:S(2)}) async-start(), calls=%async_computation.19 | async-start | bytes 4718592 | tf_op jit(solution)/shard_map/reduce_scatter | solution.py:248
  743.6 6.6 slice-start
  743.6 6.6 slice-start.1
  750.3 3.8 copy-start.20
  752.1 2.0 copy-start.2
  756.8 184.9 %reduce-scatter.7.cloned.1.call-start = ((), (), s32[]{:S(2)}) async-start(), calls=%async_computation.20 | async-start | bytes 4718592 | tf_op jit(solution)/shard_map/reduce_scatter | solution.py:254
  763.9 3.1 copy-start.17
  772.9 77.0 %all-to-all-start.5 = ((bf16[16,128,64]{1,2,0:T(8,128)(2,1)}), bf16[16,128,64]{1,2,0:T(8,128)(2,1)S(1)}, u32[]{:S(2)}, u32[]{:S(2)}) async-start(bf16[16,128,64]{1,2,0:T(8,128)(2,1)} %fusion.33), calls=%async_computation.5 | async-start | bytes 524288 | tf_op jit(solution)/shard_map/all_to_all | solution.py:263
  849.9 93.6 %copy-start.15 = (bf16[16,128,64]{1,2,0:T(8,128)(2,1)}, bf16[16,128,64]{1,2,0:T(8,128)(2,1)S(1)}, u32[]{:S(2)}) copy-start(bf16[16,128,64]{1,2,0:T(8,128)(2,1)S(1)} %all-to-all-done.5) | copy-start | bytes 786436
  849.9 93.6 %all-to-all-start.6 = ((bf16[16,128,64]{1,2,0:T(8,128)(2,1)}), bf16[16,128,64]{1,2,0:T(8,128)(2,1)}, u32[]{:S(2)}, u32[]{:S(2)}) async-start(bf16[16,128,64]{1,2,0:T(8,128)(2,1)} %convert_element_type.254), calls=%async_computation.7 | async-start | bytes 524288 | tf_op jit(solution)/shard_map/all_to_all | solution.py:264
  943.5 16.1 all-to-all-start.7
  950.9 668.9 %reduce-scatter.9.cloned.1.call-start = ((), (), s32[]{:S(2)}) async-start(), calls=%async_computation.21 | async-start | bytes 16908288 | tf_op jit(solution)/shard_map/reduce_scatter | solution.py:314
  950.9 2.7 copy-start.18
  959.6 3.1 copy-start.9
  959.6 3.1 copy-start.4
  968.7 0.9 copy-start.22
  968.7 1412.7 %reduce-scatter.11.cloned.1.call-start = ((), (), s32[]{:S(2)}) async-start(), calls=%async_computation.23 | async-start | bytes 34873344 | tf_op jit(solution)/shard_map/reduce_scatter | solution.py:322
  973.4 6.0 copy-start.14
  1012.1 1376.0 %copy-start.6 = (bf16[1024,1024]{1,0:T(8,128)(2,1)S(1)}, bf16[1024,1024]{1,0:T(8,128)(2,1)}, u32[]{:S(2)}) copy-start(bf16[1024,1024]{1,0:T(8,128)(2,1)} %all-gather.21.cloned.1.call-done) | copy-start | bytes 6291460
  1012.1 1451.3 %all-gather.33.cloned.1.call-start = ((), (), s32[]{:S(2)}) async-start(), calls=%async_computation.22 | async-start | bytes 1114112 | tf_op jit(solution)/shard_map/all_gather | solution.py:329
  1621.4 857.2 %all-gather.35.cloned.1.call-start = ((), (), s32[]{:S(2)}) async-start(), calls=%async_computation.24 | async-start | bytes 2297856 | tf_op jit(solution)/shard_map/all_gather | solution.py:332
  2383.1 4.5 copy-start.10
  2387.6 4.9 copy-start.11
  2388.1 4.5 copy-start.7
  2480.5 4.1 copy-start.5
Sparse Core Ops, SparseCore 0:
  9.7 55.2 all-gather.20
  66.6 51.3 all-gather.22
  119.7 54.2 all-gather.18
  175.9 54.3 all-gather.38
  232.3 52.8 all-gather.36
  286.7 56.4 all-gather.24
  344.9 118.9 all-gather.28
  465.5 120.1 all-gather.26
  587.3 119.5 all-gather.30
  756.9 91.1 reduce-scatter.4
  850.5 91.1 reduce-scatter.6
  968.8 650.9 reduce-scatter.8
  1622.2 759.1 reduce-scatter.10
  2384.3 44.7 all-gather.32
  2432.0 46.5 all-gather.34
where the time goes:
time: 2500 us; the launch traced here: 2490 us
  waiting for transfers between devices  2070 us (83%)
  blocking collectives  178 us (7%)
  matrix products  95.9 us (4%)
  other arithmetic  61.9 us (2%)
  starting transfers between devices  40.3 us (2%)
  local copies, waits for them, and re-layouts  33.6 us (1%)
    reduce_scatter x2, waiting for transfers between devices, per_device(): lax.psum_scatter(jnp.concatenate([first_part, second], axis=1), ('seq', '...  1370 us
    all_gather x1, waiting for transfers between devices, per_device(): lax.all_gather(up_weight, 'fsdp', axis=0, tiled=True)  118 us
    all_gather x1, waiting for transfers between devices, per_device(): lax.all_gather(gate_weight, 'fsdp', axis=0, tiled=True)  117 us
    all_gather x1, waiting for transfers between devices, per_device(): lax.all_gather(down_weight, 'fsdp', axis=1, tiled=True)  117 us
    reduce_scatter x1, waiting for transfers between devices, per_device(): lax.psum_scatter(grad_value_blk.reshape(total_seqs, length, heads_here *...  82.8 us
    reduce_scatter x1, waiting for transfers between devices, per_device(): lax.psum_scatter(grad_key_blk.reshape(total_seqs, length, heads_here * HE...  67.3 us
    psum x1, blocking collectives, per_device(): lax.psum((grad_gain_one, jnp.sum(pre_query.astype(jnp.float32), axis=0),...  66 us
    all_gather x1, waiting for transfers between devices, per_device(): lax.all_gather(key_weight, 'fsdp', axis=0, tiled=True)  50.6 us
  transfers between devices with their start and end apart: 21, of which 17 were waited for; matrix products, arithmetic and copies ran while one was open for 5% of the time, Pallas kernels for 0%

commit v1 on v0

v1 whole, which is shorter than its diff:
```python
import math

import jax
import jax.numpy as jnp
from jax import lax
from jax.experimental import pallas as pl
from jax.experimental.pallas import tpu as pltpu
from jax.sharding import PartitionSpec as P

MESH = pl.DeviceIdType.MESH
HEAD_DIM = 64
EPS = 1e-06
THETA = 1000000.0
NEG = -1000000000.0
D = 1024
PIECE = 128
BLOCK = 256
FB = 384
F32 = jnp.float32
BF16 = jnp.bfloat16


def nn(a, b):
    return lax.dot_general(a, b, (((1,), (0,)), ((), ())), preferred_element_type=F32)


def nt(a, b):
    return lax.dot_general(a, b, (((1,), (1,)), ((), ())), preferred_element_type=F32)


def tn(a, b):
    return lax.dot_general(a, b, (((0,), (0,)), ((), ())), preferred_element_type=F32)


def rms_scale(value):
    return lax.rsqrt(jnp.mean(value * value, axis=-1, keepdims=True) + EPS)


def rows(start, size):
    return pl.ds(pl.multiple_of(start, size), size)


def half_turn(value):
    lane = lax.broadcasted_iota(jnp.int32, value.shape, 1)
    ahead = pltpu.roll(value, 96, 1)
    behind = pltpu.roll(value, 32, 1)
    return jnp.where(lane % 64 < 32, ahead, behind)


def layer_kernel(
    x_in, cot_in, wq_in, wk_in, wv_in, wo_in, wg_in, wu_in, wd_in,
    vec_in, cos_ref, sin_ref, start_ref,
    layer_out, in_grad, grads_a, grads_b, vec_out,
    x_own, cot_own, hidden, g_hidden, wo, wqkv, wgu, wdn, vall,
    normed_all, cot_all, mlp_all, branch_all,
    q_h, k_h, v_h, k_t, v_t, p_t, mixed_t, mixed,
    g_act, active, g_gu, g_mixed, gk_acc, gv_acc, g_qkv,
    part, sib, far_s, far_r, fin_s, fin_r,
    dgu, ddn, dwo, dqkv, rgu, rdn, rwo, rqkv, wo_send, wo_recv,
    lo_send, ig_send, lo_recv, ig_recv,
    vs, vr, v2s, v2r,
    sem_load, swap_s, swap_r, vec_s, vec_r, w_s, w_r, ag_s, ag_r,
    sib_ss, sib_rs, far_ss, far_rs, fin_ss, fin_rs,
    pl_s, pl_r, ga_s, ga_r, v1_ss, v1_rs, v2_ss, v2_rs,
):
    s = lax.axis_index("seq")
    f = lax.axis_index("fsdp")
    xh = s // 8
    j = s % 8
    z = j // 2
    c = j % 2
    y = f // 2
    x = xh * 2 + f % 2

    def dev(x_, y_, z_, c_):
        x_, y_, z_ = (x_ + 4) % 4, (y_ + 4) % 4, (z_ + 4) % 4
        return ((x_ // 2) * 8 + z_ * 2 + c_, y_ * 2 + x_ % 2)

    sibling = dev(x, y, z, 1 - c)
    z_up = dev(x, y, z + 1, c)
    z_dn = dev(x, y, z + 3, c)
    partner = (xh * 8 + f, j)
    x_to = dev(x + 1 + 2 * c, y, z, c)
    win = (3 * j - 2 * (j // 7)) * 128

    def remote(src, dst, ss, rs, to):
        return pltpu.make_async_remote_copy(
            src_ref=src, dst_ref=dst, send_sem=ss, recv_sem=rs, device_id=to, device_id_type=MESH
        )

    loads = [
        pltpu.make_async_copy(wq_in.at[:, rows(j * 128, 128)], wqkv.at[rows(f * 128, 128), pl.ds(0, 128)], sem_load.at[0]),
        pltpu.make_async_copy(wk_in.at[:, rows(j * 128, 128)], wqkv.at[rows(f * 128, 128), pl.ds(128, 128)], sem_load.at[1]),
        pltpu.make_async_copy(wv_in.at[:, rows(j * 128, 128)], wqkv.at[rows(f * 128, 128), pl.ds(256, 128)], sem_load.at[2]),
        pltpu.make_async_copy(wg_in.at[:, pl.ds(pl.multiple_of(win, 128), FB)], wgu.at[rows(f * 128, 128), pl.ds(0, FB)], sem_load.at[3]),
        pltpu.make_async_copy(wu_in.at[:, pl.ds(pl.multiple_of(win, 128), FB)], wgu.at[rows(f * 128, 128), pl.ds(FB, FB)], sem_load.at[4]),
        pltpu.make_async_copy(wd_in.at[pl.ds(pl.multiple_of(win, 128), FB), :], wdn.at[:, rows(f * 128, 128)], sem_load.at[5]),
    ]
    for load in loads:
        load.start()

    barrier = pltpu.get_barrier_semaphore()

    def greet_plane(r, carry):
        pl.semaphore_signal(barrier, inc=1, device_id=dev(x + r // 4, y + r % 4, z, c), device_id_type=MESH)
        return carry

    def greet_seq(r, carry):
        pl.semaphore_signal(barrier, inc=1, device_id=((s + r) % 16, f), device_id_type=MESH)
        return carry

    lax.fori_loop(1, 16, greet_plane, 0)
    lax.fori_loop(1, 16, greet_seq, 0)

    @pl.when(j != f)
    def _():
        pl.semaphore_signal(barrier, inc=1, device_id=partner, device_id_type=MESH)
        pl.semaphore_wait(barrier, 31)

    @pl.when(j == f)
    def _():
        pl.semaphore_wait(barrier, 30)

    def swap_start(src, dst, n):
        @pl.when(j != f)
        def _():
            remote(src, dst, swap_s.at[n], swap_r.at[n], partner).start()

        @pl.when(j == f)
        def _():
            pltpu.make_async_copy(src, dst, swap_r.at[n]).start()

    def swap_wait(src, dst, n):
        @pl.when(j != f)
        def _():
            remote(src, dst, swap_s.at[n], swap_r.at[n], partner).wait()

        @pl.when(j == f)
        def _():
            pltpu.make_async_copy(src, dst, swap_r.at[n]).wait()

    x_src = x_in
    cot_src = cot_in
    swap_start(x_src, x_own, 0)

    def vec_copy(r):
        return remote(vec_in, vall.at[f], vec_s.at[r], vec_r.at[r], (s, (f + r) % 8))

    def vec_start(r, carry):
        vec_copy(r).start()
        return carry

    def vec_wait(r, carry):
        vec_copy(r).wait()
        return carry

    lax.fori_loop(1, 8, vec_start, 0)
    vall[pl.ds(f, 1)] = vec_in[...][None]

    def w_slice(n, f_):
        if n == 0:
            return wqkv.at[rows(f_ * 128, 128)]
        if n == 1:
            return wgu.at[rows(f_ * 128, 128)]
        return wdn.at[:, rows(f_ * 128, 128)]

    def w_y(n, r):
        ref = w_slice(n, f)
        return remote(ref, ref, w_s.at[n, r], w_r.at[n, r], dev(x, y + r, z, c))

    def w_x(n, r):
        ref = w_slice(n, ((y + 4 - r) % 4) * 2 + f % 2)
        return remote(ref, ref, w_s.at[n, 4 + r], w_r.at[n, 4 + r], x_to)

    def w_x_in(n, r):
        ref = w_slice(n, ((y + 4 - r) % 4) * 2 + 1 - f % 2)
        return remote(ref, ref, w_s.at[n, 4 + r], w_r.at[n, 4 + r], x_to)

    def w_y_in(n, r):
        ref = w_slice(n, ((y + 4 - r) % 4) * 2 + f % 2)
        return remote(ref, ref, w_s.at[n, r], w_r.at[n, r], dev(x, y + r, z, c))

    def w_start(n):
        for r in (1, 3, 2):
            w_y(n, r).start()
        w_x(n, 0).start()

    def w_forward(n):
        for r in (1, 3, 2):
            w_y_in(n, r).wait_recv()
            w_x(n, r).start()

    def w_finish(n):
        for r in range(4):
            w_x_in(n, r).wait_recv()

    for load in loads[:3]:
        load.wait()
    w_start(0)
    swap_start(wo_in, wo, 1)
    swap_start(cot_src, cot_own, 2)

    def piece(buf, z_, c_):
        return buf.at[rows((((z_ + 4) % 4) * 2 + c_) * PIECE, PIECE)]

    def half(buf, z_, c_, h):
        return buf.at[rows((((z_ + 4) % 4) * 2 + c_) * PIECE + h * 64, 64)]

    def ag(buf, k, n, recv=False):
        if n == 0:
            ref, to = (piece(buf, z - 1, c) if recv else piece(buf, z, c)), z_up
        elif n == 1:
            ref, to = (piece(buf, z + 1, c) if recv else piece(buf, z, c)), z_dn
        elif n == 2:
            ref, to = (piece(buf, z, 1 - c) if recv else piece(buf, z, c)), sibling
        elif n == 3:
            ref, to = (half(buf, z - 2, c, 0) if recv else half(buf, z - 1, c, 0)), z_up
        elif n == 4:
            ref, to = (piece(buf, z - 1, 1 - c) if recv else piece(buf, z - 1, c)), sibling
        elif n == 5:
            ref, to = (half(buf, z + 2, c, 1) if recv else half(buf, z + 1, c, 1)), z_dn
        elif n == 6:
            ref, to = (piece(buf, z + 1, 1 - c) if recv else piece(buf, z + 1, c)), sibling
        else:
            ref, to = (piece(buf, z + 2, 1 - c) if recv else piece(buf, z + 2, c)), sibling
        return remote(ref, ref, ag_s.at[k, n], ag_r.at[k, n], to)

    def ag_start(buf, k):
        for n in range(3):
            ag(buf, k, n).start()

    def ag_near(buf, k):
        ag(buf, k, 0, True).wait_recv()
        ag(buf, k, 3).start()
        ag(buf, k, 4).start()
        ag(buf, k, 1, True).wait_recv()
        ag(buf, k, 5).start()
        ag(buf, k, 6).start()

    def ag_far(buf, k):
        ag(buf, k, 3, True).wait_recv()
        ag(buf, k, 5, True).wait_recv()
        ag(buf, k, 7).start()

    def ag_run(buf, k, consume):
        def step(i, carry):
            @pl.when(i == 0)
            def _():
                ag(buf, k, 2, True).wait_recv()

            @pl.when(i == 1)
            def _():
                ag_near(buf, k)
                ag(buf, k, 4, True).wait_recv()

            @pl.when(i == 2)
            def _():
                ag(buf, k, 6, True).wait_recv()

            @pl.when(i == 3)
            def _():
                ag_far(buf, k)
                ag(buf, k, 7, True).wait_recv()

            consume((z + (3 * ((i * (i + 1)) // 2)) % 4) % 4)
            return carry

        lax.fori_loop(0, 4, step, 0)

    def other(i):
        return part.at[i, rows((1 - c) * PIECE, PIECE)]

    def own_part(i):
        return part[i, rows(c * PIECE, PIECE), :].astype(F32)

    def c_sib(k, i):
        return remote(other(i), sib.at[k, i], sib_ss.at[k, i], sib_rs.at[k, i], sibling)

    def c_far(k, n):
        return remote(far_s.at[k, pl.ds(64 * n, 64)], far_r.at[k, n], far_ss.at[k, n], far_rs.at[k, n], z_up if n == 0 else z_dn)

    def c_fin(k, n, h):
        cut = pl.ds(64 * h, 64)
        return remote(fin_s.at[k, n, cut], fin_r.at[k, n, cut], fin_ss.at[k, n, h], fin_rs.at[k, n, h], z_up if n == 0 else z_dn)

    def rs_start(k, produce):
        def step(i, carry):
            if k > 0:
                c_sib(k - 1, i).wait_send()
            part[i] = produce((z + (2 - (i * (i + 1)) // 2 + 8) % 4) % 4).astype(BF16)
            c_sib(k, i).start()

            @pl.when(i == 1)
            def _():
                c_sib(k, 0).wait_recv()
                far_s[k] = (own_part(0) + sib[k, 0].astype(F32)).astype(BF16)
                c_far(k, 0).start()
                c_far(k, 1).start()

            @pl.when(i == 2)
            def _():
                c_sib(k, 1).wait_recv()
                fin_s[k, 0] = (own_part(1) + sib[k, 1].astype(F32)).astype(BF16)
                c_fin(k, 0, 1).start()

            @pl.when(i == 3)
            def _():
                c_sib(k, 2).wait_recv()
                fin_s[k, 1] = (own_part(2) + sib[k, 2].astype(F32)).astype(BF16)
                c_fin(k, 1, 0).start()

            return carry

        lax.fori_loop(0, 4, step, 0)

    def rs_mid(k):
        for n in (0, 1):
            c_far(k, n).wait_recv()
            cut = pl.ds(64 * n, 64)
            fin_s[k, n, cut] = (fin_s[k, n, cut].astype(F32) + far_r[k, n].astype(F32)).astype(BF16)
            c_fin(k, n, n).start()

    def rs_finish(k):
        c_sib(k, 3).wait_recv()
        total = own_part(3) + sib[k, 3].astype(F32)
        for n in (0, 1):
            for h in (0, 1):
                c_fin(k, n, h).wait_recv()
        return total + fin_r[k, 0].astype(F32) + fin_r[k, 1].astype(F32)

    lax.fori_loop(1, 8, vec_wait, 0)

    def gathered(row):
        return jnp.concatenate([vall[i, row : row + 1, :] for i in range(8)], axis=1)

    swap_wait(x_src, x_own, 0)
    x32 = x_own[...].astype(F32)
    normed_all[rows(j * PIECE, PIECE), :] = (x32 * rms_scale(x32) * gathered(0)).astype(BF16)
    ag_start(normed_all, 0)
    w_forward(0)
    for load in loads[3:]:
        load.wait()
    w_start(1)
    w_start(2)
    swap_wait(cot_src, cot_own, 2)
    cot_all[rows(j * PIECE, PIECE), :] = cot_own[...]
    w_finish(0)

    def project(zz):
        cut = rows(zz * BLOCK, BLOCK)
        lin = nn(normed_all[cut, :], wqkv[...])
        cos = cos_ref[cut, :]
        sin = sin_ref[cut, :]
        bias = vall[pl.ds(j, 1)][0]
        q_lin = lin[:, :128] + bias[2:3, :]
        k_lin = lin[:, 128:256] + bias[3:4, :]
        v_lin = lin[:, 256:] + bias[4:5, :]
        q = (q_lin * cos + half_turn(q_lin) * sin).astype(BF16) * 0.125
        k32 = k_lin * cos + half_turn(k_lin) * sin
        k = k32.astype(BF16)
        v = v_lin.astype(BF16)
        for h in range(2):
            lanes = slice(64 * h, 64 * h + 64)
            q_h[h, cut, :] = q[:, lanes]
            k_h[h, cut, :] = k[:, lanes]
            v_h[h, cut, :] = v[:, lanes]
        k_t[:, cut] = k32.T.astype(BF16)
        v_t[:, cut] = v_lin.T.astype(BF16)

    ag_run(normed_all, 0, project)
    ag_start(cot_all, 1)

    def attend(i):
        width = (i + 1) * BLOCK
        cut = slice(i * BLOCK, (i + 1) * BLOCK)
        key_at = lax.broadcasted_iota(jnp.int32, (width, BLOCK), 0)
        query_at = lax.broadcasted_iota(jnp.int32, (width, BLOCK), 1) + i * BLOCK
        allowed = (key_at >= start_ref[0:1, cut]) & (key_at <= query_at)
        for h in range(2):
            scores = nt(k_h[h, :width, :], q_h[h, cut, :])
            scores = jnp.where(allowed, scores, NEG)
            weights = jnp.exp(scores - jnp.max(scores, axis=0, keepdims=True))
            inverse = 1.0 / jnp.sum(weights, axis=0, keepdims=True)
            probs = (weights * inverse).astype(BF16)
            p_t[h, i, :width, :] = probs
            mixed_t[64 * h : 64 * h + 64, cut] = nn(v_t[64 * h : 64 * h + 64, :width], probs)
        mixed[cut, :] = mixed_t[:, cut].T.astype(BF16)

    attend(0)
    attend(1)
    w_forward(1)
    w_forward(2)
    attend(2)
    ag_near(cot_all, 1)
    attend(3)
    ag_far(cot_all, 1)
    swap_wait(wo_in, wo, 1)

    rs_start(0, lambda zz: nn(mixed[rows(zz * BLOCK, BLOCK), :], wo[...]))
    w_finish(1)
    w_finish(2)
    for n in (2, 4, 6, 7):
        ag(cot_all, 1, n, True).wait_recv()
    rs_mid(0)

    def active_back(i, carry):
        cut = rows(i * BLOCK, BLOCK)
        g_act[cut, :] = nt(cot_all[cut, :], wdn[...])
        return carry

    lax.fori_loop(0, 4, active_back, 0)
    hidden[...] = x_own[...].astype(F32) + rs_finish(0)
    hid = hidden[...]
    mlp_all[rows(j * PIECE, PIECE), :] = (hid * rms_scale(hid) * gathered(1)).astype(BF16)
    ag_start(mlp_all, 2)

    unit = lax.broadcasted_iota(jnp.int32, (1, FB), 1)
    low_edge = 128 * (j // 7)
    high_edge = FB - 128 * ((j // 6) * (1 - j // 7))
    live = (unit >= low_edge) & (unit < high_edge)

    def feed(zz):
        cut = rows(zz * BLOCK, BLOCK)
        both = nn(mlp_all[cut, :], wgu[...])
        gate = both[:, :FB]
        up = both[:, FB:]
        sig = 1.0 / (1.0 + jnp.exp(-gate))
        silu = gate * sig
        back = jnp.where(live, g_act[cut, :], 0.0)
        active[cut, :] = jnp.where(live, silu * up, 0.0).astype(BF16)
        g_gu[cut, :FB] = (back * up * sig * (1.0 + gate * (1.0 - sig))).astype(BF16)
        g_gu[cut, FB:] = (back * silu).astype(BF16)

    ag_run(mlp_all, 2, feed)
    rs_start(1, lambda zz: nt(g_gu[rows(zz * BLOCK, BLOCK), :], wgu[...]))
    rs_mid(1)

    def plane_to(r):
        x_ = (x + r // 4) % 4
        y_ = (y + r % 4) % 4
        return x_ // 2, y_ * 2 + x_ % 2, dev(x_, y_, z, c)

    def p_gu(r):
        h_, f_, to = plane_to(r)
        return remote(dgu.at[rows(f_ * 128 + h_ * 64, 64)], rgu.at[r - 1], pl_s.at[0, r - 1], pl_r.at[0, r - 1], to)

    def p_dn(r):
        h_, f_, to = plane_to(r)
        return remote(ddn.at[rows(h_ * 192, 64 * 3), rows(f_ * 128, 128)], rdn.at[r - 1], pl_s.at[1, r - 1], pl_r.at[1, r - 1], to)

    def p_wo(r):
        h_, f_, to = plane_to(r)
        return remote(dwo.at[rows(h_ * 64, 64), rows(f_ * 128, 128)], rwo.at[r - 1], pl_s.at[2, r - 1], pl_r.at[2, r - 1], to)

    def p_qkv(r):
        h_, f_, to = plane_to(r)
        return remote(dqkv.at[rows(f_ * 128 + h_ * 64, 64)], rqkv.at[r - 1], pl_s.at[3, r - 1], pl_r.at[3, r - 1], to)

    def plane_start(copy):
        def go(r, carry):
            copy(r).start()
            return carry

        lax.fori_loop(1, 16, go, 0)

    def plane_wait(copy):
        def go(r, carry):
            copy(r).wait()
            return carry

        lax.fori_loop(1, 16, go, 0)

    def plane_sum(own, recv):
        return lax.fori_loop(0, 15, lambda r, total: total + recv[r].astype(F32), own.astype(F32))

    def grad_gu(i, carry):
        cut = rows(i * BLOCK, BLOCK)
        dgu[cut, :] = tn(mlp_all[:, cut], g_gu[...]).astype(BF16)
        return carry

    def grad_dn(i, carry):
        cut = rows(i * 128, 128)
        ddn[cut, :] = tn(active[:, cut], cot_all[...]).astype(BF16)
        return carry

    lax.fori_loop(0, 4, grad_gu, 0)
    plane_start(p_gu)

    grad = rs_finish(1)
    hid = hidden[...]
    scale = rms_scale(hid)
    scaled = grad * gathered(1)
    back = scale * scaled - hid * (scale * scale * scale) * jnp.mean(scaled * hid, axis=-1, keepdims=True)
    gain_two = jnp.sum(grad * hid * scale, axis=0, keepdims=True)
    g_hidden[...] = cot_own[...].astype(F32) + back
    branch_all[rows(j * PIECE, PIECE), :] = g_hidden[...].astype(BF16)
    ag_start(branch_all, 3)
    lax.fori_loop(0, 3, grad_dn, 0)
    plane_start(p_dn)

    def mixed_back(zz):
        cut = rows(zz * BLOCK, BLOCK)
        g_mixed[cut, :] = nt(branch_all[cut, :], wo[...])

    ag_run(branch_all, 3, mixed_back)
    rs_start(2, lambda zz: nn(active[rows(zz * BLOCK, BLOCK), :], wdn[...]))
    dwo[...] = tn(mixed[...], branch_all[...]).astype(BF16)
    plane_start(p_wo)

    gk_acc[...] = jnp.zeros_like(gk_acc)
    gv_acc[...] = jnp.zeros_like(gv_acc)

    def unturn(value, cut):
        value = value.astype(BF16).astype(F32)
        return (value * cos_ref[cut, :] - half_turn(value) * sin_ref[cut, :]).astype(BF16)

    def attend_back(i):
        width = (i + 1) * BLOCK
        cut = slice(i * BLOCK, (i + 1) * BLOCK)
        grad_t = g_mixed[cut, :].T
        grad_bf = g_mixed[cut, :].astype(BF16)
        products = grad_t * mixed_t[:, cut]
        queries_t = []
        for h in range(2):
            lanes = slice(64 * h, 64 * h + 64)
            grad_h = grad_bf[:, lanes]
            delta = jnp.sum(products[lanes, :], axis=0, keepdims=True)
            probs = p_t[h, i, :width, :]
            gv_acc[h, :width, :] += nn(probs, grad_h)
            g_probs = nt(v_h[h, :width, :], grad_h)
            g_scores = (probs.astype(F32) * (g_probs - delta)).astype(BF16)
            gk_acc[h, :width, :] += nn(g_scores, q_h[h, cut, :])
            queries_t.append(nn(k_t[lanes, :width], g_scores))
        g_query = (jnp.concatenate(queries_t, axis=0) * 0.125).T
        g_qkv[cut, :128] = unturn(g_query, cut)

    attend_back(0)
    attend_back(1)
    rs_mid(2)
    attend_back(2)
    attend_back(3)
    for i in range(4):
        cut = slice(i * BLOCK, (i + 1) * BLOCK)
        g_qkv[cut, 128:256] = unturn(jnp.concatenate([gk_acc[0, cut, :], gk_acc[1, cut, :]], axis=1), cut)
        g_qkv[cut, 256:] = jnp.concatenate([gv_acc[0, cut, :], gv_acc[1, cut, :]], axis=1).astype(BF16)

    lo_send[...] = (hidden[...] + rs_finish(2)).astype(BF16)
    swap_start(lo_send, lo_recv, 3)
    rs_start(3, lambda zz: nt(g_qkv[rows(zz * BLOCK, BLOCK), :], wqkv[...]))

    def grad_qkv(i, carry):
        cut = rows(i * BLOCK, BLOCK)
        dqkv[cut, :] = tn(normed_all[:, cut], g_qkv[...]).astype(BF16)
        return carry

    lax.fori_loop(0, 4, grad_qkv, 0)
    plane_start(p_qkv)
    rs_mid(3)

    mine = f * 128 + xh * 64
    plane_wait(p_wo)
    wo_send[...] = plane_sum(dwo[rows(xh * 64, 64), rows(f * 128, 128)], rwo).astype(BF16)
    swap_start(wo_send, wo_recv, 4)
    slot = j * 2 + xh
    plane_wait(p_gu)
    grads_a[pl.ds(slot, 1), :, 128:896] = plane_sum(dgu[rows(mine, 64), :], rgu).astype(BF16)[None]
    plane_wait(p_dn)
    total_dn = plane_sum(ddn[rows(xh * 192, 192), rows(f * 128, 128)], rdn).astype(BF16)
    for t in range(3):
        grads_a[pl.ds(slot, 1), :, 896 + 128 * t : 1024 + 128 * t] = total_dn[64 * t : 64 * t + 64][None]
    swap_wait(wo_send, wo_recv, 4)
    grads_a[pl.ds(slot, 1), :, :128] = wo_recv[...][None]

    def pair(buf, z_, c_):
        return buf.at[pl.ds((((z_ + 4) % 4) * 2 + c_) * 2, 2)]

    def single(buf, z_, c_, h):
        return buf.at[pl.ds((((z_ + 4) % 4) * 2 + c_) * 2 + h, 1)]

    def gg(buf, k, n, recv=False):
        if n == 0:
            ref = single(buf, z, c, (1 - xh) if recv else xh)
            to = dev(x + 2, y, z, c)
        elif n == 1:
            ref, to = pair(buf, z - 1 if recv else z, c), z_up
        elif n == 2:
            ref, to = pair(buf, z + 1 if recv else z, c), z_dn
        elif n == 3:
            ref, to = single(buf, z - 2 if recv else z - 1, c, 0), z_up
        elif n == 4:
            ref, to = single(buf, z + 2 if recv else z + 1, c, 1), z_dn
        else:
            ref, to = pair(buf, z + (n - 5), (1 - c) if recv else c), sibling
        return remote(ref, ref, ga_s.at[k, n], ga_r.at[k, n], to)

    def gg_one(buf, k):
        gg(buf, k, 0).start()

    def gg_two(buf, k):
        gg(buf, k, 0, True).wait_recv()
        gg(buf, k, 1).start()
        gg(buf, k, 2).start()
        gg(buf, k, 5).start()

    def gg_three(buf, k):
        gg(buf, k, 1, True).wait_recv()
        gg(buf, k, 3).start()
        gg(buf, k, 8).start()
        gg(buf, k, 2, True).wait_recv()
        gg(buf, k, 4).start()
        gg(buf, k, 6).start()

    def gg_four(buf, k):
        gg(buf, k, 3, True).wait_recv()
        gg(buf, k, 4, True).wait_recv()
        gg(buf, k, 7).start()

    def gg_five(buf, k):
        for n in (5, 6, 7, 8):
            gg(buf, k, n, True).wait_recv()

    gg_one(grads_a, 0)

    grad = rs_finish(3)
    gg_two(grads_a, 0)
    scale = rms_scale(x32)
    scaled = grad * gathered(0)
    back = scale * scaled - x32 * (scale * scale * scale) * jnp.mean(scaled * x32, axis=-1, keepdims=True)
    gain_one = jnp.sum(grad * x32 * scale, axis=0, keepdims=True)
    ig_send[...] = (g_hidden[...] + back).astype(BF16)
    swap_start(ig_send, ig_recv, 5)

    vs[...] = jnp.zeros_like(vs)
    for i in range(8):
        vs[i, 0:1, :] = gain_one[:, 128 * i : 128 * i + 128]
        vs[i, 1:2, :] = gain_two[:, 128 * i : 128 * i + 128]
    bias_sum = jnp.sum(g_qkv[...].astype(F32), axis=0, keepdims=True)
    for i in range(3):
        vs[pl.ds(j, 1), 2 + i : 3 + i, :] = bias_sum[:, 128 * i : 128 * i + 128][None]

    def v1_copy(r):
        return remote(vs.at[(f + r) % 8], vr.at[r - 1], v1_ss.at[r - 1], v1_rs.at[r - 1], (s, (f + r) % 8))

    def v1_start(r, carry):
        v1_copy(r).start()
        return carry

    def v1_wait(r, carry):
        v1_copy(r).wait()
        return carry

    lax.fori_loop(1, 8, v1_start, 0)

    plane_wait(p_qkv)
    grads_b[pl.ds(slot, 1)] = plane_sum(dqkv[rows(mine, 64), :], rqkv).astype(BF16)[None]
    gg_one(grads_b, 1)
    lax.fori_loop(1, 8, v1_wait, 0)
    v2s[...] = jnp.sum(vr[...], axis=0) + vs[pl.ds(f, 1)][0]

    def v2_copy(r):
        return remote(v2s, v2r.at[r - 1], v2_ss.at[r - 1], v2_rs.at[r - 1], ((s + r) % 16, f))

    def v2_start(r, carry):
        v2_copy(r).start()
        return carry

    def v2_wait(r, carry):
        v2_copy(r).wait()
        return carry

    lax.fori_loop(1, 16, v2_start, 0)
    gg_three(grads_a, 0)
    gg_two(grads_b, 1)
    gg_four(grads_a, 0)
    gg_three(grads_b, 1)
    lax.fori_loop(1, 16, v2_wait, 0)
    vec_out[...] = jnp.sum(v2r[...], axis=0) + v2s[...]
    gg_four(grads_b, 1)
    swap_wait(lo_send, lo_recv, 3)
    layer_out[...] = lo_recv[...]
    swap_wait(ig_send, ig_recv, 5)
    in_grad[...] = ig_recv[...]
    gg_five(grads_a, 0)
    gg_five(grads_b, 1)

    for n in range(3):
        for r in (1, 2, 3):
            w_y(n, r).wait_send()
        for r in range(4):
            w_x(n, r).wait_send()
    for k, buf in enumerate((normed_all, cot_all, mlp_all, branch_all)):
        for n in range(8):
            ag(buf, k, n).wait_send()
    for k in range(4):
        if k == 3:
            for i in range(4):
                c_sib(k, i).wait_send()
        for n in (0, 1):
            c_far(k, n).wait_send()
            for h in (0, 1):
                c_fin(k, n, h).wait_send()
    for k, buf in enumerate((grads_a, grads_b)):
        for n in range(9):
            gg(buf, k, n).wait_send()


def fused_layer(x, cot, wq, wk, wv, wo, wg, wu, wd, vec, cos, sin, start):
    def vmem(*shape, dtype=BF16):
        return pltpu.VMEM(shape, dtype)

    def dma(*shape):
        return pltpu.SemaphoreType.DMA(shape)

    full = vmem(D, D)
    scratch = [
        vmem(PIECE, D), vmem(PIECE, D), vmem(PIECE, D, dtype=F32), vmem(PIECE, D, dtype=F32),
        vmem(PIECE, D), vmem(D, FB), vmem(D, 2 * FB), vmem(FB, D), vmem(8, 8, 128, dtype=F32),
        full, full, full, full,
        vmem(2, D, 64), vmem(2, D, 64), vmem(2, D, 64), vmem(128, D), vmem(128, D),
        vmem(2, 4, D, BLOCK), vmem(128, D, dtype=F32), vmem(D, 128),
        vmem(D, FB, dtype=F32), vmem(D, FB), vmem(D, 2 * FB), vmem(D, 128, dtype=F32),
        vmem(2, D, 64, dtype=F32), vmem(2, D, 64, dtype=F32), vmem(D, FB),
        vmem(4, BLOCK, D), vmem(4, 4, PIECE, D), vmem(4, PIECE, D), vmem(4, 2, 64, D), vmem(4, 2, PIECE, D), vmem(4, 2, PIECE, D),
        vmem(D, 2 * FB), vmem(FB, D), vmem(128, D), vmem(D, FB),
        vmem(15, 64, 2 * FB), vmem(15, 192, 128), vmem(15, 64, 128), vmem(15, 64, FB), vmem(64, 128), vmem(64, 128),
        vmem(PIECE, D), vmem(PIECE, D), vmem(PIECE, D), vmem(PIECE, D),
        vmem(8, 8, 128, dtype=F32), vmem(7, 8, 128, dtype=F32), vmem(8, 128, dtype=F32), vmem(15, 8, 128, dtype=F32),
        dma(6), dma(6), dma(6), dma(8), dma(8), dma(3, 8), dma(3, 8), dma(4, 8), dma(4, 8),
        dma(4, 4), dma(4, 4), dma(4, 2), dma(4, 2), dma(4, 2, 2), dma(4, 2, 2),
        dma(4, 15), dma(4, 15), dma(2, 9), dma(2, 9), dma(7), dma(7), dma(15), dma(15),
    ]
    anywhere = pl.BlockSpec(memory_space=pl.ANY)
    inside = pl.BlockSpec(memory_space=pltpu.VMEM)
    return pl.pallas_call(
        layer_kernel,
        out_shape=(
            jax.ShapeDtypeStruct((PIECE, D), BF16),
            jax.ShapeDtypeStruct((PIECE, D), BF16),
            jax.ShapeDtypeStruct((16, 64, 1280), BF16),
            jax.ShapeDtypeStruct((16, 64, FB), BF16),
            jax.ShapeDtypeStruct((8, 128), F32),
        ),
        in_specs=[anywhere] * 9 + [inside] * 4,
        out_specs=[inside] * 5,
        scratch_shapes=scratch,
        compiler_params=pltpu.CompilerParams(
            collective_id=0, has_side_effects=True, vmem_limit_bytes=63 * 1024 * 1024
        ),
        name="layer",
    )(x, cot, wq, wk, wv, wo, wg, wu, wd, vec, cos, sin, start)


def per_device(
    inputs, doc_ids, positions, attn_gain, query_weight, key_weight, value_weight,
    query_bias, key_bias, value_bias, out_weight, mlp_gain, gate_weight, up_weight,
    down_weight, cotangent,
):
    del positions
    exponent = jnp.arange(HEAD_DIM // 2, dtype=F32) * (2.0 / HEAD_DIM)
    inverse = jnp.exp(-math.log(THETA) * exponent)
    angles = jnp.arange(D, dtype=F32)[:, None] * inverse
    cos_half, sin_half = jnp.cos(angles), jnp.sin(angles)
    cos = jnp.concatenate([cos_half] * 4, axis=1)
    sin = jnp.concatenate([-sin_half, sin_half] * 2, axis=1)
    seq_here = (lax.axis_index("seq") // 8) * 8 + lax.axis_index("fsdp")
    docs = lax.dynamic_slice_in_dim(doc_ids, seq_here, 1, 0)
    start = jnp.where(docs == 1, jnp.sum(1 - docs, axis=1, keepdims=True), 0)
    zero = jnp.zeros((128,), F32)
    vec = jnp.stack(
        [v.astype(F32) for v in (attn_gain, mlp_gain, query_bias, key_bias, value_bias)] + [zero] * 3
    )
    layer_out, in_grad, grads_a, grads_b, vec_out = fused_layer(
        inputs.reshape(PIECE, D), cotangent.reshape(PIECE, D),
        query_weight, key_weight, value_weight, out_weight, gate_weight, up_weight, down_weight,
        vec, cos, sin, start,
    )
    def rowwise(block):
        return block.reshape(8, 2, 64, -1).transpose(1, 2, 0, 3).reshape(128, -1).astype(F32)

    def cut_windows(block):
        return jnp.concatenate([block[:, : 6 * FB], block[:, 6 * FB : 6 * FB + 256], block[:, 7 * FB + 128 :]], axis=1)

    down = grads_a[:, :, 896:].reshape(8, 2, 64, 3, 128).transpose(0, 1, 3, 2, 4).reshape(8 * FB, 128).astype(F32)
    down = jnp.concatenate([down[: 6 * FB], down[6 * FB : 6 * FB + 256], down[7 * FB + 128 :]], axis=0)
    return (
        layer_out.reshape(inputs.shape),
        in_grad.astype(F32).reshape(inputs.shape),
        vec_out[0],
        rowwise(grads_b[:, :, :128]),
        rowwise(grads_b[:, :, 128:256]),
        rowwise(grads_b[:, :, 256:]),
        vec_out[2],
        vec_out[3],
        vec_out[4],
        rowwise(grads_a[:, :, :128]),
        vec_out[1],
        cut_windows(rowwise(grads_a[:, :, 128:512])),
        cut_windows(rowwise(grads_a[:, :, 512:896])),
        down,
    )


def solution(mesh):
    rows_spec = P("fsdp", None)
    act = P("seq", "fsdp", None)
    vec = P("fsdp")
    return jax.shard_map(
        per_device,
        mesh=mesh,
        in_specs=(
            act, P(), P("seq", "fsdp"), vec, rows_spec, rows_spec, rows_spec, vec, vec, vec,
            rows_spec, vec, rows_spec, rows_spec, P(None, "fsdp"), act,
        ),
        out_specs=(
            act, act, vec, rows_spec, rows_spec, rows_spec, vec, vec, vec, rows_spec, vec,
            rows_spec, rows_spec, P(None, "fsdp"),
        ),
        check_vma=False,
    )
```

time: 2500 us -> 239 us (0.10)
  waiting for transfers between devices: 2070 us -> 0 us
  Pallas kernels: 0 us -> 204 us
  blocking collectives: 178 us -> 0 us
  matrix products: 95.9 us -> 0 us
  other arithmetic: 61.9 us -> 15.9 us
  starting transfers between devices: 40.3 us -> 0 us
    reduce_scatter x4 -> x0, waiting for transfers between devices: 1520 us -> none  [the longest x2 1370 us: per_device(): lax.psum_scatter(jnp.concatenate([first_part, second], axis=1), ('seq', '...]
    all_gather x11 -> x0, waiting for transfers between devices: 522 us -> none  [the longest x1 118 us: per_device(): lax.all_gather(up_weight, 'fsdp', axis=0, tiled=True)]
    pallas_call x0 -> x1, Pallas kernels: none -> 204 us  [fused_layer(): pl.pallas_call(layer_kernel, out_shape=(jax.ShapeDtypeStruct((PIECE, D),...]
    dot_general x24 -> x0, matrix products: 95.9 us -> none  [the longest x4 22.2 us: inner_rows(): lax.dot_general(left_op, right_op, (((0,), (0,)), ((), ())), preferred_el...]
    all_gather x5 -> x0, blocking collectives: 74.1 us -> none  [the longest x1 17.7 us: per_device(): lax.all_gather(mlp_gain, 'fsdp', axis=0, tiled=True)]
    psum x1 -> x0, blocking collectives: 66 us -> none  [per_device(): lax.psum((grad_gain_one, jnp.sum(pre_query.astype(jnp.float32), axis=0),...]
    all_to_all x6 -> x0, starting transfers between devices: 39.2 us -> none  [the longest x1 8.13 us: per_device(): lax.all_to_all(mixed_out, 'seq', split_axis=0, concat_axis=2, tiled=True)]
    all_to_all x2 -> x0, blocking collectives: 37.6 us -> none  [the longest x1 18.8 us: per_device(): lax.all_to_all(value_rows, 'seq', split_axis=2, concat_axis=0, tiled=True)]
  transfers between devices with their start and end apart: 21 -> 0, of which waited for: 17 -> 0; matrix products, arithmetic and copies ran while one was open for 5% -> 0% of each run, Pallas kernels for 0% -> 0%
where the time goes in v1:
time: 239 us; the launch traced here: 235 us
  Pallas kernels  204 us (85%)
  other arithmetic  15.9 us (7%)
  local copies, waits for them, and re-layouts  14.5 us (6%)
    pallas_call x1, Pallas kernels, fused_layer(): pl.pallas_call(layer_kernel, out_shape=(jax.ShapeDtypeStruct((PIECE, D),...  204 us
    unnamed x17, local copies, waits for them, and re-layouts  5.26 us

profile of v1, /device:TPU:1, one launch (start us, length us, event | category | flops | bytes accessed | tf_op | source)
XLA Modules:
  0.0 235.3 jit_solution(14444258620911801493)
XLA Ops:
  0.7 1.4 subtract_reduce_fusion
  2.1 0.7 bitcast_convert_fusion.5
  2.7 0.7 bitcast_convert_fusion.3
  3.4 0.7 bitcast_convert_fusion.1
  4.1 0.6 stack.47.vec_in
  4.7 2.0 compare_select_fusion.start_ref
  6.7 2.0 fusion.2
  8.7 1.8 pad_maximum_fusion.3
  10.5 204.0 %layer.1 = (bf16[128,1024]{1,0:T(8,128)(2,1)}, bf16[128,1024]{1,0:T(8,128)(2,1)}, bf16[16,64,1280]{2,1,0:T(8,128)(2,1)}, bf16[16,64,384]{2,1,0:T(8,128)(2,1)}, f32[8,128]{1,0:T(8,128)}) custom-call(bf16[128,1024]{1,0:T(8,128)(2,1)} %bitcast.106, bf16[128,1024]{1,0:T(8,128)(2,1)} %bitcast.107, bf16[128,1024]{1,0:T(8,128)(2,1)} %wq_in.1, ...), custom_call_target="tpu_custom_call" | custom-call | tf_op jit(solution)/shard_map/layer/pallas_call | solution.py:734
  214.5 1.4 slice_bitcast_fusion
  215.9 1.0 slice.67
  216.9 0.0 copy-start.3
  216.9 0.0 copy-start.1
  216.9 0.3 copy.45
  217.2 0.9 copy.59
  218.1 0.0 copy-done.3
  218.1 0.8 bitcast_convert_fusion
  219.0 0.0 copy-done.1
  219.0 1.8 slice_convert_fusion
  220.7 2.5 %reshape.120 = f32[8,2,64,3,128]{4,3,2,1,0:T(4,128)S(1)} reshape(f32[16,64,384]{2,1,0:T(8,128)} %get-tuple-element.24) | data formatting | bytes 3145728 | tf_op jit(solution)/shard_map/convert_element_type | solution.py:783
  223.2 0.2 copy.48
  223.5 0.1 slice.82
  223.6 0.0 copy-start
  223.6 1.2 pad_maximum_fusion.2
  224.8 0.2 copy-done
  225.0 0.2 convert_bitcast_fusion
  225.2 0.9 copy.47
  226.1 0.3 copy.54
  226.4 0.1 slice.80
  226.5 0.0 copy-start.2
  226.5 1.2 pad_maximum_fusion.1
  227.7 0.2 copy-done.2
  227.9 0.2 fusion.3
  228.2 0.3 copy.43
  228.5 0.9 copy.61
  229.4 0.3 copy.44
  229.7 0.9 copy.60
  230.7 0.3 copy.42
  231.0 0.9 copy.62
  231.9 0.2 convert_bitcast_fusion.1
  232.1 0.9 copy.46
  233.0 0.3 copy.53
  233.3 0.1 slice.78
  233.4 0.0 copy-start.4
  233.4 1.2 pad_maximum_fusion
  234.6 0.0 copy-done.4
  234.6 0.7 copy.64
  (10 shorter events, 0.2 us)
Async XLA Ops:
  216.9 1.3 copy-start.3
  216.9 2.1 copy-start.1
  223.6 1.4 copy-start
  226.5 1.4 copy-start.2
  233.4 1.2 copy-start.4

commit v2 on v1

v2 whole, which is shorter than its diff:
```python
import math

import jax
import jax.numpy as jnp
import numpy as np
from jax import lax
from jax.experimental import pallas as pl
from jax.experimental.pallas import tpu as pltpu
from jax.sharding import PartitionSpec as P

MESH = pl.DeviceIdType.MESH
HEAD_DIM = 64
EPS = 1e-06
THETA = 1000000.0
NEG = -1000000000.0
D = 1024
PIECE = 128
BLOCK = 256
FB = 384
F32 = jnp.float32
BF16 = jnp.bfloat16


def nn(a, b):
    return lax.dot_general(a, b, (((1,), (0,)), ((), ())), preferred_element_type=F32)


def nt(a, b):
    return lax.dot_general(a, b, (((1,), (1,)), ((), ())), preferred_element_type=F32)


def tn(a, b):
    return lax.dot_general(a, b, (((0,), (0,)), ((), ())), preferred_element_type=F32)


def rms_scale(value):
    return lax.rsqrt(jnp.mean(value * value, axis=-1, keepdims=True) + EPS)


def rows(start, size):
    return pl.ds(pl.multiple_of(start, size), size)


def half_turn(value):
    lane = lax.broadcasted_iota(jnp.int32, value.shape, 1)
    ahead = pltpu.roll(value, 96, 1)
    behind = pltpu.roll(value, 32, 1)
    return jnp.where(lane % 64 < 32, ahead, behind)


def layer_kernel(
    x_in, cot_in, wq_in, wk_in, wv_in, wo_in, wg_in, wu_in, wd_in, cos_in, sin_in,
    gain_a, gain_m, bias_q, bias_k, bias_v, docs,
    layer_out, in_grad, all_gu, all_dn, all_wo, all_qkv, vec_out,
    cos_ref, sin_ref, start_ref, vec_in,
    x_own, cot_own, hidden, g_hidden, wo_all, wqkv, wgu, wdn, vall,
    normed_all, cot_all, mlp_all, branch_all,
    q_h, k_h, v_h, k_t, v_t, p_t, mixed_t, mixed, mixed_own,
    g_act, active, active_t, g_gu, g_mixed, gk_acc, gv_acc, g_qkv,
    part, sib, far_s, far_r, fin_s, fin_r,
    dga, dgb, ddn, dwo, dqkv, ra, rb, rd, ha, hb, hd, sa, sb, sd, rwo, rqkv, wo_send, sum_gu, sum_dn, sum_qkv,
    lo_send, ig_send,
    vs, vr, v2s, v2r, v3s, v3r,
    sem_load, swap_s, swap_r, vec_s, vec_r, wy_s, wy_r, wz_s, wz_r, wx_s, wx_r, wp_s, wp_r, mx_s, mx_r, ag_s, ag_r,
    sib_ss, sib_rs, far_ss, far_rs, fin_ss, fin_rs,
    pl_s, pl_r, f1_s, f1_r, f2_s, f2_r, ya_s, ya_r, rg_s, rg_r, gd_s, gd_r, gp_s, gp_r, v1_ss, v1_rs, v2_ss, v2_rs, v3_ss, v3_rs,
):
    s = lax.axis_index("seq")
    f = lax.axis_index("fsdp")
    xh = s // 8
    z = (s % 8) // 2
    c = s % 2
    y = f // 2
    xl = f % 2
    x = xh * 2 + xl
    j = y * 2 + c
    place = z * 2 + xh

    def dev(x_, y_, z_, c_):
        x_, y_, z_ = (x_ + 4) % 4, (y_ + 4) % 4, (z_ + 4) % 4
        return ((x_ // 2) * 8 + z_ * 2 + c_, y_ * 2 + x_ % 2)

    sibling = dev(x, y, z, 1 - c)
    y_up = dev(x, y + 1, z, c)
    y_dn = dev(x, y + 3, z, c)
    moves = (c + xl) % 2
    partner = dev(xh * 2 + 1 - xl, y, z, 1 - c)
    x_to = dev(x + 1 + 2 * c, y, z, c)

    def window(m):
        return (3 * m - 2 * (m // 7)) * 128

    def remote(src, dst, ss, rs, to):
        return pltpu.make_async_remote_copy(
            src_ref=src, dst_ref=dst, send_sem=ss, recv_sem=rs, device_id=to, device_id_type=MESH
        )

    def at(start, size, unit):
        return pl.ds(pl.multiple_of(start, unit), size)

    own_rows = rows(f * 128, 128)
    own_win = at(window(j), FB, 128)
    loads = [
        pltpu.make_async_copy(wq_in.at[:, rows(j * 128, 128)], wqkv.at[own_rows, pl.ds(0, 128)], sem_load.at[0]),
        pltpu.make_async_copy(wk_in.at[:, rows(j * 128, 128)], wqkv.at[own_rows, pl.ds(128, 128)], sem_load.at[1]),
        pltpu.make_async_copy(wv_in.at[:, rows(j * 128, 128)], wqkv.at[own_rows, pl.ds(256, 128)], sem_load.at[2]),
        pltpu.make_async_copy(wo_in, wo_all.at[own_rows], sem_load.at[3]),
        pltpu.make_async_copy(wg_in.at[:, own_win], wgu.at[own_rows, pl.ds(0, FB)], sem_load.at[4]),
        pltpu.make_async_copy(wu_in.at[:, own_win], wgu.at[own_rows, pl.ds(FB, FB)], sem_load.at[5]),
        pltpu.make_async_copy(wd_in.at[own_win, :], wdn.at[:, own_rows], sem_load.at[6]),
        pltpu.make_async_copy(cos_in, cos_ref, sem_load.at[7]),
        pltpu.make_async_copy(sin_in, sin_ref, sem_load.at[8]),
    ]
    for load in loads:
        load.start()

    barrier = pltpu.get_barrier_semaphore()

    def greet(to):
        pl.semaphore_signal(barrier, inc=1, device_id=to, device_id_type=MESH)

    def greet_plane(r, carry):
        greet(dev(x + r // 4, y, z + r % 4, c))
        return carry

    def greet_fsdp(r, carry):
        greet((s, (f + r) % 8))
        return carry

    def greet_cross(r, carry):
        greet(dev(x, y + r, z, 1 - c))
        return carry

    lax.fori_loop(1, 16, greet_plane, 0)
    lax.fori_loop(1, 8, greet_fsdp, 0)
    lax.fori_loop(0, 4, greet_cross, 0)

    @pl.when(moves == 1)
    def _():
        greet(partner)
        pl.semaphore_wait(barrier, 27)

    @pl.when(moves == 0)
    def _():
        pl.semaphore_wait(barrier, 26)

    def swap_start(src, dst, n):
        @pl.when(moves == 1)
        def _():
            remote(src, dst, swap_s.at[n], swap_r.at[n], partner).start()

        @pl.when(moves == 0)
        def _():
            pltpu.make_async_copy(src, dst, swap_r.at[n]).start()

    def swap_wait(src, dst, n):
        @pl.when(moves == 1)
        def _():
            remote(src, dst, swap_s.at[n], swap_r.at[n], partner).wait()

        @pl.when(moves == 0)
        def _():
            pltpu.make_async_copy(src, dst, swap_r.at[n]).wait()

    def vec_copy(r):
        return remote(vec_in, vall.at[f], vec_s.at[r], vec_r.at[r], (s, (f + r) % 8))

    def vec_start(r, carry):
        vec_copy(r).start()
        return carry

    def vec_wait(r, carry):
        vec_copy(r).wait()
        return carry

    vec_in[...] = jnp.zeros_like(vec_in)
    for i, ref in enumerate((gain_a, gain_m, bias_q, bias_k, bias_v)):
        vec_in[i : i + 1, :] = ref[...].astype(F32)
    lax.fori_loop(1, 8, vec_start, 0)
    swap_start(x_in, x_own, 0)
    vall[pl.ds(f, 1)] = vec_in[...][None]
    doc_row = docs[pl.ds(xh * 8 + z * 2 + xl, 1), :]
    start_ref[...] = jnp.where(doc_row == 1, jnp.sum(1 - doc_row, axis=1, keepdims=True), 0)

    PARTS = (3, 2, 1, 1)

    def shard(r):
        return ((y + 4 - r) % 4) * 2 + xl

    def w_quarter(n, f_, q, p=None):
        if n == 0:
            return wqkv.at[at(f_ * 128 + q * 32, 32, 32), slice(None) if p is None else pl.ds(p * 128, 128)]
        if n == 1:
            return wgu.at[at(f_ * 128 + q * 32, 32, 32), slice(None) if p is None else pl.ds(p * FB, FB)]
        if n == 2:
            return wdn.at[at(q * 96, 96, 32), rows(f_ * 128, 128)]
        return wo_all.at[at(f_ * 128 + c * 64 + q * 16, 16, 16)]

    def w_rows(n, f_):
        if n == 0:
            return wqkv.at[rows(f_ * 128, 128)]
        if n == 1:
            return wgu.at[rows(f_ * 128, 128)]
        if n == 2:
            return wdn.at[:, rows(f_ * 128, 128)]
        return wo_all.at[rows(f_ * 128 + c * 64, 64)]

    def w_y(n, p, r, recv=False):
        m = ((y + r) % 4) * 2 + c
        if n == 0:
            src = (wq_in, wk_in, wv_in)[p].at[at(z * 32, 32, 32), rows(m * 128, 128)]
        elif n == 1:
            src = (wg_in, wu_in)[p].at[at(z * 32, 32, 32), at(window(m), FB, 128)]
        elif n == 2:
            src = wd_in.at[at(window(m) + z * 96, 96, 32), :]
        else:
            src = wo_in.at[at(c * 64 + z * 16, 16, 16)]
        dst = w_quarter(n, shard(r) if recv else f, z, p)
        return remote(src, dst, wy_s.at[n, p, r], wy_r.at[n, p, r], dev(x, y + r, z, c))

    def w_z(n, r, dz, recv=False):
        src = w_quarter(n, shard(r), z)
        dst = w_quarter(n, shard(r), (z + 4 - dz) % 4) if recv else src
        return remote(src, dst, wz_s.at[n, r, dz], wz_r.at[n, r, dz], dev(x, y, z + dz, c))

    def w_x(n, r, recv=False):
        src = w_rows(n, shard(r))
        dst = w_rows(n, ((y + 4 - r) % 4) * 2 + 1 - xl) if recv else src
        return remote(src, dst, wx_s.at[n, r], wx_r.at[n, r], x_to)

    def w_ystart(n):
        for r in (1, 3, 2):
            for p in range(PARTS[n]):
                w_y(n, p, r).start()

    def w_own(n):
        for load in (loads[:3], loads[4:6], loads[6:7], loads[3:4])[n]:
            load.wait()
        w_x(n, 0).start()

    def w_zstart(n):
        for r in (1, 3, 2):
            for p in range(PARTS[n]):
                w_y(n, p, r, True).wait_recv()
            for dz in (1, 3, 2):
                w_z(n, r, dz).start()

    def w_xstart(n):
        for r in (1, 3, 2):
            for dz in (1, 3, 2):
                w_z(n, r, dz, True).wait_recv()
            w_x(n, r).start()
            if n == 3:
                wo_pass(2 * ((4 - r) % 4)).start()

    def w_finish(n):
        for r in range(4):
            w_x(n, r, True).wait_recv()

    def wo_pass(n, recv=False):
        f_ = ((y + n // 2) % 4) * 2 + (xl + n % 2) % 2
        ref = wo_all.at[rows(f_ * 128 + ((1 - c) if recv else c) * 64, 64)]
        return remote(ref, ref, wp_s.at[n], wp_r.at[n], sibling)

    def wo_pass_x():
        for r in range(4):
            w_x(3, r, True).wait_recv()
            wo_pass(2 * ((4 - r) % 4) + 1).start()

    def wo_pass_finish():
        for n in range(1, 8):
            wo_pass(n, True).wait_recv()

    for n in (0, 3, 1, 2):
        w_ystart(n)
    w_own(0)

    def piece(buf, y_, c_):
        return buf.at[rows((((y_ + 4) % 4) * 2 + c_) * PIECE, PIECE)]

    def half(buf, y_, c_, h):
        return buf.at[rows((((y_ + 4) % 4) * 2 + c_) * PIECE + h * 64, 64)]

    def ag(buf, k, n, recv=False):
        if n == 0:
            ref, to = (piece(buf, y - 1, c) if recv else piece(buf, y, c)), y_up
        elif n == 1:
            ref, to = (piece(buf, y + 1, c) if recv else piece(buf, y, c)), y_dn
        elif n == 2:
            ref, to = (piece(buf, y, 1 - c) if recv else piece(buf, y, c)), sibling
        elif n == 3:
            ref, to = (half(buf, y - 2, c, 0) if recv else half(buf, y - 1, c, 0)), y_up
        elif n == 4:
            ref, to = (piece(buf, y - 1, 1 - c) if recv else piece(buf, y - 1, c)), sibling
        elif n == 5:
            ref, to = (half(buf, y + 2, c, 1) if recv else half(buf, y + 1, c, 1)), y_dn
        elif n == 6:
            ref, to = (piece(buf, y + 1, 1 - c) if recv else piece(buf, y + 1, c)), sibling
        else:
            ref, to = (piece(buf, y + 2, 1 - c) if recv else piece(buf, y + 2, c)), sibling
        return remote(ref, ref, ag_s.at[k, n], ag_r.at[k, n], to)

    def ag_start(buf, k):
        for n in range(3):
            ag(buf, k, n).start()

    def ag_near(buf, k):
        ag(buf, k, 0, True).wait_recv()
        ag(buf, k, 3).start()
        ag(buf, k, 4).start()
        ag(buf, k, 1, True).wait_recv()
        ag(buf, k, 5).start()
        ag(buf, k, 6).start()

    def ag_far(buf, k):
        ag(buf, k, 3, True).wait_recv()
        ag(buf, k, 5, True).wait_recv()
        ag(buf, k, 7).start()

    def ag_run(buf, k, consume, after_far=None):
        def step(i, carry):
            @pl.when(i == 0)
            def _():
                ag(buf, k, 2, True).wait_recv()

            @pl.when(i == 1)
            def _():
                ag_near(buf, k)
                ag(buf, k, 4, True).wait_recv()

            @pl.when(i == 2)
            def _():
                ag(buf, k, 6, True).wait_recv()

            @pl.when(i == 3)
            def _():
                ag_far(buf, k)
                if after_far is not None:
                    after_far()
                ag(buf, k, 7, True).wait_recv()

            consume((y + (3 * ((i * (i + 1)) // 2)) % 4) % 4)
            return carry

        lax.fori_loop(0, 4, step, 0)

    def other(i):
        return part.at[i, rows((1 - c) * PIECE, PIECE)]

    def own_part(i):
        return part[i, rows(c * PIECE, PIECE), :].astype(F32)

    def c_sib(k, i):
        return remote(other(i), sib.at[k, i], sib_ss.at[k, i], sib_rs.at[k, i], sibling)

    def c_far(k, n):
        return remote(far_s.at[k, pl.ds(64 * n, 64)], far_r.at[k, n], far_ss.at[k, n], far_rs.at[k, n], y_up if n == 0 else y_dn)

    def c_fin(k, n, h):
        cut = pl.ds(64 * h, 64)
        return remote(fin_s.at[k, n, cut], fin_r.at[k, n, cut], fin_ss.at[k, n, h], fin_rs.at[k, n, h], y_up if n == 0 else y_dn)

    def rs_far(k):
        c_sib(k, 0).wait_recv()
        far_s[k] = (own_part(0) + sib[k, 0].astype(F32)).astype(BF16)
        c_far(k, 0).start()
        c_far(k, 1).start()

    def rs_near(k, n):
        c_sib(k, 1 + n).wait_recv()
        fin_s[k, n] = (own_part(1 + n) + sib[k, 1 + n].astype(F32)).astype(BF16)
        c_fin(k, n, 1 - n).start()

    def rs_start(k, produce, eager=True):
        def step(i, carry):
            if k > 1:
                c_sib(k - 1, i).wait_send()
            part[i] = produce((y + (2 - (i * (i + 1)) // 2 + 8) % 4) % 4).astype(BF16)
            c_sib(k, i).start()
            if eager:
                @pl.when(i == 1)
                def _():
                    rs_far(k)

                @pl.when(i == 2)
                def _():
                    rs_near(k, 0)

                @pl.when(i == 3)
                def _():
                    rs_near(k, 1)

            return carry

        lax.fori_loop(0, 4, step, 0)

    def rs_mid(k):
        for n in (0, 1):
            c_far(k, n).wait_recv()
            cut = pl.ds(64 * n, 64)
            fin_s[k, n, cut] = (fin_s[k, n, cut].astype(F32) + far_r[k, n].astype(F32)).astype(BF16)
            c_fin(k, n, n).start()

    def rs_finish(k):
        c_sib(k, 3).wait_recv()
        total = own_part(3) + sib[k, 3].astype(F32)
        for n in (0, 1):
            for h in (0, 1):
                c_fin(k, n, h).wait_recv()
        return total + fin_r[k, 0].astype(F32) + fin_r[k, 1].astype(F32)

    w_zstart(0)
    lax.fori_loop(1, 8, vec_wait, 0)

    def gathered(row):
        return jnp.concatenate([vall[i, row : row + 1, :] for i in range(8)], axis=1)

    swap_wait(x_in, x_own, 0)
    x32 = x_own[...].astype(F32)
    normed_all[rows(j * PIECE, PIECE), :] = (x32 * rms_scale(x32) * gathered(0)).astype(BF16)
    ag_start(normed_all, 0)
    w_xstart(0)
    swap_start(cot_in, cot_own, 1)
    w_zstart(3)
    w_own(3)
    w_zstart(1)
    w_own(1)
    w_zstart(2)
    w_own(2)
    for load in loads[7:]:
        load.wait()
    w_finish(0)

    def project(yy):
        cut = rows(yy * BLOCK, BLOCK)
        lin = nn(normed_all[cut, :], wqkv[...])
        cos = cos_ref[cut, :]
        sin = sin_ref[cut, :]
        bias = vall[pl.ds(j, 1)][0]
        q_lin = lin[:, :128] + bias[2:3, :]
        k_lin = lin[:, 128:256] + bias[3:4, :]
        v_lin = lin[:, 256:] + bias[4:5, :]
        q = (q_lin * cos + half_turn(q_lin) * sin).astype(BF16) * 0.125
        k32 = k_lin * cos + half_turn(k_lin) * sin
        k = k32.astype(BF16)
        v = v_lin.astype(BF16)
        for h in range(2):
            lanes = slice(64 * h, 64 * h + 64)
            q_h[h, cut, :] = q[:, lanes]
            k_h[h, cut, :] = k[:, lanes]
            v_h[h, cut, :] = v[:, lanes]
        k_t[:, cut] = k32.T.astype(BF16)
        v_t[:, cut] = v_lin.T.astype(BF16)

    def cot_start():
        swap_wait(cot_in, cot_own, 1)
        cot_all[rows(j * PIECE, PIECE), :] = cot_own[...]
        ag_start(cot_all, 1)

    ag_run(normed_all, 0, project, cot_start)

    def attend(i):
        width = (i + 1) * BLOCK
        cut = slice(i * BLOCK, (i + 1) * BLOCK)
        key_at = lax.broadcasted_iota(jnp.int32, (width, BLOCK), 0)
        query_at = lax.broadcasted_iota(jnp.int32, (width, BLOCK), 1) + i * BLOCK
        allowed = (key_at >= start_ref[0:1, cut]) & (key_at <= query_at)
        for h in range(2):
            scores = nt(k_h[h, :width, :], q_h[h, cut, :])
            scores = jnp.where(allowed, scores, NEG)
            weights = jnp.exp(scores - jnp.max(scores, axis=0, keepdims=True))
            inverse = 1.0 / jnp.sum(weights, axis=0, keepdims=True)
            probs = (weights * inverse).astype(BF16)
            p_t[h, i, :width, :] = probs
            mixed_t[64 * h : 64 * h + 64, cut] = nn(v_t[64 * h : 64 * h + 64, :width], probs)
        mixed[cut, :] = mixed_t[:, cut].T.astype(BF16)
        for m in (2 * i, 2 * i + 1):
            mix_start(m)

    def mix(m, sender):
        return remote(
            mixed.at[rows(m * PIECE, PIECE), :], mixed_own.at[:, rows(sender * 128, 128)],
            mx_s.at[m], mx_r.at[sender], dev(x, m // 2, z, m % 2),
        )

    def mix_start(m):
        @pl.when(j != m)
        def _():
            mix(m, j).start()

        @pl.when(j == m)
        def _():
            mixed_own[:, rows(j * 128, 128)] = mixed[m * PIECE : (m + 1) * PIECE, :]

    def mix_wait(r, carry):
        m = (j + r) % 8
        mix(m, m).wait_recv()
        mix(m, j).wait_send()
        return carry

    w_xstart(3)
    attend(0)
    w_xstart(2)
    attend(1)
    w_xstart(1)
    attend(2)
    wo_pass_x()
    attend(3)
    ag_near(cot_all, 1)
    wo_pass_finish()
    lax.fori_loop(1, 8, mix_wait, 0)

    hidden[...] = x_own[...].astype(F32) + nn(mixed_own[...], wo_all[...])
    hid = hidden[...]
    mlp_all[rows(j * PIECE, PIECE), :] = (hid * rms_scale(hid) * gathered(1)).astype(BF16)
    ag_start(mlp_all, 2)
    ag_far(cot_all, 1)
    w_finish(2)
    for n in (2, 4, 6, 7):
        ag(cot_all, 1, n, True).wait_recv()

    def active_back(i, carry):
        cut = rows(i * BLOCK, BLOCK)
        g_act[cut, :] = nt(cot_all[cut, :], wdn[...])
        return carry

    lax.fori_loop(0, 4, active_back, 0)
    w_finish(1)

    unit = lax.broadcasted_iota(jnp.int32, (1, FB), 1)
    low_edge = 128 * (j // 7)
    high_edge = FB - 128 * ((j // 6) * (1 - j // 7))
    live = (unit >= low_edge) & (unit < high_edge)

    def feed(yy):
        cut = rows(yy * BLOCK, BLOCK)
        both = nn(mlp_all[cut, :], wgu[...])
        gate = both[:, :FB]
        up = both[:, FB:]
        sig = 1.0 / (1.0 + jnp.exp(-gate))
        silu = gate * sig
        back = jnp.where(live, g_act[cut, :], 0.0)
        act = jnp.where(live, silu * up, 0.0)
        active[cut, :] = act.astype(BF16)
        active_t[:, cut] = act.T.astype(BF16)
        g_gu[cut, :FB] = (back * up * sig * (1.0 + gate * (1.0 - sig))).astype(BF16)
        g_gu[cut, FB:] = (back * silu).astype(BF16)

    ag_run(mlp_all, 2, feed)
    rs_start(1, lambda yy: nt(g_gu[rows(yy * BLOCK, BLOCK), :], wgu[...]))

    def plane(n, r):
        x_, z_ = (x + r // 4) % 4, (z + r % 4) % 4
        src = (dwo, dqkv)[n].at[x_ * 4 + z_]
        dst = (rwo, rqkv)[n].at[r - 1]
        return remote(src, dst, pl_s.at[n, r - 1], pl_r.at[n, r - 1], dev(x_, y, z_, c))

    def plane_start(n):
        def go(r, carry):
            plane(n, r).start()
            return carry

        lax.fori_loop(1, 16, go, 0)

    def plane_sum(n):
        own, recv = ((dwo, rwo), (dqkv, rqkv))[n]

        def go(r, total):
            plane(n, r).wait()
            return total + recv[r - 1].astype(F32)

        return lax.fori_loop(1, 16, go, own[x * 4 + z].astype(F32))

    def first(n, r):
        if n == 0:
            src, to = dga.at[(x + r) % 4], dev(x + r, y, z, c)
        else:
            src, to = (dgb, ddn)[n - 1].at[:, (z + r) % 4], dev(x, y, z + r, c)
        return remote(src, (ra, rb, rd)[n].at[r - 1], f1_s.at[n, r], f1_r.at[n, r], to)

    def second(n, r):
        src = (ha, hb, hd)[n].at[((z if n == 0 else x) + r) % 4]
        to = dev(x, y, z + r, c) if n == 0 else dev(x + r, y, z, c)
        return remote(src, (sa, sb, sd)[n].at[r - 1], f2_s.at[n, r], f2_r.at[n, r], to)

    def first_start(n):
        for r in (1, 3, 2):
            first(n, r).start()

    def first_sum(n):
        total = (dga[x] if n == 0 else (dgb, ddn)[n - 1][:, z]).astype(F32)
        for r in (1, 3, 2):
            first(n, r).wait()
            total = total + (ra, rb, rd)[n][r - 1].astype(F32)
        (ha, hb, hd)[n][...] = total.astype(BF16)
        for r in (1, 3, 2):
            second(n, r).start()

    def second_sum(n):
        total = (ha, hb, hd)[n][z if n == 0 else x].astype(F32)
        for r in (1, 3, 2):
            second(n, r).wait()
            total = total + (sa, sb, sd)[n][r - 1].astype(F32)
        return total.astype(BF16)

    def chunk(t, xl_):
        return (t % 2) * 2 + xl_, t // 2

    def grad_gu(i, carry):
        got = tn(mlp_all[:, rows(i * BLOCK, BLOCK)], g_gu[...]).astype(BF16)
        for xl_ in range(2):
            for t in range(8):
                x_, z_ = chunk(t, xl_)
                share = got[xl_ * 128 + t * 16 : xl_ * 128 + t * 16 + 16]
                dga[x_, z_, i] = share[:, :512]
                dgb[x_, z_, i] = share[:, 512:]
        return carry

    def grad_dn(i, carry):
        got = nn(active_t[...], cot_all[:, rows(i * BLOCK, BLOCK)]).astype(BF16)
        for xl_ in range(2):
            for t in range(8):
                x_, z_ = chunk(t, xl_)
                ddn[x_, z_, i] = got[t * 48 : t * 48 + 48, xl_ * 128 : xl_ * 128 + 128]
        return carry

    def grad_qkv(i, carry):
        got = tn(normed_all[:, rows(i * BLOCK, BLOCK)], g_qkv[...]).astype(BF16)
        for xl_ in range(2):
            for t in range(8):
                x_, z_ = chunk(t, xl_)
                dqkv[x_ * 4 + z_, i] = got[xl_ * 128 + t * 16 : xl_ * 128 + t * 16 + 16]
        return carry

    def grad_wo():
        got = tn(mixed[...], branch_all[...]).astype(BF16)
        for h in range(2):
            for t in range(8):
                to = ((t % 2) * 2 + (h + c) % 2) * 4 + t // 2
                dwo[pl.ds(to, 1)] = got[h * 64 : h * 64 + 64, t * 128 : t * 128 + 128][None]

    lax.fori_loop(0, 2, grad_gu, 0)
    rs_mid(1)
    lax.fori_loop(2, 4, grad_gu, 0)
    first_start(1)
    first_start(0)
    lax.fori_loop(0, 4, grad_dn, 0)
    first_start(2)

    grad = rs_finish(1)
    hid = hidden[...]
    scale = rms_scale(hid)
    scaled = grad * gathered(1)
    back = scale * scaled - hid * (scale * scale * scale) * jnp.mean(scaled * hid, axis=-1, keepdims=True)
    gain_two = jnp.sum(grad * hid * scale, axis=0, keepdims=True)
    g_hidden[...] = cot_own[...].astype(F32) + back
    branch_all[rows(j * PIECE, PIECE), :] = g_hidden[...].astype(BF16)
    ag_start(branch_all, 3)

    def mixed_back(yy):
        cut = rows(yy * BLOCK, BLOCK)
        g_mixed[cut, :] = nt(branch_all[cut, :], wo_all[rows(j * 128, 128), :])

    gk_acc[...] = jnp.zeros_like(gk_acc)
    gv_acc[...] = jnp.zeros_like(gv_acc)
    ag_run(branch_all, 3, mixed_back)
    for n in (1, 0, 2):
        first_sum(n)
    rs_start(2, lambda yy: nn(active[rows(yy * BLOCK, BLOCK), :], wdn[...]), eager=False)

    def along_y(n, r, recv=False):
        src = (sum_gu, sum_dn, sum_qkv)[n].at[(y + r) % 4]
        dst = (all_gu, all_dn, all_qkv)[n].at[place, c, (y + 4 - r) % 4 if recv else y]
        return remote(src, dst, ya_s.at[n, r], ya_r.at[n, r], dev(x, y + r, z, c))

    def share(n):
        total, every = ((sum_gu, all_gu), (sum_dn, all_dn), (sum_qkv, all_qkv))[n]
        if n == 0:
            total[:, :, :512] = second_sum(0)
            total[:, :, 512:] = second_sum(1)
        elif n == 1:
            total[...] = second_sum(2)
        else:
            total[...] = plane_sum(1).astype(BF16)
        for r in (1, 3, 2):
            along_y(n, r).start()
        every[place, c, y] = total[y]

    arrays = (all_gu, all_dn, all_wo, all_qkv)

    def spot(n, r, c_):
        return arrays[n].at[((z + 4 - r % 4) % 4) * 2 + (xh + r // 4) % 2, c_]

    def gd(n, r, recv=False):
        ref = spot(n, r if recv else 0, c)
        return remote(ref, ref, gd_s.at[n, r], gd_r.at[n, r], dev(x + 2 * (r // 4), y, z + r % 4, c))

    def gp(n, r, recv=False):
        ref = spot(n, r, (1 - c) if recv else c)
        return remote(ref, ref, gp_s.at[n, r], gp_r.at[n, r], sibling)

    def pair(n, z_, c_):
        return arrays[n].at[pl.ds(((z_ + 4) % 4) * 2, 2), c_]

    def single(n, z_, h):
        return arrays[n].at[pl.ds(((z_ + 4) % 4) * 2 + h, 1), c]

    def ring(n, k, recv=False):
        if k == 0:
            ref, to = single(n, z, (1 - xh) if recv else xh), dev(x + 2, y, z, c)
        elif k == 1:
            ref, to = pair(n, z - 1 if recv else z, c), dev(x, y, z + 1, c)
        elif k == 2:
            ref, to = pair(n, z + 1 if recv else z, c), dev(x, y, z + 3, c)
        elif k == 3:
            ref, to = single(n, z - 2 if recv else z - 1, 0), dev(x, y, z + 1, c)
        elif k == 4:
            ref, to = single(n, z + 2 if recv else z + 1, 1), dev(x, y, z + 3, c)
        else:
            ref, to = pair(n, z + (k - 5), (1 - c) if recv else c), sibling
        return remote(ref, ref, rg_s.at[n, k], rg_r.at[n, k], to)

    def ring_one(n):
        for r in (1, 3, 2):
            along_y(n, r, True).wait_recv()
        ring(n, 0).start()

    def ring_two(n):
        ring(n, 0, True).wait_recv()
        for k in (1, 2, 5):
            ring(n, k).start()

    def ring_three(n):
        ring(n, 1, True).wait_recv()
        ring(n, 3).start()
        ring(n, 8).start()
        ring(n, 2, True).wait_recv()
        ring(n, 4).start()
        ring(n, 6).start()

    def ring_four(n):
        ring(n, 3, True).wait_recv()
        ring(n, 4, True).wait_recv()
        ring(n, 7).start()

    def ring_five(n):
        for k in (5, 6, 7, 8):
            ring(n, k, True).wait_recv()

    def spread_start(n):
        if n != 2:
            for r in (1, 3, 2):
                along_y(min(n, 2), r, True).wait_recv()
        for r in (2, 1, 3, 6, 5, 7, 4):
            gd(n, r).start()
        gp(n, 0).start()

    def spread_pass(n):
        for r in (1, 3, 2, 4, 5, 7, 6):
            gd(n, r, True).wait_recv()
            gp(n, r).start()

    def spread_finish(n):
        for r in range(8):
            gp(n, r, True).wait_recv()

    def unturn(value, cut):
        value = value.astype(BF16).astype(F32)
        return (value * cos_ref[cut, :] - half_turn(value) * sin_ref[cut, :]).astype(BF16)

    def attend_back(i):
        width = (i + 1) * BLOCK
        cut = slice(i * BLOCK, (i + 1) * BLOCK)
        grad_t = g_mixed[cut, :].T
        grad_bf = g_mixed[cut, :].astype(BF16)
        products = grad_t * mixed_t[:, cut]
        queries_t = []
        for h in range(2):
            lanes = slice(64 * h, 64 * h + 64)
            grad_h = grad_bf[:, lanes]
            delta = jnp.sum(products[lanes, :], axis=0, keepdims=True)
            probs = p_t[h, i, :width, :]
            gv_acc[h, :width, :] += nn(probs, grad_h)
            g_probs = nt(v_h[h, :width, :], grad_h)
            g_scores = (probs.astype(F32) * (g_probs - delta)).astype(BF16)
            gk_acc[h, :width, :] += nn(g_scores, q_h[h, cut, :])
            queries_t.append(nn(k_t[lanes, :width], g_scores))
        g_query = (jnp.concatenate(queries_t, axis=0) * 0.125).T
        g_qkv[cut, :128] = unturn(g_query, cut)

    attend_back(0)
    rs_far(2)
    attend_back(1)
    rs_near(2, 0)
    rs_near(2, 1)
    attend_back(2)
    rs_mid(2)
    share(0)
    share(1)
    attend_back(3)
    for i in range(4):
        cut = slice(i * BLOCK, (i + 1) * BLOCK)
        g_qkv[cut, 128:256] = unturn(jnp.concatenate([gk_acc[0, cut, :], gk_acc[1, cut, :]], axis=1), cut)
        g_qkv[cut, 256:] = jnp.concatenate([gv_acc[0, cut, :], gv_acc[1, cut, :]], axis=1).astype(BF16)
    lo_last = own_part(3)
    rs_start(3, lambda yy: nt(g_qkv[rows(yy * BLOCK, BLOCK), :], wqkv[...]))
    lax.fori_loop(0, 4, grad_qkv, 0)
    plane_start(1)
    ring_one(0)
    ring_one(1)
    rs_mid(3)
    grad_wo()
    plane_start(0)
    ring_two(0)
    ring_two(1)

    c_sib(2, 3).wait_recv()
    for n in (0, 1):
        for h in (0, 1):
            c_fin(2, n, h).wait_recv()
    lo_send[...] = (
        hidden[...] + lo_last + sib[2, 3].astype(F32) + fin_r[2, 0].astype(F32) + fin_r[2, 1].astype(F32)
    ).astype(BF16)
    swap_start(lo_send, layer_out, 2)

    ring_three(0)
    ring_three(1)

    grad = rs_finish(3)
    scale = rms_scale(x32)
    scaled = grad * gathered(0)
    back = scale * scaled - x32 * (scale * scale * scale) * jnp.mean(scaled * x32, axis=-1, keepdims=True)
    gain_one = jnp.sum(grad * x32 * scale, axis=0, keepdims=True)
    ig_send[...] = (g_hidden[...] + back).astype(BF16)
    swap_start(ig_send, in_grad, 3)

    vs[...] = jnp.zeros_like(vs)
    for i in range(8):
        vs[i, 0:1, :] = gain_one[:, 128 * i : 128 * i + 128]
        vs[i, 1:2, :] = gain_two[:, 128 * i : 128 * i + 128]
    bias_sum = jnp.sum(g_qkv[...].astype(F32), axis=0, keepdims=True)
    for i in range(3):
        vs[pl.ds(j, 1), 2 + i : 3 + i, :] = bias_sum[:, 128 * i : 128 * i + 128][None]

    def v1_copy(r):
        return remote(vs.at[(f + r) % 8], vr.at[r - 1], v1_ss.at[r - 1], v1_rs.at[r - 1], (s, (f + r) % 8))

    def v1_start(r, carry):
        v1_copy(r).start()
        return carry

    def v1_wait(r, carry):
        v1_copy(r).wait()
        return carry

    lax.fori_loop(1, 8, v1_start, 0)
    share(2)
    wo_send[...] = plane_sum(0).astype(BF16)
    swap_start(wo_send, all_wo.at[place, (c + moves) % 2], 4)
    lax.fori_loop(1, 8, v1_wait, 0)
    v2s[...] = jnp.sum(vr[...], axis=0) + vs[pl.ds(f, 1)][0]

    def v2_copy(r):
        to = dev(x + 2 * (r // 4), y, z + r % 4, c)
        return remote(v2s, v2r.at[r - 1], v2_ss.at[r - 1], v2_rs.at[r - 1], to)

    def v2_start(r, carry):
        v2_copy(r).start()
        return carry

    def v2_wait(r, carry):
        v2_copy(r).wait()
        return carry

    lax.fori_loop(1, 8, v2_start, 0)
    spread_start(3)
    swap_wait(wo_send, all_wo.at[place, c], 4)
    spread_start(2)
    lax.fori_loop(1, 8, v2_wait, 0)
    v3s[...] = jnp.sum(v2r[...], axis=0) + v2s[...]
    v3_copy = remote(v3s, v3r, v3_ss.at[0], v3_rs.at[0], sibling)
    v3_copy.start()
    ring_four(0)
    ring_four(1)
    for n in (3, 2):
        spread_pass(n)
    v3_copy.wait()
    vec_out[...] = v3s[...] + v3r[...]
    swap_wait(lo_send, layer_out, 2)
    swap_wait(ig_send, in_grad, 3)
    for n in (0, 1):
        ring_five(n)
    for n in (3, 2):
        spread_finish(n)

    for n in range(4):
        for r in (1, 2, 3):
            for p in range(PARTS[n]):
                w_y(n, p, r).wait_send()
            for dz in (1, 2, 3):
                w_z(n, r, dz).wait_send()
        for r in range(4):
            w_x(n, r).wait_send()
    for n in range(1, 8):
        wo_pass(n).wait_send()
    for k, buf in enumerate((normed_all, cot_all, mlp_all, branch_all)):
        for n in range(8):
            ag(buf, k, n).wait_send()
    for k in range(1, 4):
        if k == 3:
            for i in range(4):
                c_sib(k, i).wait_send()
        for n in (0, 1):
            c_far(k, n).wait_send()
            for h in (0, 1):
                c_fin(k, n, h).wait_send()
    for n in range(3):
        for r in (1, 2, 3):
            along_y(n, r).wait_send()
    for n in (0, 1):
        for k in range(9):
            ring(n, k).wait_send()
    for n in (2, 3):
        for r in range(8):
            if r > 0:
                gd(n, r).wait_send()
            gp(n, r).wait_send()


def fused_layer(*args):
    def vmem(*shape, dtype=BF16):
        return pltpu.VMEM(shape, dtype)

    def dma(*shape):
        return pltpu.SemaphoreType.DMA(shape)

    full = vmem(D, D)
    scratch = [
        vmem(D, 128, dtype=F32), vmem(D, 128, dtype=F32), vmem(1, D, dtype=jnp.int32), vmem(8, 128, dtype=F32),
        vmem(PIECE, D), vmem(PIECE, D), vmem(PIECE, D, dtype=F32), vmem(PIECE, D, dtype=F32),
        full, vmem(D, FB), vmem(D, 2 * FB), vmem(FB, D), vmem(8, 8, 128, dtype=F32),
        full, full, full, full,
        vmem(2, D, 64), vmem(2, D, 64), vmem(2, D, 64), vmem(128, D), vmem(128, D),
        vmem(2, 4, D, BLOCK), vmem(128, D, dtype=F32), vmem(D, 128), vmem(PIECE, D),
        vmem(D, FB, dtype=F32), vmem(D, FB), vmem(FB, D), vmem(D, 2 * FB), vmem(D, 128, dtype=F32),
        vmem(2, D, 64, dtype=F32), vmem(2, D, 64, dtype=F32), vmem(D, FB),
        vmem(4, BLOCK, D), vmem(4, 4, PIECE, D), vmem(4, PIECE, D), vmem(4, 2, 64, D), vmem(4, 2, PIECE, D), vmem(4, 2, PIECE, D),
        vmem(4, 4, 4, 16, 512), vmem(4, 4, 4, 16, 256), vmem(4, 4, 4, 48, 128), vmem(16, 64, 128), vmem(16, 4, 16, FB),
        vmem(3, 4, 4, 16, 512), vmem(3, 4, 4, 16, 256), vmem(3, 4, 4, 48, 128),
        vmem(4, 4, 16, 512), vmem(4, 4, 16, 256), vmem(4, 4, 48, 128),
        vmem(3, 4, 16, 512), vmem(3, 4, 16, 256), vmem(3, 4, 48, 128),
        vmem(15, 64, 128), vmem(15, 4, 16, FB),
        vmem(64, 128), vmem(4, 16, 2 * FB), vmem(4, 48, 128), vmem(4, 16, FB),
        vmem(PIECE, D), vmem(PIECE, D),
        vmem(8, 8, 128, dtype=F32), vmem(7, 8, 128, dtype=F32), vmem(8, 128, dtype=F32), vmem(7, 8, 128, dtype=F32),
        vmem(8, 128, dtype=F32), vmem(8, 128, dtype=F32),
        dma(9), dma(5), dma(5), dma(8), dma(8), dma(4, 3, 4), dma(4, 3, 4), dma(4, 4, 4), dma(4, 4, 4), dma(4, 4), dma(4, 4),
        dma(8), dma(8), dma(8), dma(8), dma(4, 8), dma(4, 8),
        dma(4, 4), dma(4, 4), dma(4, 2), dma(4, 2), dma(4, 2, 2), dma(4, 2, 2),
        dma(2, 15), dma(2, 15), dma(3, 4), dma(3, 4), dma(3, 4), dma(3, 4), dma(3, 4), dma(3, 4), dma(2, 9), dma(2, 9), dma(4, 8), dma(4, 8), dma(4, 8), dma(4, 8),
        dma(7), dma(7), dma(7), dma(7), dma(1), dma(1),
    ]
    anywhere = pl.BlockSpec(memory_space=pl.ANY)
    inside = pl.BlockSpec(memory_space=pltpu.VMEM)

    def out(*shape, dtype=BF16):
        return jax.ShapeDtypeStruct(shape, dtype)

    return pl.pallas_call(
        layer_kernel,
        out_shape=(
            out(PIECE, D), out(PIECE, D), out(8, 2, 4, 16, 2 * FB), out(8, 2, 4, 48, 128), out(8, 2, 64, 128),
            out(8, 2, 4, 16, FB), out(8, 128, dtype=F32),
        ),
        in_specs=[anywhere] * 11 + [inside] * 6,
        out_specs=[inside] * 7,
        scratch_shapes=scratch,
        compiler_params=pltpu.CompilerParams(
            collective_id=0, has_side_effects=True, vmem_limit_bytes=63 * 1024 * 1024
        ),
        name="layer",
    )(*args)


def spread_kernel(
    lo_in, ig_in, gu_in, dn_in, wo_in, qkv_in, vec_in,
    lo, ig, d_gain_a, d_q, d_k, d_v, d_bq, d_bk, d_bv, d_o, d_gain_m, d_gate, d_up, d_down,
    lo_v, ig_v, gu, dn, wo, qkv, vec, sems,
):
    loads = [
        pltpu.make_async_copy(src, dst, sems.at[i])
        for i, (src, dst) in enumerate(
            ((vec_in, vec), (qkv_in, qkv), (wo_in, wo), (gu_in, gu), (dn_in, dn), (ig_in, ig_v), (lo_in, lo_v))
        )
    ]
    for load in loads:
        load.start()
    loads[0].wait()
    for ref, row in ((d_gain_a, 0), (d_gain_m, 1), (d_bq, 2), (d_bk, 3), (d_bv, 4)):
        ref[...] = vec[row : row + 1, :]
    loads[1].wait()
    for t in range(8):
        cut = slice(16 * t, 16 * t + 16)
        for m in range(8):
            for i, ref in enumerate((d_q, d_k, d_v)):
                ref[cut, 128 * m : 128 * m + 128] = qkv[t, m % 2, m // 2, :, 128 * i : 128 * i + 128].astype(F32)
    loads[2].wait()
    flip = lax.axis_index("fsdp") % 2
    for t in range(8):
        for core in range(2):
            to = pl.ds(pl.multiple_of(64 * ((core + flip) % 2), 64), 64)
            d_o[to, 128 * t : 128 * t + 128] = wo[t, core].astype(F32)
    loads[3].wait()
    loads[4].wait()
    for m in range(8):
        first = 128 if m == 7 else 0
        count = 256 if m >= 6 else FB
        start = min(m, 6) * FB + (256 if m == 7 else 0)
        for t in range(8):
            cut = slice(16 * t, 16 * t + 16)
            d_gate[cut, start : start + count] = gu[t, m % 2, m // 2, :, first : first + count].astype(F32)
            d_up[cut, start : start + count] = gu[t, m % 2, m // 2, :, FB + first : FB + first + count].astype(F32)
            low, high = max(48 * t, first), min(48 * t + 48, first + count)
            if low < high:
                d_down[start + low - first : start + high - first, :] = dn[
                    t, m % 2, m // 2, low - 48 * t : high - 48 * t, :
                ].astype(F32)
    loads[5].wait()
    ig[...] = ig_v[...].astype(F32)
    loads[6].wait()
    lo[...] = lo_v[...]


def spread(*args):
    def out(*shape, dtype=F32):
        return jax.ShapeDtypeStruct(shape, dtype)

    inside = pl.BlockSpec(memory_space=pltpu.VMEM)
    vec, square, wide = out(1, 128), out(128, D), out(128, 2816)
    return pl.pallas_call(
        spread_kernel,
        out_shape=(
            out(PIECE, D, dtype=BF16), out(PIECE, D), vec, square, square, square, vec, vec, vec,
            square, vec, wide, wide, out(2816, 128),
        ),
        in_specs=[pl.BlockSpec(memory_space=pl.ANY)] * 7,
        out_specs=[inside] * 14,
        scratch_shapes=[pltpu.VMEM(a.shape, a.dtype) for a in args] + [pltpu.SemaphoreType.DMA((7,))],
        compiler_params=pltpu.CompilerParams(vmem_limit_bytes=60 * 1024 * 1024),
        name="spread",
    )(*args)


def rotary_tables():
    exponent = np.arange(HEAD_DIM // 2, dtype=np.float32) * np.float32(2.0 / HEAD_DIM)
    inverse = np.exp(np.float32(-math.log(THETA)) * exponent)
    angles = np.arange(D, dtype=np.float32)[:, None] * inverse
    cos, sin = np.cos(angles), np.sin(angles)
    return np.concatenate([cos] * 4, axis=1), np.concatenate([-sin, sin] * 2, axis=1)


def per_device(
    inputs, doc_ids, positions, attn_gain, query_weight, key_weight, value_weight,
    query_bias, key_bias, value_bias, out_weight, mlp_gain, gate_weight, up_weight,
    down_weight, cotangent,
):
    del positions
    cos, sin = rotary_tables()
    vectors = [v.reshape(1, 128) for v in (attn_gain, mlp_gain, query_bias, key_bias, value_bias)]
    blocks = fused_layer(
        inputs.reshape(PIECE, D), cotangent.reshape(PIECE, D),
        query_weight, key_weight, value_weight, out_weight, gate_weight, up_weight, down_weight,
        jnp.asarray(cos), jnp.asarray(sin), *vectors, doc_ids,
    )
    outs = list(spread(*blocks))
    outs[0] = outs[0].reshape(inputs.shape)
    outs[1] = outs[1].reshape(inputs.shape)
    return tuple(o.reshape(128) if o.shape == (1, 128) else o for o in outs)


def solution(mesh):
    rows_spec = P("fsdp", None)
    act = P("seq", "fsdp", None)
    vec = P("fsdp")
    return jax.shard_map(
        per_device,
        mesh=mesh,
        in_specs=(
            act, P(), P("seq", "fsdp"), vec, rows_spec, rows_spec, rows_spec, vec, vec, vec,
            rows_spec, vec, rows_spec, rows_spec, P(None, "fsdp"), act,
        ),
        out_specs=(
            act, act, vec, rows_spec, rows_spec, rows_spec, vec, vec, vec, rows_spec, vec,
            rows_spec, rows_spec, P(None, "fsdp"),
        ),
        check_vma=False,
    )
```

time: 239 us -> 159 us (0.67); the launches traced: 235 us -> 159 us
  Pallas kernels: 204 us -> 158 us
  other arithmetic: 15.9 us -> 0 us
  local copies, waits for them, and re-layouts: 14.5 us -> 0 us
    pallas_call x1 -> x2, Pallas kernels: 204 us -> 158 us  [the longest x1 153 us: fused_layer(): pl.pallas_call(layer_kernel, out_shape=(out(PIECE, D), out(PIECE, D), out...]
    convert_element_type x8 -> x0, local copies, waits for them, and re-layouts: 5.76 us -> none  [the longest x6 3.07 us: rowwise(): block.reshape(8, 2, 64, -1).transpose(1, 2, 0, 3).reshape(128, -1)]
    concatenate x4 -> x0, other arithmetic: 5.43 us -> none  [the longest x2 2.39 us: cut_windows(): jnp.concatenate([block[:, :6 * FB], block[:, 6 * FB:6 * FB + 256], block[...]
    unnamed x17 -> x0, local copies, waits for them, and re-layouts: 5.26 us -> none
where the time goes in v2:
time: 159 us
  Pallas kernels  158 us (99%)
    pallas_call x1, Pallas kernels, fused_layer(): pl.pallas_call(layer_kernel, out_shape=(out(PIECE, D), out(PIECE, D), out...  153 us
    pallas_call x1, Pallas kernels, spread(): pl.pallas_call(spread_kernel, out_shape=(out(PIECE, D, dtype=BF16), out(P...  5.33 us

profile of v2, /device:TPU:1, one launch (start us, length us, event | category | flops | bytes accessed | tf_op | source)
XLA Modules:
  0.0 158.8 jit_solution(1541466836551985892)
XLA Ops:
  0.7 152.6 %layer.1 = (bf16[128,1024]{1,0:T(8,128)(2,1)}, bf16[128,1024]{1,0:T(8,128)(2,1)}, bf16[8,2,4,16,768]{4,3,2,1,0:T(8,128)(2,1)}, bf16[8,2,4,48,128]{4,3,2,1,0:T(8,...) custom-call(bf16[128,1024]{1,0:T(8,128)(2,1)} %bitcast.14, ...), custom_call_target="tpu_custom_call" | custom-call | tf_op jit(solution)/shard_map/layer/pallas_call | solution.py:969
  153.3 5.3 %spread.1 = (bf16[128,1024]{1,0:T(8,128)(2,1)}, f32[128,1024]{1,0:T(8,128)}, f32[1,128]{1,0:T(1,128)}, f32[128,1024]{1,0:T(8,128)}, f32[128,1024]{1,0:T(8,128)},...) custom-call(bf16[128,1024]{1,0:T(8,128)(2,1)} %get-tuple-element.35., ...), custom_call_target="tpu_custom_call" | custom-call | tf_op jit(solution)/shard_map/spread/pallas_call | solution.py:1040

commit v3 on v2

--- a/solution.py
+++ b/solution.py
@@ -55,15 +55,15 @@
     cos_ref, sin_ref, start_ref, vec_in,
     x_own, cot_own, hidden, g_hidden, wo_all, wqkv, wgu, wdn, vall,
     normed_all, cot_all, mlp_all, branch_all,
-    q_h, k_h, v_h, k_t, v_t, p_t, mixed_t, mixed, mixed_own,
+    q_h, k_h, v_h, k_t, v_t, p_t, mixed_t, mixed, mixed_own, mixed_grad,
     g_act, active, active_t, g_gu, g_mixed, gk_acc, gv_acc, g_qkv,
     part, sib, far_s, far_r, fin_s, fin_r,
-    dga, dgb, ddn, dwo, dqkv, ra, rb, rd, ha, hb, hd, sa, sb, sd, rwo, rqkv, wo_send, sum_gu, sum_dn, sum_qkv,
+    dga, dgb, ddn, dqa, dqb, dwo, ra, rb, rd, rqa, rqb, rw, ha, hb, hd, hqa, hqb, hw, sa, sb, sd, sqa, sqb, sw, wo_send, sum_gu, sum_dn, sum_qkv,
     lo_send, ig_send,
     vs, vr, v2s, v2r, v3s, v3r,
-    sem_load, swap_s, swap_r, vec_s, vec_r, wy_s, wy_r, wz_s, wz_r, wx_s, wx_r, wp_s, wp_r, mx_s, mx_r, ag_s, ag_r,
+    sem_load, swap_s, swap_r, vec_s, vec_r, wy_s, wy_r, wz_s, wz_r, wx_s, wx_r, wp_s, wp_r, mx_s, mx_r, um_s, um_r, ag_s, ag_r,
     sib_ss, sib_rs, far_ss, far_rs, fin_ss, fin_rs,
-    pl_s, pl_r, f1_s, f1_r, f2_s, f2_r, ya_s, ya_r, rg_s, rg_r, gd_s, gd_r, gp_s, gp_r, v1_ss, v1_rs, v2_ss, v2_rs, v3_ss, v3_rs,
+    f1_s, f1_r, f2_s, f2_r, ya_s, ya_r, rg_s, rg_r, gd_s, gd_r, gp_s, gp_r, v1_ss, v1_rs, v2_ss, v2_rs, v3_ss, v3_rs,
 ):
     s = lax.axis_index("seq")
     f = lax.axis_index("fsdp")
@@ -119,8 +119,10 @@
     def greet(to):
         pl.semaphore_signal(barrier, inc=1, device_id=to, device_id_type=MESH)
 
-    def greet_plane(r, carry):
-        greet(dev(x + r // 4, y, z + r % 4, c))
+    def greet_near(r, carry):
+        greet(dev(x + r, y, z, c))
+        greet(dev(x, y, z + r, c))
+        greet(dev(x + 2, y, z + r, c))
         return carry
 
     def greet_fsdp(r, carry):
@@ -131,18 +133,18 @@
         greet(dev(x, y + r, z, 1 - c))
         return carry
 
-    lax.fori_loop(1, 16, greet_plane, 0)
+    lax.fori_loop(1, 4, greet_near, 0)
     lax.fori_loop(1, 8, greet_fsdp, 0)
     lax.fori_loop(0, 4, greet_cross, 0)
 
     @pl.when(moves == 1)
     def _():
         greet(partner)
-        pl.semaphore_wait(barrier, 27)
+        pl.semaphore_wait(barrier, 21)
 
     @pl.when(moves == 0)
     def _():
-        pl.semaphore_wait(barrier, 26)
+        pl.semaphore_wait(barrier, 20)
 
     def swap_start(src, dst, n):
         @pl.when(moves == 1)
@@ -271,7 +273,7 @@
         for n in range(1, 8):
             wo_pass(n, True).wait_recv()
 
-    for n in (0, 3, 1, 2):
+    for n in (0, 3, 2, 1):
         w_ystart(n)
     w_own(0)
 
@@ -282,10 +284,12 @@
         return buf.at[rows((((y_ + 4) % 4) * 2 + c_) * PIECE + h * 64, 64)]
 
     def ag(buf, k, n, recv=False):
-        if n == 0:
-            ref, to = (piece(buf, y - 1, c) if recv else piece(buf, y, c)), y_up
-        elif n == 1:
-            ref, to = (piece(buf, y + 1, c) if recv else piece(buf, y, c)), y_dn
+        if n in (0, 8):
+            h = 0 if n == 0 else 1
+            ref, to = (half(buf, y - 1, c, h) if recv else half(buf, y, c, h)), y_up
+        elif n in (1, 9):
+            h = 1 if n == 1 else 0
+            ref, to = (half(buf, y + 1, c, h) if recv else half(buf, y, c, h)), y_dn
         elif n == 2:
             ref, to = (piece(buf, y, 1 - c) if recv else piece(buf, y, c)), sibling
         elif n == 3:
@@ -301,15 +305,19 @@
         return remote(ref, ref, ag_s.at[k, n], ag_r.at[k, n], to)
 
     def ag_start(buf, k):
-        for n in range(3):
+        for n in (0, 1, 2, 8, 9):
             ag(buf, k, n).start()
 
     def ag_near(buf, k):
         ag(buf, k, 0, True).wait_recv()
         ag(buf, k, 3).start()
-        ag(buf, k, 4).start()
         ag(buf, k, 1, True).wait_recv()
         ag(buf, k, 5).start()
+
+    def ag_pass(buf, k):
+        ag(buf, k, 8, True).wait_recv()
+        ag(buf, k, 4).start()
+        ag(buf, k, 9, True).wait_recv()
         ag(buf, k, 6).start()
 
     def ag_far(buf, k):
@@ -317,7 +325,11 @@
         ag(buf, k, 5, True).wait_recv()
         ag(buf, k, 7).start()
 
-    def ag_run(buf, k, consume, after_far=None):
+    def ag_finish(buf, k):
+        for n in (2, 4, 6, 7):
+            ag(buf, k, n, True).wait_recv()
+
+    def ag_run(buf, k, consume, after_pass=None, after_far=None):
         def step(i, carry):
             @pl.when(i == 0)
             def _():
@@ -325,33 +337,42 @@
 
             @pl.when(i == 1)
             def _():
-                ag_near(buf, k)
+                ag_pass(buf, k)
+                if after_pass is not None:
+                    after_pass()
                 ag(buf, k, 4, True).wait_recv()
 
             @pl.when(i == 2)
             def _():
                 ag(buf, k, 6, True).wait_recv()
+                ag_far(buf, k)
 
             @pl.when(i == 3)
             def _():
-                ag_far(buf, k)
                 if after_far is not None:
                     after_far()
                 ag(buf, k, 7, True).wait_recv()
 
             consume((y + (3 * ((i * (i + 1)) // 2)) % 4) % 4)
+
+            @pl.when(i == 0)
+            def _():
+                if k > 0:
+                    ag_near(buf, k)
+
             return carry
 
         lax.fori_loop(0, 4, step, 0)
 
-    def other(i):
-        return part.at[i, rows((1 - c) * PIECE, PIECE)]
-
-    def own_part(i):
-        return part[i, rows(c * PIECE, PIECE), :].astype(F32)
-
-    def c_sib(k, i):
-        return remote(other(i), sib.at[k, i], sib_ss.at[k, i], sib_rs.at[k, i], sibling)
+    def held(k):
+        return part.at[1 if k == 2 else 0]
+
+    def own_part(k, a):
+        return held(k)[a, rows(c * PIECE, PIECE), :].astype(F32)
+
+    def c_sib(k, a):
+        src = held(k).at[a, rows((1 - c) * PIECE, PIECE)]
+        return remote(src, sib.at[k, a], sib_ss.at[k, a], sib_rs.at[k, a], sibling)
 
     def c_far(k, n):
         return remote(far_s.at[k, pl.ds(64 * n, 64)], far_r.at[k, n], far_ss.at[k, n], far_rs.at[k, n], y_up if n == 0 else y_dn)
@@ -360,39 +381,24 @@
         cut = pl.ds(64 * h, 64)
         return remote(fin_s.at[k, n, cut], fin_r.at[k, n, cut], fin_ss.at[k, n, h], fin_rs.at[k, n, h], y_up if n == 0 else y_dn)
 
+    def rs_put(k, a, value):
+        if k == 3:
+            c_sib(1, a).wait_send()
+        held(k)[a] = value.astype(BF16)
+        c_sib(k, a).start()
+
+    def rs_pair(k, a):
+        c_sib(k, a).wait_recv()
+        return own_part(k, a) + sib[k, a].astype(F32)
+
     def rs_far(k):
-        c_sib(k, 0).wait_recv()
-        far_s[k] = (own_part(0) + sib[k, 0].astype(F32)).astype(BF16)
+        far_s[k] = rs_pair(k, (y + 2) % 4).astype(BF16)
         c_far(k, 0).start()
         c_far(k, 1).start()
 
     def rs_near(k, n):
-        c_sib(k, 1 + n).wait_recv()
-        fin_s[k, n] = (own_part(1 + n) + sib[k, 1 + n].astype(F32)).astype(BF16)
+        fin_s[k, n] = rs_pair(k, (y + 1 + 2 * n) % 4).astype(BF16)
         c_fin(k, n, 1 - n).start()
-
-    def rs_start(k, produce, eager=True):
-        def step(i, carry):
-            if k > 1:
-                c_sib(k - 1, i).wait_send()
-            part[i] = produce((y + (2 - (i * (i + 1)) // 2 + 8) % 4) % 4).astype(BF16)
-            c_sib(k, i).start()
-            if eager:
-                @pl.when(i == 1)
-                def _():
-                    rs_far(k)
-
-                @pl.when(i == 2)
-                def _():
-                    rs_near(k, 0)
-
-                @pl.when(i == 3)
-                def _():
-                    rs_near(k, 1)
-
-            return carry
-
-        lax.fori_loop(0, 4, step, 0)
 
     def rs_mid(k):
         for n in (0, 1):
@@ -402,8 +408,7 @@
             c_fin(k, n, n).start()
 
     def rs_finish(k):
-        c_sib(k, 3).wait_recv()
-        total = own_part(3) + sib[k, 3].astype(F32)
+        total = rs_pair(k, y)
         for n in (0, 1):
             for h in (0, 1):
                 c_fin(k, n, h).wait_recv()
@@ -423,10 +428,11 @@
     swap_start(cot_in, cot_own, 1)
     w_zstart(3)
     w_own(3)
+    w_zstart(2)
+    w_own(2)
     w_zstart(1)
     w_own(1)
-    w_zstart(2)
-    w_own(2)
+    ag_near(normed_all, 0)
     for load in loads[7:]:
         load.wait()
     w_finish(0)
@@ -457,7 +463,7 @@
         cot_all[rows(j * PIECE, PIECE), :] = cot_own[...]
         ag_start(cot_all, 1)
 
-    ag_run(normed_all, 0, project, cot_start)
+    ag_run(normed_all, 0, project, lambda: w_xstart(3), cot_start)
 
     def attend(i):
         width = (i + 1) * BLOCK
@@ -498,15 +504,15 @@
         mix(m, j).wait_send()
         return carry
 
-    w_xstart(3)
+    w_xstart(2)
     attend(0)
-    w_xstart(2)
+    w_xstart(1)
+    ag_near(cot_all, 1)
     attend(1)
-    w_xstart(1)
     attend(2)
     wo_pass_x()
     attend(3)
-    ag_near(cot_all, 1)
+    ag_pass(cot_all, 1)
     wo_pass_finish()
     lax.fori_loop(1, 8, mix_wait, 0)
 
@@ -516,8 +522,7 @@
     ag_start(mlp_all, 2)
     ag_far(cot_all, 1)
     w_finish(2)
-    for n in (2, 4, 6, 7):
-        ag(cot_all, 1, n, True).wait_recv()
+    ag_finish(cot_all, 1)
 
     def active_back(i, carry):
         cut = rows(i * BLOCK, BLOCK)
@@ -542,65 +547,50 @@
         back = jnp.where(live, g_act[cut, :], 0.0)
         act = jnp.where(live, silu * up, 0.0)
         active[cut, :] = act.astype(BF16)
-        active_t[:, cut] = act.T.astype(BF16)
         g_gu[cut, :FB] = (back * up * sig * (1.0 + gate * (1.0 - sig))).astype(BF16)
         g_gu[cut, FB:] = (back * silu).astype(BF16)
+        rs_put(1, yy, nt(g_gu[cut, :], wgu[...]))
 
     ag_run(mlp_all, 2, feed)
-    rs_start(1, lambda yy: nt(g_gu[rows(yy * BLOCK, BLOCK), :], wgu[...]))
-
-    def plane(n, r):
-        x_, z_ = (x + r // 4) % 4, (z + r % 4) % 4
-        src = (dwo, dqkv)[n].at[x_ * 4 + z_]
-        dst = (rwo, rqkv)[n].at[r - 1]
-        return remote(src, dst, pl_s.at[n, r - 1], pl_r.at[n, r - 1], dev(x_, y, z_, c))
-
-    def plane_start(n):
-        def go(r, carry):
-            plane(n, r).start()
-            return carry
-
-        lax.fori_loop(1, 16, go, 0)
-
-    def plane_sum(n):
-        own, recv = ((dwo, rwo), (dqkv, rqkv))[n]
-
-        def go(r, total):
-            plane(n, r).wait()
-            return total + recv[r - 1].astype(F32)
-
-        return lax.fori_loop(1, 16, go, own[x * 4 + z].astype(F32))
+    rs_far(1)
+
+    terms = (dga, dgb, ddn, dqa, dqb, dwo)
+    term_in = (ra, rb, rd, rqa, rqb, rw)
+    halfway = (ha, hb, hd, hqa, hqb, hw)
+    half_in = (sa, sb, sd, sqa, sqb, sw)
 
     def first(n, r):
-        if n == 0:
-            src, to = dga.at[(x + r) % 4], dev(x + r, y, z, c)
+        if n in (0, 3, 5):
+            src, to = terms[n].at[(x + r) % 4], dev(x + r, y, z, c)
         else:
-            src, to = (dgb, ddn)[n - 1].at[:, (z + r) % 4], dev(x, y, z + r, c)
-        return remote(src, (ra, rb, rd)[n].at[r - 1], f1_s.at[n, r], f1_r.at[n, r], to)
+            src, to = terms[n].at[:, (z + r) % 4], dev(x, y, z + r, c)
+        return remote(src, term_in[n].at[r - 1], f1_s.at[n, r], f1_r.at[n, r], to)
 
     def second(n, r):
-        src = (ha, hb, hd)[n].at[((z if n == 0 else x) + r) % 4]
-        to = dev(x, y, z + r, c) if n == 0 else dev(x + r, y, z, c)
-        return remote(src, (sa, sb, sd)[n].at[r - 1], f2_s.at[n, r], f2_r.at[n, r], to)
+        if n in (0, 3, 5):
+            src, to = halfway[n].at[(z + r) % 4], dev(x, y, z + r, c)
+        else:
+            src, to = halfway[n].at[(x + r) % 4], dev(x + r, y, z, c)
+        return remote(src, half_in[n].at[r - 1], f2_s.at[n, r], f2_r.at[n, r], to)
 
     def first_start(n):
         for r in (1, 3, 2):
             first(n, r).start()
 
     def first_sum(n):
-        total = (dga[x] if n == 0 else (dgb, ddn)[n - 1][:, z]).astype(F32)
+        total = (terms[n][x] if n in (0, 3, 5) else terms[n][:, z]).astype(F32)
         for r in (1, 3, 2):
             first(n, r).wait()
-            total = total + (ra, rb, rd)[n][r - 1].astype(F32)
-        (ha, hb, hd)[n][...] = total.astype(BF16)
+            total = total + term_in[n][r - 1].astype(F32)
+        halfway[n][...] = total.astype(BF16)
         for r in (1, 3, 2):
             second(n, r).start()
 
     def second_sum(n):
-        total = (ha, hb, hd)[n][z if n == 0 else x].astype(F32)
+        total = halfway[n][z if n in (0, 3, 5) else x].astype(F32)
         for r in (1, 3, 2):
             second(n, r).wait()
-            total = total + (sa, sb, sd)[n][r - 1].astype(F32)
+            total = total + half_in[n][r - 1].astype(F32)
         return total.astype(BF16)
 
     def chunk(t, xl_):
@@ -629,21 +619,25 @@
         for xl_ in range(2):
             for t in range(8):
                 x_, z_ = chunk(t, xl_)
-                dqkv[x_ * 4 + z_, i] = got[xl_ * 128 + t * 16 : xl_ * 128 + t * 16 + 16]
+                share = got[xl_ * 128 + t * 16 : xl_ * 128 + t * 16 + 16]
+                dqa[x_, z_, i] = share[:, :256]
+                dqb[x_, z_, i] = share[:, 256:]
         return carry
 
     def grad_wo():
         got = tn(mixed[...], branch_all[...]).astype(BF16)
         for h in range(2):
             for t in range(8):
-                to = ((t % 2) * 2 + (h + c) % 2) * 4 + t // 2
-                dwo[pl.ds(to, 1)] = got[h * 64 : h * 64 + 64, t * 128 : t * 128 + 128][None]
-
-    lax.fori_loop(0, 2, grad_gu, 0)
-    rs_mid(1)
-    lax.fori_loop(2, 4, grad_gu, 0)
+                x_, z_ = chunk(t, (h + c) % 2)
+                dwo[pl.ds(x_, 1), z_] = got[h * 64 : h * 64 + 64, t * 128 : t * 128 + 128][None]
+
+    lax.fori_loop(0, 4, grad_gu, 0)
+    rs_near(1, 0)
+    rs_near(1, 1)
     first_start(1)
     first_start(0)
+    rs_mid(1)
+    active_t[...] = active[...].T
     lax.fori_loop(0, 4, grad_dn, 0)
     first_start(2)
 
@@ -655,18 +649,43 @@
     gain_two = jnp.sum(grad * hid * scale, axis=0, keepdims=True)
     g_hidden[...] = cot_own[...].astype(F32) + back
     branch_all[rows(j * PIECE, PIECE), :] = g_hidden[...].astype(BF16)
+
+    def unmix_term(i, carry):
+        cut = rows(i * BLOCK, BLOCK)
+        mixed_grad[:, cut] = nt(branch_all[rows(j * PIECE, PIECE), :], wo_all[cut, :]).astype(BF16)
+        return carry
+
+    lax.fori_loop(0, 4, unmix_term, 0)
+    g_mixed[rows(j * PIECE, PIECE), :] = mixed_grad[:, rows(j * 128, 128)]
+
+    def unmix(m, sender):
+        return remote(
+            mixed_grad.at[:, rows(m * 128, 128)], g_mixed.at[rows(sender * PIECE, PIECE), :],
+            um_s.at[m], um_r.at[sender], dev(x, m // 2, z, m % 2),
+        )
+
+    def unmix_start(r, carry):
+        unmix((j + r) % 8, j).start()
+        return carry
+
+    def unmix_wait(r, carry):
+        m = (j + r) % 8
+        unmix(m, m).wait_recv()
+        unmix(m, j).wait_send()
+        return carry
+
+    lax.fori_loop(1, 8, unmix_start, 0)
     ag_start(branch_all, 3)
-
-    def mixed_back(yy):
-        cut = rows(yy * BLOCK, BLOCK)
-        g_mixed[cut, :] = nt(branch_all[cut, :], wo_all[rows(j * 128, 128), :])
-
     gk_acc[...] = jnp.zeros_like(gk_acc)
     gv_acc[...] = jnp.zeros_like(gv_acc)
-    ag_run(branch_all, 3, mixed_back)
-    for n in (1, 0, 2):
-        first_sum(n)
-    rs_start(2, lambda yy: nn(active[rows(yy * BLOCK, BLOCK), :], wdn[...]), eager=False)
+
+    def output_term(i, carry):
+        rs_put(2, i, nn(active[rows(i * BLOCK, BLOCK), :], wdn[...]))
+        return carry
+
+    lax.fori_loop(0, 4, output_term, 0)
+    first_sum(0)
+    lax.fori_loop(1, 8, unmix_wait, 0)
 
     def along_y(n, r, recv=False):
         src = (sum_gu, sum_dn, sum_qkv)[n].at[(y + r) % 4]
@@ -681,7 +700,8 @@
         elif n == 1:
             total[...] = second_sum(2)
         else:
-            total[...] = plane_sum(1).astype(BF16)
+            total[:, :, :256] = second_sum(3)
+            total[:, :, 256:] = second_sum(4)
         for r in (1, 3, 2):
             along_y(n, r).start()
         every[place, c, y] = total[y]
@@ -771,8 +791,8 @@
     def attend_back(i):
         width = (i + 1) * BLOCK
         cut = slice(i * BLOCK, (i + 1) * BLOCK)
-        grad_t = g_mixed[cut, :].T
-        grad_bf = g_mixed[cut, :].astype(BF16)
+        grad_bf = g_mixed[cut, :]
+        grad_t = grad_bf.astype(F32).T
         products = grad_t * mixed_t[:, cut]
         queries_t = []
         for h in range(2):
@@ -788,43 +808,41 @@
         g_query = (jnp.concatenate(queries_t, axis=0) * 0.125).T
         g_qkv[cut, :128] = unturn(g_query, cut)
 
-    attend_back(0)
-    rs_far(2)
-    attend_back(1)
-    rs_near(2, 0)
-    rs_near(2, 1)
-    attend_back(2)
-    rs_mid(2)
+    def block_back(i):
+        cut = slice(i * BLOCK, (i + 1) * BLOCK)
+        attend_back(i)
+        g_qkv[cut, 128:256] = unturn(jnp.concatenate([gk_acc[0, cut, :], gk_acc[1, cut, :]], axis=1), cut)
+        g_qkv[cut, 256:] = jnp.concatenate([gv_acc[0, cut, :], gv_acc[1, cut, :]], axis=1).astype(BF16)
+        rs_put(3, i, nt(g_qkv[cut, :], wqkv[...]))
+
+    block_back(3)
+    ag_near(branch_all, 3)
+    first_sum(1)
+    first_sum(2)
+    block_back(2)
+    ag_pass(branch_all, 3)
+    block_back(1)
     share(0)
     share(1)
-    attend_back(3)
-    for i in range(4):
-        cut = slice(i * BLOCK, (i + 1) * BLOCK)
-        g_qkv[cut, 128:256] = unturn(jnp.concatenate([gk_acc[0, cut, :], gk_acc[1, cut, :]], axis=1), cut)
-        g_qkv[cut, 256:] = jnp.concatenate([gv_acc[0, cut, :], gv_acc[1, cut, :]], axis=1).astype(BF16)
-    lo_last = own_part(3)
-    rs_start(3, lambda yy: nt(g_qkv[rows(yy * BLOCK, BLOCK), :], wqkv[...]))
+    block_back(0)
+    rs_far(3)
     lax.fori_loop(0, 4, grad_qkv, 0)
-    plane_start(1)
+    rs_near(3, 0)
+    rs_near(3, 1)
+    first_start(3)
+    first_start(4)
+    ag_far(branch_all, 3)
     ring_one(0)
     ring_one(1)
     rs_mid(3)
+    rs_far(2)
+    ag_finish(branch_all, 3)
     grad_wo()
-    plane_start(0)
+    first_start(5)
+    first_sum(3)
+    first_sum(4)
     ring_two(0)
     ring_two(1)
-
-    c_sib(2, 3).wait_recv()
-    for n in (0, 1):
-        for h in (0, 1):
-            c_fin(2, n, h).wait_recv()
-    lo_send[...] = (
-        hidden[...] + lo_last + sib[2, 3].astype(F32) + fin_r[2, 0].astype(F32) + fin_r[2, 1].astype(F32)
-    ).astype(BF16)
-    swap_start(lo_send, layer_out, 2)
-
-    ring_three(0)
-    ring_three(1)
 
     grad = rs_finish(3)
     scale = rms_scale(x32)
@@ -854,9 +872,10 @@
         return carry
 
     lax.fori_loop(1, 8, v1_start, 0)
+    rs_near(2, 0)
+    rs_near(2, 1)
+    first_sum(5)
     share(2)
-    wo_send[...] = plane_sum(0).astype(BF16)
-    swap_start(wo_send, all_wo.at[place, (c + moves) % 2], 4)
     lax.fori_loop(1, 8, v1_wait, 0)
     v2s[...] = jnp.sum(vr[...], axis=0) + vs[pl.ds(f, 1)][0]
 
@@ -874,16 +893,23 @@
 
     lax.fori_loop(1, 8, v2_start, 0)
     spread_start(3)
+    wo_send[...] = second_sum(5)
+    swap_start(wo_send, all_wo.at[place, (c + moves) % 2], 4)
+    rs_mid(2)
+    ring_three(0)
+    ring_three(1)
     swap_wait(wo_send, all_wo.at[place, c], 4)
     spread_start(2)
     lax.fori_loop(1, 8, v2_wait, 0)
     v3s[...] = jnp.sum(v2r[...], axis=0) + v2s[...]
     v3_copy = remote(v3s, v3r, v3_ss.at[0], v3_rs.at[0], sibling)
     v3_copy.start()
+    lo_send[...] = (hidden[...] + rs_finish(2)).astype(BF16)
+    swap_start(lo_send, layer_out, 2)
+    spread_pass(3)
     ring_four(0)
     ring_four(1)
-    for n in (3, 2):
-        spread_pass(n)
+    spread_pass(2)
     v3_copy.wait()
     vec_out[...] = v3s[...] + v3r[...]
     swap_wait(lo_send, layer_out, 2)
@@ -904,10 +930,10 @@
     for n in range(1, 8):
         wo_pass(n).wait_send()
     for k, buf in enumerate((normed_all, cot_all, mlp_all, branch_all)):
-        for n in range(8):
+        for n in range(10):
             ag(buf, k, n).wait_send()
     for k in range(1, 4):
-        if k == 3:
+        if k > 1:
             for i in range(4):
                 c_sib(k, i).wait_send()
         for n in (0, 1):
@@ -935,29 +961,29 @@
         return pltpu.SemaphoreType.DMA(shape)
 
     full = vmem(D, D)
+    shares = ((4, 16, 512), (4, 16, 256), (4, 48, 128), (4, 16, 256), (4, 16, 128), (64, 128))
     scratch = [
         vmem(D, 128, dtype=F32), vmem(D, 128, dtype=F32), vmem(1, D, dtype=jnp.int32), vmem(8, 128, dtype=F32),
         vmem(PIECE, D), vmem(PIECE, D), vmem(PIECE, D, dtype=F32), vmem(PIECE, D, dtype=F32),
         full, vmem(D, FB), vmem(D, 2 * FB), vmem(FB, D), vmem(8, 8, 128, dtype=F32),
         full, full, full, full,
         vmem(2, D, 64), vmem(2, D, 64), vmem(2, D, 64), vmem(128, D), vmem(128, D),
-        vmem(2, 4, D, BLOCK), vmem(128, D, dtype=F32), vmem(D, 128), vmem(PIECE, D),
-        vmem(D, FB, dtype=F32), vmem(D, FB), vmem(FB, D), vmem(D, 2 * FB), vmem(D, 128, dtype=F32),
+        vmem(2, 4, D, BLOCK), vmem(128, D, dtype=F32), vmem(D, 128), vmem(PIECE, D), vmem(PIECE, D),
+        vmem(D, FB, dtype=F32), vmem(D, FB), vmem(FB, D), vmem(D, 2 * FB), vmem(D, 128),
         vmem(2, D, 64, dtype=F32), vmem(2, D, 64, dtype=F32), vmem(D, FB),
-        vmem(4, BLOCK, D), vmem(4, 4, PIECE, D), vmem(4, PIECE, D), vmem(4, 2, 64, D), vmem(4, 2, PIECE, D), vmem(4, 2, PIECE, D),
-        vmem(4, 4, 4, 16, 512), vmem(4, 4, 4, 16, 256), vmem(4, 4, 4, 48, 128), vmem(16, 64, 128), vmem(16, 4, 16, FB),
-        vmem(3, 4, 4, 16, 512), vmem(3, 4, 4, 16, 256), vmem(3, 4, 4, 48, 128),
-        vmem(4, 4, 16, 512), vmem(4, 4, 16, 256), vmem(4, 4, 48, 128),
-        vmem(3, 4, 16, 512), vmem(3, 4, 16, 256), vmem(3, 4, 48, 128),
-        vmem(15, 64, 128), vmem(15, 4, 16, FB),
+        vmem(2, 4, BLOCK, D), vmem(4, 4, PIECE, D), vmem(4, PIECE, D), vmem(4, 2, 64, D), vmem(4, 2, PIECE, D), vmem(4, 2, PIECE, D),
+        *(vmem(4, 4, *dims) for dims in shares),
+        *(vmem(3, 4, *dims) for dims in shares),
+        *(vmem(4, *dims) for dims in shares),
+        *(vmem(3, *dims) for dims in shares),
         vmem(64, 128), vmem(4, 16, 2 * FB), vmem(4, 48, 128), vmem(4, 16, FB),
         vmem(PIECE, D), vmem(PIECE, D),
         vmem(8, 8, 128, dtype=F32), vmem(7, 8, 128, dtype=F32), vmem(8, 128, dtype=F32), vmem(7, 8, 128, dtype=F32),
         vmem(8, 128, dtype=F32), vmem(8, 128, dtype=F32),
         dma(9), dma(5), dma(5), dma(8), dma(8), dma(4, 3, 4), dma(4, 3, 4), dma(4, 4, 4), dma(4, 4, 4), dma(4, 4), dma(4, 4),
-        dma(8), dma(8), dma(8), dma(8), dma(4, 8), dma(4, 8),
+        dma(8), dma(8), dma(8), dma(8), dma(8), dma(8), dma(4, 10), dma(4, 10),
         dma(4, 4), dma(4, 4), dma(4, 2), dma(4, 2), dma(4, 2, 2), dma(4, 2, 2),
-        dma(2, 15), dma(2, 15), dma(3, 4), dma(3, 4), dma(3, 4), dma(3, 4), dma(3, 4), dma(3, 4), dma(2, 9), dma(2, 9), dma(4, 8), dma(4, 8), dma(4, 8), dma(4, 8),
+        dma(6, 4), dma(6, 4), dma(6, 4), dma(6, 4), dma(3, 4), dma(3, 4), dma(2, 9), dma(2, 9), dma(4, 8), dma(4, 8), dma(4, 8), dma(4, 8),
         dma(7), dma(7), dma(7), dma(7), dma(1), dma(1),
     ]
     anywhere = pl.BlockSpec(memory_space=pl.ANY)

time: 159 us -> 138 us (0.87)
  Pallas kernels: 158 us -> 137 us
    pallas_call x1, Pallas kernels: 153 us -> 132 us  [fused_layer(): pl.pallas_call(layer_kernel, out_shape=(out(PIECE, D), out(PIECE, D), out...]
where the time goes in v3:
time: 138 us
  Pallas kernels  137 us (99%)
    pallas_call x1, Pallas kernels, fused_layer(): pl.pallas_call(layer_kernel, out_shape=(out(PIECE, D), out(PIECE, D), out...  132 us
    pallas_call x1, Pallas kernels, spread(): pl.pallas_call(spread_kernel, out_shape=(out(PIECE, D, dtype=BF16), out(P...  5.33 us

profile of v3, /device:TPU:1, one launch (start us, length us, event | category | flops | bytes accessed | tf_op | source)
XLA Modules:
  0.0 137.8 jit_solution(4127751300762231811)
XLA Ops:
  0.7 131.6 %layer.1 = (bf16[128,1024]{1,0:T(8,128)(2,1)}, bf16[128,1024]{1,0:T(8,128)(2,1)}, bf16[8,2,4,16,768]{4,3,2,1,0:T(8,128)(2,1)}, bf16[8,2,4,48,128]{4,3,2,1,0:T(8,...) custom-call(bf16[128,1024]{1,0:T(8,128)(2,1)} %bitcast.14, ...), custom_call_target="tpu_custom_call" | custom-call | tf_op jit(solution)/shard_map/layer/pallas_call | solution.py:995
  132.3 5.3 %spread.1 = (bf16[128,1024]{1,0:T(8,128)(2,1)}, f32[128,1024]{1,0:T(8,128)}, f32[1,128]{1,0:T(1,128)}, f32[128,1024]{1,0:T(8,128)}, f32[128,1024]{1,0:T(8,128)},...) custom-call(bf16[128,1024]{1,0:T(8,128)(2,1)} %get-tuple-element.35., ...), custom_call_target="tpu_custom_call" | custom-call | tf_op jit(solution)/shard_map/spread/pallas_call | solution.py:1066

commit v4 on v3

--- a/solution.py
+++ b/solution.py
@@ -506,9 +506,9 @@
 
     w_xstart(2)
     attend(0)
+    attend(1)
     w_xstart(1)
     ag_near(cot_all, 1)
-    attend(1)
     attend(2)
     wo_pass_x()
     attend(3)
@@ -646,7 +646,6 @@
     scale = rms_scale(hid)
     scaled = grad * gathered(1)
     back = scale * scaled - hid * (scale * scale * scale) * jnp.mean(scaled * hid, axis=-1, keepdims=True)
-    gain_two = jnp.sum(grad * hid * scale, axis=0, keepdims=True)
     g_hidden[...] = cot_own[...].astype(F32) + back
     branch_all[rows(j * PIECE, PIECE), :] = g_hidden[...].astype(BF16)
 
@@ -675,7 +674,7 @@
         return carry
 
     lax.fori_loop(1, 8, unmix_start, 0)
-    ag_start(branch_all, 3)
+    gain_two = jnp.sum(grad * hid * scale, axis=0, keepdims=True)
     gk_acc[...] = jnp.zeros_like(gk_acc)
     gv_acc[...] = jnp.zeros_like(gv_acc)
 
@@ -684,8 +683,10 @@
         return carry
 
     lax.fori_loop(0, 4, output_term, 0)
+    first_sum(1)
     first_sum(0)
     lax.fori_loop(1, 8, unmix_wait, 0)
+    ag_start(branch_all, 3)
 
     def along_y(n, r, recv=False):
         src = (sum_gu, sum_dn, sum_qkv)[n].at[(y + r) % 4]
@@ -712,8 +713,8 @@
         return arrays[n].at[((z + 4 - r % 4) % 4) * 2 + (xh + r // 4) % 2, c_]
 
     def gd(n, r, recv=False):
-        ref = spot(n, r if recv else 0, c)
-        return remote(ref, ref, gd_s.at[n, r], gd_r.at[n, r], dev(x + 2 * (r // 4), y, z + r % 4, c))
+        ref = spot(n, r if recv else 4 * (r // 5), c)
+        return remote(ref, ref, gd_s.at[n, r], gd_r.at[n, r], dev(x + 2 * (r == 4), y, z + r % 4, c))
 
     def gp(n, r, recv=False):
         ref = spot(n, r, (1 - c) if recv else c)
@@ -771,12 +772,18 @@
         if n != 2:
             for r in (1, 3, 2):
                 along_y(min(n, 2), r, True).wait_recv()
-        for r in (2, 1, 3, 6, 5, 7, 4):
+        for r in (4, 2, 1, 3):
             gd(n, r).start()
         gp(n, 0).start()
 
+    def spread_next(n):
+        gd(n, 4, True).wait_recv()
+        for r in (6, 5, 7):
+            gd(n, r).start()
+        gp(n, 4).start()
+
     def spread_pass(n):
-        for r in (1, 3, 2, 4, 5, 7, 6):
+        for r in (1, 3, 2, 5, 7, 6):
             gd(n, r, True).wait_recv()
             gp(n, r).start()
 
@@ -816,42 +823,45 @@
         rs_put(3, i, nt(g_qkv[cut, :], wqkv[...]))
 
     block_back(3)
+    block_back(2)
+    share(0)
+    first_sum(2)
     ag_near(branch_all, 3)
-    first_sum(1)
-    first_sum(2)
-    block_back(2)
-    ag_pass(branch_all, 3)
     block_back(1)
-    share(0)
-    share(1)
     block_back(0)
     rs_far(3)
+    ag_pass(branch_all, 3)
+    ring_one(0)
+    share(1)
     lax.fori_loop(0, 4, grad_qkv, 0)
+    first_start(4)
+    first_start(3)
     rs_near(3, 0)
     rs_near(3, 1)
-    first_start(3)
-    first_start(4)
+    ring_two(0)
+    ring_one(1)
     ag_far(branch_all, 3)
-    ring_one(0)
-    ring_one(1)
     rs_mid(3)
     rs_far(2)
     ag_finish(branch_all, 3)
     grad_wo()
     first_start(5)
+    rs_near(2, 0)
+    rs_near(2, 1)
     first_sum(3)
     first_sum(4)
-    ring_two(0)
     ring_two(1)
 
     grad = rs_finish(3)
     scale = rms_scale(x32)
     scaled = grad * gathered(0)
     back = scale * scaled - x32 * (scale * scale * scale) * jnp.mean(scaled * x32, axis=-1, keepdims=True)
-    gain_one = jnp.sum(grad * x32 * scale, axis=0, keepdims=True)
     ig_send[...] = (g_hidden[...] + back).astype(BF16)
     swap_start(ig_send, in_grad, 3)
-
+    share(2)
+    first_sum(5)
+
+    gain_one = jnp.sum(grad * x32 * scale, axis=0, keepdims=True)
     vs[...] = jnp.zeros_like(vs)
     for i in range(8):
         vs[i, 0:1, :] = gain_one[:, 128 * i : 128 * i + 128]
@@ -872,10 +882,11 @@
         return carry
 
     lax.fori_loop(1, 8, v1_start, 0)
-    rs_near(2, 0)
-    rs_near(2, 1)
-    first_sum(5)
-    share(2)
+    ring_three(0)
+    spread_start(3)
+    rs_mid(2)
+    wo_send[...] = second_sum(5)
+    swap_start(wo_send, all_wo.at[place, (c + moves) % 2], 4)
     lax.fori_loop(1, 8, v1_wait, 0)
     v2s[...] = jnp.sum(vr[...], axis=0) + vs[pl.ds(f, 1)][0]
 
@@ -892,20 +903,17 @@
         return carry
 
     lax.fori_loop(1, 8, v2_start, 0)
-    spread_start(3)
-    wo_send[...] = second_sum(5)
-    swap_start(wo_send, all_wo.at[place, (c + moves) % 2], 4)
-    rs_mid(2)
-    ring_three(0)
-    ring_three(1)
+    spread_next(3)
     swap_wait(wo_send, all_wo.at[place, c], 4)
     spread_start(2)
+    ring_three(1)
+    lo_send[...] = (hidden[...] + rs_finish(2)).astype(BF16)
+    swap_start(lo_send, layer_out, 2)
+    spread_next(2)
     lax.fori_loop(1, 8, v2_wait, 0)
     v3s[...] = jnp.sum(v2r[...], axis=0) + v2s[...]
     v3_copy = remote(v3s, v3r, v3_ss.at[0], v3_rs.at[0], sibling)
     v3_copy.start()
-    lo_send[...] = (hidden[...] + rs_finish(2)).astype(BF16)
-    swap_start(lo_send, layer_out, 2)
     spread_pass(3)
     ring_four(0)
     ring_four(1)
@@ -990,7 +998,7 @@
     inside = pl.BlockSpec(memory_space=pltpu.VMEM)
 
     def out(*shape, dtype=BF16):
-        return jax.ShapeDtypeStruct(shape, dtype)
+        return pltpu.VMEM(shape, dtype)
 
     return pl.pallas_call(
         layer_kernel,
@@ -1002,59 +1010,64 @@
         out_specs=[inside] * 7,
         scratch_shapes=scratch,
         compiler_params=pltpu.CompilerParams(
-            collective_id=0, has_side_effects=True, vmem_limit_bytes=63 * 1024 * 1024
+            collective_id=0, has_side_effects=True, vmem_limit_bytes=57 * 1024 * 1024
         ),
         name="layer",
     )(*args)
 
 
 def spread_kernel(
-    lo_in, ig_in, gu_in, dn_in, wo_in, qkv_in, vec_in,
+    lo_in, ig_in, gu, dn, wo, qkv, vec,
     lo, ig, d_gain_a, d_q, d_k, d_v, d_bq, d_bk, d_bv, d_o, d_gain_m, d_gate, d_up, d_down,
-    lo_v, ig_v, gu, dn, wo, qkv, vec, sems,
+    ig_v, q_v, k_v, v_v, o_v, gate_v, up_v, down_v, sems,
 ):
-    loads = [
-        pltpu.make_async_copy(src, dst, sems.at[i])
-        for i, (src, dst) in enumerate(
-            ((vec_in, vec), (qkv_in, qkv), (wo_in, wo), (gu_in, gu), (dn_in, dn), (ig_in, ig_v), (lo_in, lo_v))
-        )
-    ]
-    for load in loads:
-        load.start()
-    loads[0].wait()
+    stores = []
+
+    def store(src, dst):
+        copy = pltpu.make_async_copy(src, dst, sems.at[len(stores)])
+        copy.start()
+        stores.append(copy)
+
     for ref, row in ((d_gain_a, 0), (d_gain_m, 1), (d_bq, 2), (d_bk, 3), (d_bv, 4)):
         ref[...] = vec[row : row + 1, :]
-    loads[1].wait()
-    for t in range(8):
-        cut = slice(16 * t, 16 * t + 16)
-        for m in range(8):
-            for i, ref in enumerate((d_q, d_k, d_v)):
-                ref[cut, 128 * m : 128 * m + 128] = qkv[t, m % 2, m // 2, :, 128 * i : 128 * i + 128].astype(F32)
-    loads[2].wait()
-    flip = lax.axis_index("fsdp") % 2
-    for t in range(8):
-        for core in range(2):
-            to = pl.ds(pl.multiple_of(64 * ((core + flip) % 2), 64), 64)
-            d_o[to, 128 * t : 128 * t + 128] = wo[t, core].astype(F32)
-    loads[3].wait()
-    loads[4].wait()
+    store(lo_in, lo)
     for m in range(8):
         first = 128 if m == 7 else 0
         count = 256 if m >= 6 else FB
         start = min(m, 6) * FB + (256 if m == 7 else 0)
         for t in range(8):
-            cut = slice(16 * t, 16 * t + 16)
-            d_gate[cut, start : start + count] = gu[t, m % 2, m // 2, :, first : first + count].astype(F32)
-            d_up[cut, start : start + count] = gu[t, m % 2, m // 2, :, FB + first : FB + first + count].astype(F32)
             low, high = max(48 * t, first), min(48 * t + 48, first + count)
             if low < high:
-                d_down[start + low - first : start + high - first, :] = dn[
+                down_v[start + low - first : start + high - first, :] = dn[
                     t, m % 2, m // 2, low - 48 * t : high - 48 * t, :
                 ].astype(F32)
-    loads[5].wait()
-    ig[...] = ig_v[...].astype(F32)
-    loads[6].wait()
-    lo[...] = lo_v[...]
+    store(down_v, d_down)
+    for ref, off, dst in ((gate_v, 0, d_gate), (up_v, FB, d_up)):
+        for m in range(8):
+            first = 128 if m == 7 else 0
+            count = 256 if m >= 6 else FB
+            start = min(m, 6) * FB + (256 if m == 7 else 0)
+            for t in range(8):
+                cut = slice(16 * t, 16 * t + 16)
+                ref[cut, start : start + count] = gu[t, m % 2, m // 2, :, off + first : off + first + count].astype(F32)
+        store(ref, dst)
+    for i, (ref, dst) in enumerate(((q_v, d_q), (k_v, d_k), (v_v, d_v))):
+        for t in range(8):
+            for m in range(8):
+                ref[16 * t : 16 * t + 16, 128 * m : 128 * m + 128] = qkv[
+                    t, m % 2, m // 2, :, 128 * i : 128 * i + 128
+                ].astype(F32)
+        store(ref, dst)
+    flip = lax.axis_index("fsdp") % 2
+    for t in range(8):
+        for core in range(2):
+            to = pl.ds(pl.multiple_of(64 * ((core + flip) % 2), 64), 64)
+            o_v[to, 128 * t : 128 * t + 128] = wo[t, core].astype(F32)
+    store(o_v, d_o)
+    ig_v[...] = ig_in[...].astype(F32)
+    store(ig_v, ig)
+    for copy in stores:
+        copy.wait()
 
 
 def spread(*args):
@@ -1062,17 +1075,20 @@
         return jax.ShapeDtypeStruct(shape, dtype)
 
     inside = pl.BlockSpec(memory_space=pltpu.VMEM)
-    vec, square, wide = out(1, 128), out(128, D), out(128, 2816)
+    anywhere = pl.BlockSpec(memory_space=pl.ANY)
+    vec, square, wide, tall = out(1, 128), out(128, D), out(128, 2816), out(2816, 128)
     return pl.pallas_call(
         spread_kernel,
         out_shape=(
             out(PIECE, D, dtype=BF16), out(PIECE, D), vec, square, square, square, vec, vec, vec,
-            square, vec, wide, wide, out(2816, 128),
+            square, vec, wide, wide, tall,
         ),
-        in_specs=[pl.BlockSpec(memory_space=pl.ANY)] * 7,
-        out_specs=[inside] * 14,
-        scratch_shapes=[pltpu.VMEM(a.shape, a.dtype) for a in args] + [pltpu.SemaphoreType.DMA((7,))],
-        compiler_params=pltpu.CompilerParams(vmem_limit_bytes=60 * 1024 * 1024),
+        in_specs=[inside] * 7,
+        out_specs=[anywhere, anywhere, inside, anywhere, anywhere, anywhere, inside, inside, inside]
+        + [anywhere, inside, anywhere, anywhere, anywhere],
+        scratch_shapes=[pltpu.VMEM(o.shape, o.dtype) for o in (square,) * 5 + (wide, wide, tall)]
+        + [pltpu.SemaphoreType.DMA((9,))],
+        compiler_params=pltpu.CompilerParams(vmem_limit_bytes=24 * 1024 * 1024),
         name="spread",
     )(*args)
 

time: 138 us -> 128 us (0.928)
  Pallas kernels: 137 us -> 127 us
    pallas_call x1, Pallas kernels: 132 us -> 124 us  [fused_layer(): pl.pallas_call(layer_kernel, out_shape=(out(PIECE, D), out(PIECE, D), out...]
    pallas_call x1, Pallas kernels: 5.33 us -> 3.56 us  [spread(): pl.pallas_call(spread_kernel, out_shape=(out(PIECE, D, dtype=BF16), out(P...]
where the time goes in v4:
time: 128 us
  Pallas kernels  127 us (99%)
    pallas_call x1, Pallas kernels, fused_layer(): pl.pallas_call(layer_kernel, out_shape=(out(PIECE, D), out(PIECE, D), out...  124 us
    pallas_call x1, Pallas kernels, spread(): pl.pallas_call(spread_kernel, out_shape=(out(PIECE, D, dtype=BF16), out(P...  3.56 us

profile of v4, /device:TPU:1, one launch (start us, length us, event | category | flops | bytes accessed | tf_op | source)
XLA Modules:
  0.0 128.3 jit_solution(6641850334224387260)
XLA Ops:
  0.7 123.9 %layer.1 = (bf16[128,1024]{1,0:T(8,128)(2,1)S(1)}, bf16[128,1024]{1,0:T(8,128)(2,1)S(1)}, bf16[8,2,4,16,768]{4,3,2,1,0:T(8,128)(2,1)S(1)}, bf16[8,2,4,48,128]{4,...) custom-call(bf16[128,1024]{1,0:T(8,128)(2,1)} %bitcast.14, ...), custom_call_target="tpu_custom_call" | custom-call | tf_op jit(solution)/shard_map/layer/pallas_call | solution.py:1003
  124.6 3.6 %spread.1 = (bf16[128,1024]{1,0:T(8,128)(2,1)}, f32[128,1024]{1,0:T(8,128)}, f32[1,128]{1,0:T(1,128)}, f32[128,1024]{1,0:T(8,128)}, f32[128,1024]{1,0:T(8,128)},...) custom-call(bf16[128,1024]{1,0:T(8,128)(2,1)S(1)} %get-tuple-element, ...), custom_call_target="tpu_custom_call" | custom-call | tf_op jit(solution)/shard_map/spread/pallas_call | solution.py:1080

commit v5 on v4

--- a/solution.py
+++ b/solution.py
@@ -13,6 +13,8 @@
 EPS = 1e-06
 THETA = 1000000.0
 NEG = -1000000000.0
+OTHER_DOC = -(2.0**30)
+LOG2_E = math.log2(math.e)
 D = 1024
 PIECE = 128
 BLOCK = 256
@@ -52,10 +54,10 @@
     x_in, cot_in, wq_in, wk_in, wv_in, wo_in, wg_in, wu_in, wd_in, cos_in, sin_in,
     gain_a, gain_m, bias_q, bias_k, bias_v, docs,
     layer_out, in_grad, all_gu, all_dn, all_wo, all_qkv, vec_out,
-    cos_ref, sin_ref, start_ref, vec_in,
+    cos_ref, sin_ref, vec_in,
     x_own, cot_own, hidden, g_hidden, wo_all, wqkv, wgu, wdn, vall,
     normed_all, cot_all, mlp_all, branch_all,
-    q_h, k_h, v_h, k_t, v_t, p_t, mixed_t, mixed, mixed_own, mixed_grad,
+    q_two, k_all, v_all, k_t, v_t, p_t, inv, mixed_t, mixed, mixed_own, mixed_grad,
     g_act, active, active_t, g_gu, g_mixed, gk_acc, gv_acc, g_qkv,
     part, sib, far_s, far_r, fin_s, fin_r,
     dga, dgb, ddn, dqa, dqb, dwo, ra, rb, rd, rqa, rqb, rw, ha, hb, hd, hqa, hqb, hw, sa, sb, sd, sqa, sqb, sw, wo_send, sum_gu, sum_dn, sum_qkv,
@@ -182,7 +184,6 @@
     swap_start(x_in, x_own, 0)
     vall[pl.ds(f, 1)] = vec_in[...][None]
     doc_row = docs[pl.ds(xh * 8 + z * 2 + xl, 1), :]
-    start_ref[...] = jnp.where(doc_row == 1, jnp.sum(1 - doc_row, axis=1, keepdims=True), 0)
 
     PARTS = (3, 2, 1, 1)
 
@@ -437,6 +438,23 @@
         load.wait()
     w_finish(0)
 
+    doc = jnp.broadcast_to(doc_row, (8, D)).astype(F32).T[:, :1]
+    feature = lax.broadcasted_iota(jnp.int32, (D, 128), 1)
+    k_all[:, 128:] = jnp.where(
+        feature == 0, OTHER_DOC * (1.0 - doc), jnp.where(feature == 1, OTHER_DOC * doc, 0.0)
+    ).astype(BF16)
+    q_more = jnp.where(feature == 0, doc, jnp.where(feature == 1, 1.0 - doc, 0.0)).astype(BF16)
+    for i in range(4):
+        for h in range(2):
+            q_two[i, BLOCK * h : BLOCK * h + BLOCK, 128:] = q_more[BLOCK * i : BLOCK * i + BLOCK]
+
+    def two_heads(value):
+        first_head = lax.broadcasted_iota(jnp.int32, value.shape, 1) < HEAD_DIM
+        return jnp.concatenate([jnp.where(first_head, value, 0.0), jnp.where(first_head, 0.0, value)], axis=0)
+
+    def own_quarters(value):
+        return jnp.concatenate([value[:HEAD_DIM, :BLOCK], value[HEAD_DIM:, BLOCK:]], axis=0)
+
     def project(yy):
         cut = rows(yy * BLOCK, BLOCK)
         lin = nn(normed_all[cut, :], wqkv[...])
@@ -446,15 +464,11 @@
         q_lin = lin[:, :128] + bias[2:3, :]
         k_lin = lin[:, 128:256] + bias[3:4, :]
         v_lin = lin[:, 256:] + bias[4:5, :]
-        q = (q_lin * cos + half_turn(q_lin) * sin).astype(BF16) * 0.125
+        q = (q_lin * cos + half_turn(q_lin) * sin) * (0.125 * LOG2_E)
         k32 = k_lin * cos + half_turn(k_lin) * sin
-        k = k32.astype(BF16)
-        v = v_lin.astype(BF16)
-        for h in range(2):
-            lanes = slice(64 * h, 64 * h + 64)
-            q_h[h, cut, :] = q[:, lanes]
-            k_h[h, cut, :] = k[:, lanes]
-            v_h[h, cut, :] = v[:, lanes]
+        q_two[pl.ds(yy, 1), :, :128] = two_heads(q).astype(BF16)[None]
+        k_all[cut, :128] = k32.astype(BF16)
+        v_all[cut, :] = v_lin.astype(BF16)
         k_t[:, cut] = k32.T.astype(BF16)
         v_t[:, cut] = v_lin.T.astype(BF16)
 
@@ -467,18 +481,26 @@
 
     def attend(i):
         width = (i + 1) * BLOCK
-        cut = slice(i * BLOCK, (i + 1) * BLOCK)
-        key_at = lax.broadcasted_iota(jnp.int32, (width, BLOCK), 0)
-        query_at = lax.broadcasted_iota(jnp.int32, (width, BLOCK), 1) + i * BLOCK
-        allowed = (key_at >= start_ref[0:1, cut]) & (key_at <= query_at)
-        for h in range(2):
-            scores = nt(k_h[h, :width, :], q_h[h, cut, :])
-            scores = jnp.where(allowed, scores, NEG)
-            weights = jnp.exp(scores - jnp.max(scores, axis=0, keepdims=True))
-            inverse = 1.0 / jnp.sum(weights, axis=0, keepdims=True)
-            probs = (weights * inverse).astype(BF16)
-            p_t[h, i, :width, :] = probs
-            mixed_t[64 * h : 64 * h + 64, cut] = nn(v_t[64 * h : 64 * h + 64, :width], probs)
+        before = i * BLOCK
+        cut = slice(before, width)
+        scores = nt(k_all[:width, :], q_two[i])
+        key_at = lax.broadcasted_iota(jnp.int32, (BLOCK, 2 * BLOCK), 0)
+        query_at = lax.broadcasted_iota(jnp.int32, (BLOCK, 2 * BLOCK), 1) % BLOCK
+        last = jnp.where(key_at <= query_at, scores[before:], NEG)
+        top = jnp.max(last, axis=0, keepdims=True)
+        if i > 0:
+            top = jnp.maximum(top, jnp.max(scores[:before], axis=0, keepdims=True))
+        weights = jnp.exp2(last - top)
+        total = jnp.sum(weights, axis=0, keepdims=True)
+        p_t[i, before:width, :] = weights.astype(BF16)
+        if i > 0:
+            weights = jnp.exp2(scores[:before] - top)
+            total = total + jnp.sum(weights, axis=0, keepdims=True)
+            p_t[i, :before, :] = weights.astype(BF16)
+        inverse = 1.0 / total
+        inv[i : i + 1, :] = inverse
+        both = nn(v_t[:, :width], p_t[i, :width, :]) * inverse
+        mixed_t[:, cut] = own_quarters(both)
         mixed[cut, :] = mixed_t[:, cut].T.astype(BF16)
         for m in (2 * i, 2 * i + 1):
             mix_start(m)
@@ -614,15 +636,16 @@
                 ddn[x_, z_, i] = got[t * 48 : t * 48 + 48, xl_ * 128 : xl_ * 128 + 128]
         return carry
 
-    def grad_qkv(i, carry):
-        got = tn(normed_all[:, rows(i * BLOCK, BLOCK)], g_qkv[...]).astype(BF16)
-        for xl_ in range(2):
-            for t in range(8):
-                x_, z_ = chunk(t, xl_)
-                share = got[xl_ * 128 + t * 16 : xl_ * 128 + t * 16 + 16]
-                dqa[x_, z_, i] = share[:, :256]
-                dqb[x_, z_, i] = share[:, 256:]
-        return carry
+    def grad_qkv(part_ref, base):
+        def go(i, carry):
+            got = tn(normed_all[:, rows((base + i) * BLOCK, BLOCK)], g_qkv[...]).astype(BF16)
+            for xl_ in range(2):
+                for t in range(8):
+                    x_, z_ = chunk(t, xl_)
+                    part_ref[x_, z_, i] = got[xl_ * 128 + t * 16 : xl_ * 128 + t * 16 + 16]
+            return carry
+
+        lax.fori_loop(0, 2, go, 0)
 
     def grad_wo():
         got = tn(mixed[...], branch_all[...]).astype(BF16)
@@ -701,8 +724,8 @@
         elif n == 1:
             total[...] = second_sum(2)
         else:
-            total[:, :, :256] = second_sum(3)
-            total[:, :, 256:] = second_sum(4)
+            total[:2] = second_sum(3)
+            total[2:] = second_sum(4)
         for r in (1, 3, 2):
             along_y(n, r).start()
         every[place, c, y] = total[y]
@@ -713,6 +736,9 @@
         return arrays[n].at[((z + 4 - r % 4) % 4) * 2 + (xh + r // 4) % 2, c_]
 
     def gd(n, r, recv=False):
+        if n == 2:
+            ref = spot(n, r if recv else 0, c)
+            return remote(ref, ref, gd_s.at[n, r], gd_r.at[n, r], dev(x + 2 * (r // 4), y, z + r % 4, c))
         ref = spot(n, r if recv else 4 * (r // 5), c)
         return remote(ref, ref, gd_s.at[n, r], gd_r.at[n, r], dev(x + 2 * (r == 4), y, z + r % 4, c))
 
@@ -772,13 +798,13 @@
         if n != 2:
             for r in (1, 3, 2):
                 along_y(min(n, 2), r, True).wait_recv()
-        for r in (4, 2, 1, 3):
+        for r in (6, 4, 5, 7, 2, 1, 3) if n == 2 else (4, 2, 1, 3):
             gd(n, r).start()
         gp(n, 0).start()
 
     def spread_next(n):
         gd(n, 4, True).wait_recv()
-        for r in (6, 5, 7):
+        for r in () if n == 2 else (6, 5, 7):
             gd(n, r).start()
         gp(n, 4).start()
 
@@ -797,29 +823,28 @@
 
     def attend_back(i):
         width = (i + 1) * BLOCK
-        cut = slice(i * BLOCK, (i + 1) * BLOCK)
-        grad_bf = g_mixed[cut, :]
-        grad_t = grad_bf.astype(F32).T
+        cut = slice(i * BLOCK, width)
+        inverse = inv[i : i + 1, :]
+        grad_t = g_mixed[cut, :].astype(F32).T
         products = grad_t * mixed_t[:, cut]
-        queries_t = []
-        for h in range(2):
-            lanes = slice(64 * h, 64 * h + 64)
-            grad_h = grad_bf[:, lanes]
-            delta = jnp.sum(products[lanes, :], axis=0, keepdims=True)
-            probs = p_t[h, i, :width, :]
-            gv_acc[h, :width, :] += nn(probs, grad_h)
-            g_probs = nt(v_h[h, :width, :], grad_h)
-            g_scores = (probs.astype(F32) * (g_probs - delta)).astype(BF16)
-            gk_acc[h, :width, :] += nn(g_scores, q_h[h, cut, :])
-            queries_t.append(nn(k_t[lanes, :width], g_scores))
-        g_query = (jnp.concatenate(queries_t, axis=0) * 0.125).T
-        g_qkv[cut, :128] = unturn(g_query, cut)
+        scaled = jnp.concatenate([grad_t[:HEAD_DIM] * inverse[:, :BLOCK], grad_t[HEAD_DIM:] * inverse[:, BLOCK:]], axis=0)
+        delta = inverse * jnp.concatenate(
+            [jnp.sum(products[:HEAD_DIM], axis=0, keepdims=True), jnp.sum(products[HEAD_DIM:], axis=0, keepdims=True)], axis=1
+        )
+        grad_two = two_heads(scaled.T).astype(BF16)
+        weights = p_t[i, :width, :]
+        gv_acc[:width, :] += nn(weights, grad_two)
+        g_probs = nt(v_all[:width, :], grad_two)
+        g_scores = (weights.astype(F32) * (g_probs - delta)).astype(BF16)
+        gk_acc[:width, :] += nn(g_scores, q_two[i, :, :128])
+        g_query = own_quarters(nn(k_t[:, :width], g_scores)) * 0.125
+        g_qkv[cut, :128] = unturn(g_query.T, cut)
 
     def block_back(i):
         cut = slice(i * BLOCK, (i + 1) * BLOCK)
         attend_back(i)
-        g_qkv[cut, 128:256] = unturn(jnp.concatenate([gk_acc[0, cut, :], gk_acc[1, cut, :]], axis=1), cut)
-        g_qkv[cut, 256:] = jnp.concatenate([gv_acc[0, cut, :], gv_acc[1, cut, :]], axis=1).astype(BF16)
+        g_qkv[cut, 128:256] = unturn(gk_acc[cut, :] * (1.0 / LOG2_E), cut)
+        g_qkv[cut, 256:] = gv_acc[cut, :].astype(BF16)
         rs_put(3, i, nt(g_qkv[cut, :], wqkv[...]))
 
     block_back(3)
@@ -833,24 +858,25 @@
     ag_pass(branch_all, 3)
     ring_one(0)
     share(1)
-    lax.fori_loop(0, 4, grad_qkv, 0)
+    grad_qkv(dqb, 2)
     first_start(4)
+    grad_qkv(dqa, 0)
     first_start(3)
     rs_near(3, 0)
     rs_near(3, 1)
     ring_two(0)
-    ring_one(1)
     ag_far(branch_all, 3)
     rs_mid(3)
+    ring_one(1)
+    first_sum(4)
+    first_sum(3)
     rs_far(2)
     ag_finish(branch_all, 3)
     grad_wo()
     first_start(5)
+    ring_two(1)
     rs_near(2, 0)
     rs_near(2, 1)
-    first_sum(3)
-    first_sum(4)
-    ring_two(1)
 
     grad = rs_finish(3)
     scale = rms_scale(x32)
@@ -884,6 +910,7 @@
     lax.fori_loop(1, 8, v1_start, 0)
     ring_three(0)
     spread_start(3)
+    ring_three(1)
     rs_mid(2)
     wo_send[...] = second_sum(5)
     swap_start(wo_send, all_wo.at[place, (c + moves) % 2], 4)
@@ -906,17 +933,16 @@
     spread_next(3)
     swap_wait(wo_send, all_wo.at[place, c], 4)
     spread_start(2)
-    ring_three(1)
     lo_send[...] = (hidden[...] + rs_finish(2)).astype(BF16)
     swap_start(lo_send, layer_out, 2)
-    spread_next(2)
     lax.fori_loop(1, 8, v2_wait, 0)
     v3s[...] = jnp.sum(v2r[...], axis=0) + v2s[...]
     v3_copy = remote(v3s, v3r, v3_ss.at[0], v3_rs.at[0], sibling)
     v3_copy.start()
+    ring_four(0)
     spread_pass(3)
-    ring_four(0)
     ring_four(1)
+    spread_next(2)
     spread_pass(2)
     v3_copy.wait()
     vec_out[...] = v3s[...] + v3r[...]
@@ -969,16 +995,16 @@
         return pltpu.SemaphoreType.DMA(shape)
 
     full = vmem(D, D)
-    shares = ((4, 16, 512), (4, 16, 256), (4, 48, 128), (4, 16, 256), (4, 16, 128), (64, 128))
+    shares = ((4, 16, 512), (4, 16, 256), (4, 48, 128), (2, 16, FB), (2, 16, FB), (64, 128))
     scratch = [
-        vmem(D, 128, dtype=F32), vmem(D, 128, dtype=F32), vmem(1, D, dtype=jnp.int32), vmem(8, 128, dtype=F32),
+        vmem(D, 128, dtype=F32), vmem(D, 128, dtype=F32), vmem(8, 128, dtype=F32),
         vmem(PIECE, D), vmem(PIECE, D), vmem(PIECE, D, dtype=F32), vmem(PIECE, D, dtype=F32),
         full, vmem(D, FB), vmem(D, 2 * FB), vmem(FB, D), vmem(8, 8, 128, dtype=F32),
         full, full, full, full,
-        vmem(2, D, 64), vmem(2, D, 64), vmem(2, D, 64), vmem(128, D), vmem(128, D),
-        vmem(2, 4, D, BLOCK), vmem(128, D, dtype=F32), vmem(D, 128), vmem(PIECE, D), vmem(PIECE, D),
+        vmem(4, 2 * BLOCK, 256), vmem(D, 256), vmem(D, 128), vmem(128, D), vmem(128, D),
+        vmem(4, D, 2 * BLOCK), vmem(8, 2 * BLOCK, dtype=F32), vmem(128, D, dtype=F32), vmem(D, 128), vmem(PIECE, D), vmem(PIECE, D),
         vmem(D, FB, dtype=F32), vmem(D, FB), vmem(FB, D), vmem(D, 2 * FB), vmem(D, 128),
-        vmem(2, D, 64, dtype=F32), vmem(2, D, 64, dtype=F32), vmem(D, FB),
+        vmem(D, 128, dtype=F32), vmem(D, 128, dtype=F32), vmem(D, FB),
         vmem(2, 4, BLOCK, D), vmem(4, 4, PIECE, D), vmem(4, PIECE, D), vmem(4, 2, 64, D), vmem(4, 2, PIECE, D), vmem(4, 2, PIECE, D),
         *(vmem(4, 4, *dims) for dims in shares),
         *(vmem(3, 4, *dims) for dims in shares),

time: 128 us -> 126 us (0.984)
  Pallas kernels: 127 us -> 125 us
    pallas_call x1, Pallas kernels: 124 us -> 122 us  [fused_layer(): pl.pallas_call(layer_kernel, out_shape=(out(PIECE, D), out(PIECE, D), out...]
where the time goes in v5:
time: 126 us
  Pallas kernels  125 us (99%)
    pallas_call x1, Pallas kernels, fused_layer(): pl.pallas_call(layer_kernel, out_shape=(out(PIECE, D), out(PIECE, D), out...  122 us
    pallas_call x1, Pallas kernels, spread(): pl.pallas_call(spread_kernel, out_shape=(out(PIECE, D, dtype=BF16), out(P...  3.56 us

profile of v5, /device:TPU:1, one launch (start us, length us, event | category | flops | bytes accessed | tf_op | source)
XLA Modules:
  0.0 126.2 jit_solution(8100080366637983489)
XLA Ops:
  0.7 121.8 %layer.1 = (bf16[128,1024]{1,0:T(8,128)(2,1)S(1)}, bf16[128,1024]{1,0:T(8,128)(2,1)S(1)}, bf16[8,2,4,16,768]{4,3,2,1,0:T(8,128)(2,1)S(1)}, bf16[8,2,4,48,128]{4,...) custom-call(bf16[128,1024]{1,0:T(8,128)(2,1)} %bitcast.14, ...), custom_call_target="tpu_custom_call" | custom-call | tf_op jit(solution)/shard_map/layer/pallas_call | solution.py:1029
  122.4 3.6 %spread.1 = (bf16[128,1024]{1,0:T(8,128)(2,1)}, f32[128,1024]{1,0:T(8,128)}, f32[1,128]{1,0:T(1,128)}, f32[128,1024]{1,0:T(8,128)}, f32[128,1024]{1,0:T(8,128)},...) custom-call(bf16[128,1024]{1,0:T(8,128)(2,1)S(1)} %get-tuple-element, ...), custom_call_target="tpu_custom_call" | custom-call | tf_op jit(solution)/shard_map/spread/pallas_call | solution.py:1106

commit v6 on v5

--- a/solution.py
+++ b/solution.py
@@ -97,6 +97,12 @@
             src_ref=src, dst_ref=dst, send_sem=ss, recv_sem=rs, device_id=to, device_id_type=MESH
         )
 
+    def all_in(ref, sem):
+        remote(ref, ref, sem, sem, sibling).wait_recv()
+
+    def all_sent(ref, sem):
+        remote(ref, ref, sem, sem, sibling).wait_send()
+
     def at(start, size, unit):
         return pl.ds(pl.multiple_of(start, unit), size)
 
@@ -104,14 +110,14 @@
     own_win = at(window(j), FB, 128)
     loads = [
         pltpu.make_async_copy(wq_in.at[:, rows(j * 128, 128)], wqkv.at[own_rows, pl.ds(0, 128)], sem_load.at[0]),
-        pltpu.make_async_copy(wk_in.at[:, rows(j * 128, 128)], wqkv.at[own_rows, pl.ds(128, 128)], sem_load.at[1]),
-        pltpu.make_async_copy(wv_in.at[:, rows(j * 128, 128)], wqkv.at[own_rows, pl.ds(256, 128)], sem_load.at[2]),
-        pltpu.make_async_copy(wo_in, wo_all.at[own_rows], sem_load.at[3]),
-        pltpu.make_async_copy(wg_in.at[:, own_win], wgu.at[own_rows, pl.ds(0, FB)], sem_load.at[4]),
-        pltpu.make_async_copy(wu_in.at[:, own_win], wgu.at[own_rows, pl.ds(FB, FB)], sem_load.at[5]),
-        pltpu.make_async_copy(wd_in.at[own_win, :], wdn.at[:, own_rows], sem_load.at[6]),
-        pltpu.make_async_copy(cos_in, cos_ref, sem_load.at[7]),
-        pltpu.make_async_copy(sin_in, sin_ref, sem_load.at[8]),
+        pltpu.make_async_copy(wk_in.at[:, rows(j * 128, 128)], wqkv.at[own_rows, pl.ds(128, 128)], sem_load.at[0]),
+        pltpu.make_async_copy(wv_in.at[:, rows(j * 128, 128)], wqkv.at[own_rows, pl.ds(256, 128)], sem_load.at[0]),
+        pltpu.make_async_copy(wo_in, wo_all.at[own_rows], sem_load.at[1]),
+        pltpu.make_async_copy(wg_in.at[:, own_win], wgu.at[own_rows, pl.ds(0, FB)], sem_load.at[2]),
+        pltpu.make_async_copy(wu_in.at[:, own_win], wgu.at[own_rows, pl.ds(FB, FB)], sem_load.at[2]),
+        pltpu.make_async_copy(wd_in.at[own_win, :], wdn.at[:, own_rows], sem_load.at[3]),
+        pltpu.make_async_copy(cos_in, cos_ref, sem_load.at[4]),
+        pltpu.make_async_copy(sin_in, sin_ref, sem_load.at[5]),
     ]
     for load in loads:
         load.start()
@@ -167,14 +173,10 @@
             pltpu.make_async_copy(src, dst, swap_r.at[n]).wait()
 
     def vec_copy(r):
-        return remote(vec_in, vall.at[f], vec_s.at[r], vec_r.at[r], (s, (f + r) % 8))
+        return remote(vec_in, vall.at[f], vec_s.at[0], vec_r.at[0], (s, (f + r) % 8))
 
     def vec_start(r, carry):
         vec_copy(r).start()
-        return carry
-
-    def vec_wait(r, carry):
-        vec_copy(r).wait()
         return carry
 
     vec_in[...] = jnp.zeros_like(vec_in)
@@ -219,17 +221,27 @@
         else:
             src = wo_in.at[at(c * 64 + z * 16, 16, 16)]
         dst = w_quarter(n, shard(r) if recv else f, z, p)
-        return remote(src, dst, wy_s.at[n, p, r], wy_r.at[n, p, r], dev(x, y + r, z, c))
+        return remote(src, dst, wy_s.at[n], wy_r.at[n, r - 1], dev(x, y + r, z, c))
 
     def w_z(n, r, dz, recv=False):
         src = w_quarter(n, shard(r), z)
         dst = w_quarter(n, shard(r), (z + 4 - dz) % 4) if recv else src
-        return remote(src, dst, wz_s.at[n, r, dz], wz_r.at[n, r, dz], dev(x, y, z + dz, c))
+        return remote(src, dst, wz_s.at[n], wz_r.at[n, r - 1], dev(x, y, z + dz, c))
 
     def w_x(n, r, recv=False):
         src = w_rows(n, shard(r))
         dst = w_rows(n, ((y + 4 - r) % 4) * 2 + 1 - xl) if recv else src
-        return remote(src, dst, wx_s.at[n, r], wx_r.at[n, r], x_to)
+        return remote(src, dst, wx_s.at[n], wx_r.at[n], x_to)
+
+    def quarters(n, count):
+        if n == 2:
+            return wdn.at[pl.ds(0, 96 * count)] if count == 1 else wdn.at[pl.ds(0, 288), pl.ds(0, 128 * (count // 3))]
+        return (wqkv, wgu, None, wo_all)[n].at[pl.ds(0, (32, 32, 0, 16)[n] * count)]
+
+    def blocks(n, count):
+        if n == 2:
+            return wdn.at[:, pl.ds(0, 128 * count)]
+        return (wqkv, wgu, None, wo_all)[n].at[pl.ds(0, (128, 128, 0, 64)[n] * count)]
 
     def w_ystart(n):
         for r in (1, 3, 2):
@@ -237,42 +249,38 @@
                 w_y(n, p, r).start()
 
     def w_own(n):
-        for load in (loads[:3], loads[4:6], loads[6:7], loads[3:4])[n]:
-            load.wait()
+        own = wo_all.at[own_rows] if n == 3 else w_rows(n, f)
+        pltpu.make_async_copy(own, own, sem_load.at[(0, 2, 3, 1)[n]]).wait()
         w_x(n, 0).start()
 
     def w_zstart(n):
         for r in (1, 3, 2):
-            for p in range(PARTS[n]):
-                w_y(n, p, r, True).wait_recv()
+            all_in(w_quarter(n, shard(r), z), wy_r.at[n, r - 1])
             for dz in (1, 3, 2):
                 w_z(n, r, dz).start()
 
     def w_xstart(n):
         for r in (1, 3, 2):
-            for dz in (1, 3, 2):
-                w_z(n, r, dz, True).wait_recv()
+            all_in(quarters(n, 3), wz_r.at[n, r - 1])
             w_x(n, r).start()
             if n == 3:
                 wo_pass(2 * ((4 - r) % 4)).start()
 
     def w_finish(n):
-        for r in range(4):
-            w_x(n, r, True).wait_recv()
+        all_in(blocks(n, 4), wx_r.at[n])
 
     def wo_pass(n, recv=False):
         f_ = ((y + n // 2) % 4) * 2 + (xl + n % 2) % 2
         ref = wo_all.at[rows(f_ * 128 + ((1 - c) if recv else c) * 64, 64)]
-        return remote(ref, ref, wp_s.at[n], wp_r.at[n], sibling)
+        return remote(ref, ref, wp_s.at[0], wp_r.at[0], sibling)
 
     def wo_pass_x():
+        all_in(blocks(3, 4), wx_r.at[3])
         for r in range(4):
-            w_x(3, r, True).wait_recv()
             wo_pass(2 * ((4 - r) % 4) + 1).start()
 
     def wo_pass_finish():
-        for n in range(1, 8):
-            wo_pass(n, True).wait_recv()
+        all_in(wo_all.at[pl.ds(0, 448)], wp_r.at[0])
 
     for n in (0, 3, 2, 1):
         w_ystart(n)
@@ -303,27 +311,24 @@
             ref, to = (piece(buf, y + 1, 1 - c) if recv else piece(buf, y + 1, c)), sibling
         else:
             ref, to = (piece(buf, y + 2, 1 - c) if recv else piece(buf, y + 2, c)), sibling
-        return remote(ref, ref, ag_s.at[k, n], ag_r.at[k, n], to)
+        return remote(ref, ref, ag_s.at[k], ag_r.at[k, (0, 0, 3, 2, 4, 2, 5, 6, 1, 1)[n]], to)
 
     def ag_start(buf, k):
         for n in (0, 1, 2, 8, 9):
             ag(buf, k, n).start()
 
     def ag_near(buf, k):
-        ag(buf, k, 0, True).wait_recv()
+        all_in(buf.at[pl.ds(0, PIECE)], ag_r.at[k, 0])
         ag(buf, k, 3).start()
-        ag(buf, k, 1, True).wait_recv()
         ag(buf, k, 5).start()
 
     def ag_pass(buf, k):
-        ag(buf, k, 8, True).wait_recv()
+        all_in(buf.at[pl.ds(0, PIECE)], ag_r.at[k, 1])
         ag(buf, k, 4).start()
-        ag(buf, k, 9, True).wait_recv()
         ag(buf, k, 6).start()
 
     def ag_far(buf, k):
-        ag(buf, k, 3, True).wait_recv()
-        ag(buf, k, 5, True).wait_recv()
+        all_in(buf.at[pl.ds(0, PIECE)], ag_r.at[k, 2])
         ag(buf, k, 7).start()
 
     def ag_finish(buf, k):
@@ -373,18 +378,16 @@
 
     def c_sib(k, a):
         src = held(k).at[a, rows((1 - c) * PIECE, PIECE)]
-        return remote(src, sib.at[k, a], sib_ss.at[k, a], sib_rs.at[k, a], sibling)
+        return remote(src, sib.at[k, a], sib_ss.at[k], sib_rs.at[k, a], sibling)
 
     def c_far(k, n):
-        return remote(far_s.at[k, pl.ds(64 * n, 64)], far_r.at[k, n], far_ss.at[k, n], far_rs.at[k, n], y_up if n == 0 else y_dn)
+        return remote(far_s.at[k, pl.ds(64 * n, 64)], far_r.at[k, n], far_ss.at[k], far_rs.at[k], y_up if n == 0 else y_dn)
 
     def c_fin(k, n, h):
         cut = pl.ds(64 * h, 64)
-        return remote(fin_s.at[k, n, cut], fin_r.at[k, n, cut], fin_ss.at[k, n, h], fin_rs.at[k, n, h], y_up if n == 0 else y_dn)
+        return remote(fin_s.at[k, n, cut], fin_r.at[k, n, cut], fin_ss.at[k], fin_rs.at[k], y_up if n == 0 else y_dn)
 
     def rs_put(k, a, value):
-        if k == 3:
-            c_sib(1, a).wait_send()
         held(k)[a] = value.astype(BF16)
         c_sib(k, a).start()
 
@@ -402,21 +405,20 @@
         c_fin(k, n, 1 - n).start()
 
     def rs_mid(k):
+        all_in(far_r.at[k], far_rs.at[k])
         for n in (0, 1):
-            c_far(k, n).wait_recv()
             cut = pl.ds(64 * n, 64)
             fin_s[k, n, cut] = (fin_s[k, n, cut].astype(F32) + far_r[k, n].astype(F32)).astype(BF16)
             c_fin(k, n, n).start()
 
     def rs_finish(k):
         total = rs_pair(k, y)
-        for n in (0, 1):
-            for h in (0, 1):
-                c_fin(k, n, h).wait_recv()
+        all_in(fin_r.at[k], fin_rs.at[k])
         return total + fin_r[k, 0].astype(F32) + fin_r[k, 1].astype(F32)
 
     w_zstart(0)
-    lax.fori_loop(1, 8, vec_wait, 0)
+    all_in(vall.at[pl.ds(0, 7)], vec_r.at[0])
+    all_sent(vall.at[pl.ds(0, 7)], vec_s.at[0])
 
     def gathered(row):
         return jnp.concatenate([vall[i, row : row + 1, :] for i in range(8)], axis=1)
@@ -508,7 +510,7 @@
     def mix(m, sender):
         return remote(
             mixed.at[rows(m * PIECE, PIECE), :], mixed_own.at[:, rows(sender * 128, 128)],
-            mx_s.at[m], mx_r.at[sender], dev(x, m // 2, z, m % 2),
+            mx_s.at[0], mx_r.at[0], dev(x, m // 2, z, m % 2),
         )
 
     def mix_start(m):
@@ -519,12 +521,6 @@
         @pl.when(j == m)
         def _():
             mixed_own[:, rows(j * 128, 128)] = mixed[m * PIECE : (m + 1) * PIECE, :]
-
-    def mix_wait(r, carry):
-        m = (j + r) % 8
-        mix(m, m).wait_recv()
-        mix(m, j).wait_send()
-        return carry
 
     w_xstart(2)
     attend(0)
@@ -536,7 +532,8 @@
     attend(3)
     ag_pass(cot_all, 1)
     wo_pass_finish()
-    lax.fori_loop(1, 8, mix_wait, 0)
+    all_in(mixed_own.at[:, pl.ds(0, 896)], mx_r.at[0])
+    all_sent(mixed.at[pl.ds(0, 896)], mx_s.at[0])
 
     hidden[...] = x_own[...].astype(F32) + nn(mixed_own[...], wo_all[...])
     hid = hidden[...]
@@ -586,14 +583,14 @@
             src, to = terms[n].at[(x + r) % 4], dev(x + r, y, z, c)
         else:
             src, to = terms[n].at[:, (z + r) % 4], dev(x, y, z + r, c)
-        return remote(src, term_in[n].at[r - 1], f1_s.at[n, r], f1_r.at[n, r], to)
+        return remote(src, term_in[n].at[r - 1], f1_s.at[n], f1_r.at[n], to)
 
     def second(n, r):
         if n in (0, 3, 5):
             src, to = halfway[n].at[(z + r) % 4], dev(x, y, z + r, c)
         else:
             src, to = halfway[n].at[(x + r) % 4], dev(x + r, y, z, c)
-        return remote(src, half_in[n].at[r - 1], f2_s.at[n, r], f2_r.at[n, r], to)
+        return remote(src, half_in[n].at[r - 1], f2_s.at[n], f2_r.at[n], to)
 
     def first_start(n):
         for r in (1, 3, 2):
@@ -601,8 +598,8 @@
 
     def first_sum(n):
         total = (terms[n][x] if n in (0, 3, 5) else terms[n][:, z]).astype(F32)
+        all_in(term_in[n], f1_r.at[n])
         for r in (1, 3, 2):
-            first(n, r).wait()
             total = total + term_in[n][r - 1].astype(F32)
         halfway[n][...] = total.astype(BF16)
         for r in (1, 3, 2):
@@ -610,8 +607,8 @@
 
     def second_sum(n):
         total = halfway[n][z if n in (0, 3, 5) else x].astype(F32)
+        all_in(half_in[n], f2_r.at[n])
         for r in (1, 3, 2):
-            second(n, r).wait()
             total = total + half_in[n][r - 1].astype(F32)
         return total.astype(BF16)
 
@@ -683,17 +680,11 @@
     def unmix(m, sender):
         return remote(
             mixed_grad.at[:, rows(m * 128, 128)], g_mixed.at[rows(sender * PIECE, PIECE), :],
-            um_s.at[m], um_r.at[sender], dev(x, m // 2, z, m % 2),
+            um_s.at[0], um_r.at[0], dev(x, m // 2, z, m % 2),
         )
 
     def unmix_start(r, carry):
         unmix((j + r) % 8, j).start()
-        return carry
-
-    def unmix_wait(r, carry):
-        m = (j + r) % 8
-        unmix(m, m).wait_recv()
-        unmix(m, j).wait_send()
         return carry
 
     lax.fori_loop(1, 8, unmix_start, 0)
@@ -708,13 +699,15 @@
     lax.fori_loop(0, 4, output_term, 0)
     first_sum(1)
     first_sum(0)
-    lax.fori_loop(1, 8, unmix_wait, 0)
+    all_in(g_mixed.at[pl.ds(0, 896)], um_r.at[0])
+    all_sent(mixed_grad.at[:, pl.ds(0, 896)], um_s.at[0])
+    all_sent(sib.at[1], sib_ss.at[1])
     ag_start(branch_all, 3)
 
     def along_y(n, r, recv=False):
         src = (sum_gu, sum_dn, sum_qkv)[n].at[(y + r) % 4]
         dst = (all_gu, all_dn, all_qkv)[n].at[place, c, (y + 4 - r) % 4 if recv else y]
-        return remote(src, dst, ya_s.at[n, r], ya_r.at[n, r], dev(x, y + r, z, c))
+        return remote(src, dst, ya_s.at[n], ya_r.at[n], dev(x, y + r, z, c))
 
     def share(n):
         total, every = ((sum_gu, all_gu), (sum_dn, all_dn), (sum_qkv, all_qkv))[n]
@@ -738,13 +731,13 @@
     def gd(n, r, recv=False):
         if n == 2:
             ref = spot(n, r if recv else 0, c)
-            return remote(ref, ref, gd_s.at[n, r], gd_r.at[n, r], dev(x + 2 * (r // 4), y, z + r % 4, c))
+            return remote(ref, ref, gd_s.at[n - 2], gd_r.at[3 if n == 2 else (0, 1, 1, 1, 0, 2, 2, 2)[r]], dev(x + 2 * (r // 4), y, z + r % 4, c))
         ref = spot(n, r if recv else 4 * (r // 5), c)
-        return remote(ref, ref, gd_s.at[n, r], gd_r.at[n, r], dev(x + 2 * (r == 4), y, z + r % 4, c))
+        return remote(ref, ref, gd_s.at[n - 2], gd_r.at[3 if n == 2 else (0, 1, 1, 1, 0, 2, 2, 2)[r]], dev(x + 2 * (r == 4), y, z + r % 4, c))
 
     def gp(n, r, recv=False):
         ref = spot(n, r, (1 - c) if recv else c)
-        return remote(ref, ref, gp_s.at[n, r], gp_r.at[n, r], sibling)
+        return remote(ref, ref, gp_s.at[n - 2], gp_r.at[n - 2], sibling)
 
     def pair(n, z_, c_):
         return arrays[n].at[pl.ds(((z_ + 4) % 4) * 2, 2), c_]
@@ -765,11 +758,10 @@
             ref, to = single(n, z + 2 if recv else z + 1, 1), dev(x, y, z + 3, c)
         else:
             ref, to = pair(n, z + (k - 5), (1 - c) if recv else c), sibling
-        return remote(ref, ref, rg_s.at[n, k], rg_r.at[n, k], to)
+        return remote(ref, ref, rg_s.at[n, k // 5], rg_r.at[n, (0, 1, 1, 2, 2, 3, 3, 3, 3)[k]], to)
 
     def ring_one(n):
-        for r in (1, 3, 2):
-            along_y(n, r, True).wait_recv()
+        all_in(arrays[n].at[place, c, pl.ds(0, 3)], ya_r.at[n])
         ring(n, 0).start()
 
     def ring_two(n):
@@ -778,44 +770,44 @@
             ring(n, k).start()
 
     def ring_three(n):
-        ring(n, 1, True).wait_recv()
-        ring(n, 3).start()
-        ring(n, 8).start()
-        ring(n, 2, True).wait_recv()
-        ring(n, 4).start()
-        ring(n, 6).start()
+        all_in(arrays[n].at[pl.ds(0, 4), c], rg_r.at[n, 1])
+        for k in (3, 4, 8, 6):
+            ring(n, k).start()
 
     def ring_four(n):
-        ring(n, 3, True).wait_recv()
-        ring(n, 4, True).wait_recv()
+        all_in(arrays[n].at[pl.ds(0, 2), c], rg_r.at[n, 2])
         ring(n, 7).start()
 
     def ring_five(n):
-        for k in (5, 6, 7, 8):
-            ring(n, k, True).wait_recv()
+        all_in(arrays[n].at[:, c], rg_r.at[n, 3])
 
     def spread_start(n):
         if n != 2:
-            for r in (1, 3, 2):
-                along_y(min(n, 2), r, True).wait_recv()
+            all_in(arrays[n].at[place, c, pl.ds(0, 3)], ya_r.at[min(n, 2)])
         for r in (6, 4, 5, 7, 2, 1, 3) if n == 2 else (4, 2, 1, 3):
             gd(n, r).start()
         gp(n, 0).start()
 
     def spread_next(n):
-        gd(n, 4, True).wait_recv()
-        for r in () if n == 2 else (6, 5, 7):
-            gd(n, r).start()
-        gp(n, 4).start()
+        if n == 3:
+            gd(n, 4, True).wait_recv()
+            for r in (6, 5, 7):
+                gd(n, r).start()
+            gp(n, 4).start()
 
     def spread_pass(n):
-        for r in (1, 3, 2, 5, 7, 6):
-            gd(n, r, True).wait_recv()
-            gp(n, r).start()
+        if n == 2:
+            all_in(arrays[n].at[pl.ds(0, 7), c], gd_r.at[3])
+            for r in range(1, 8):
+                gp(n, r).start()
+        else:
+            for i, steps in ((1, (1, 3, 2)), (2, (5, 7, 6))):
+                all_in(arrays[n].at[pl.ds(0, 3), c], gd_r.at[i])
+                for r in steps:
+                    gp(n, r).start()
 
     def spread_finish(n):
-        for r in range(8):
-            gp(n, r, True).wait_recv()
+        all_in(arrays[n].at[:, c], gp_r.at[n - 2])
 
     def unturn(value, cut):
         value = value.astype(BF16).astype(F32)
@@ -826,9 +818,10 @@
         cut = slice(i * BLOCK, width)
         inverse = inv[i : i + 1, :]
         grad_t = g_mixed[cut, :].astype(F32).T
-        products = grad_t * mixed_t[:, cut]
         scaled = jnp.concatenate([grad_t[:HEAD_DIM] * inverse[:, :BLOCK], grad_t[HEAD_DIM:] * inverse[:, BLOCK:]], axis=0)
-        delta = inverse * jnp.concatenate(
+        scaled = scaled.astype(BF16).astype(F32)
+        products = scaled * mixed_t[:, cut]
+        delta = jnp.concatenate(
             [jnp.sum(products[:HEAD_DIM], axis=0, keepdims=True), jnp.sum(products[HEAD_DIM:], axis=0, keepdims=True)], axis=1
         )
         grad_two = two_heads(scaled.T).astype(BF16)
@@ -855,26 +848,25 @@
     block_back(1)
     block_back(0)
     rs_far(3)
-    ag_pass(branch_all, 3)
-    ring_one(0)
-    share(1)
     grad_qkv(dqb, 2)
     first_start(4)
+    ring_one(0)
     grad_qkv(dqa, 0)
     first_start(3)
     rs_near(3, 0)
     rs_near(3, 1)
-    ring_two(0)
+    ag_pass(branch_all, 3)
+    share(1)
     ag_far(branch_all, 3)
     rs_mid(3)
-    ring_one(1)
+    ring_two(0)
     first_sum(4)
     first_sum(3)
+    ring_one(1)
     rs_far(2)
     ag_finish(branch_all, 3)
     grad_wo()
     first_start(5)
-    ring_two(1)
     rs_near(2, 0)
     rs_near(2, 1)
 
@@ -885,6 +877,7 @@
     ig_send[...] = (g_hidden[...] + back).astype(BF16)
     swap_start(ig_send, in_grad, 3)
     share(2)
+    ring_two(1)
     first_sum(5)
 
     gain_one = jnp.sum(grad * x32 * scale, axis=0, keepdims=True)
@@ -897,14 +890,10 @@
         vs[pl.ds(j, 1), 2 + i : 3 + i, :] = bias_sum[:, 128 * i : 128 * i + 128][None]
 
     def v1_copy(r):
-        return remote(vs.at[(f + r) % 8], vr.at[r - 1], v1_ss.at[r - 1], v1_rs.at[r - 1], (s, (f + r) % 8))
+        return remote(vs.at[(f + r) % 8], vr.at[r - 1], v1_ss.at[0], v1_rs.at[0], (s, (f + r) % 8))
 
     def v1_start(r, carry):
         v1_copy(r).start()
-        return carry
-
-    def v1_wait(r, carry):
-        v1_copy(r).wait()
         return carry
 
     lax.fori_loop(1, 8, v1_start, 0)
@@ -914,19 +903,16 @@
     rs_mid(2)
     wo_send[...] = second_sum(5)
     swap_start(wo_send, all_wo.at[place, (c + moves) % 2], 4)
-    lax.fori_loop(1, 8, v1_wait, 0)
+    all_in(vr, v1_rs.at[0])
+    all_sent(vr, v1_ss.at[0])
     v2s[...] = jnp.sum(vr[...], axis=0) + vs[pl.ds(f, 1)][0]
 
     def v2_copy(r):
         to = dev(x + 2 * (r // 4), y, z + r % 4, c)
-        return remote(v2s, v2r.at[r - 1], v2_ss.at[r - 1], v2_rs.at[r - 1], to)
+        return remote(v2s, v2r.at[r - 1], v2_ss.at[0], v2_rs.at[0], to)
 
     def v2_start(r, carry):
         v2_copy(r).start()
-        return carry
-
-    def v2_wait(r, carry):
-        v2_copy(r).wait()
         return carry
 
     lax.fori_loop(1, 8, v2_start, 0)
@@ -935,7 +921,8 @@
     spread_start(2)
     lo_send[...] = (hidden[...] + rs_finish(2)).astype(BF16)
     swap_start(lo_send, layer_out, 2)
-    lax.fori_loop(1, 8, v2_wait, 0)
+    all_in(v2r, v2_rs.at[0])
+    all_sent(v2r, v2_ss.at[0])
     v3s[...] = jnp.sum(v2r[...], axis=0) + v2s[...]
     v3_copy = remote(v3s, v3r, v3_ss.at[0], v3_rs.at[0], sibling)
     v3_copy.start()
@@ -954,37 +941,28 @@
         spread_finish(n)
 
     for n in range(4):
-        for r in (1, 2, 3):
-            for p in range(PARTS[n]):
-                w_y(n, p, r).wait_send()
-            for dz in (1, 2, 3):
-                w_z(n, r, dz).wait_send()
-        for r in range(4):
-            w_x(n, r).wait_send()
-    for n in range(1, 8):
-        wo_pass(n).wait_send()
+        all_sent(quarters(n, 3), wy_s.at[n])
+        all_sent(quarters(n, 9), wz_s.at[n])
+        all_sent(blocks(n, 4), wx_s.at[n])
+    all_sent(wo_all.at[pl.ds(0, 448)], wp_s.at[0])
     for k, buf in enumerate((normed_all, cot_all, mlp_all, branch_all)):
-        for n in range(10):
-            ag(buf, k, n).wait_send()
+        all_sent(buf.at[pl.ds(0, 896)], ag_s.at[k])
     for k in range(1, 4):
         if k > 1:
-            for i in range(4):
-                c_sib(k, i).wait_send()
-        for n in (0, 1):
-            c_far(k, n).wait_send()
-            for h in (0, 1):
-                c_fin(k, n, h).wait_send()
-    for n in range(3):
-        for r in (1, 2, 3):
-            along_y(n, r).wait_send()
+            all_sent(sib.at[k], sib_ss.at[k])
+        all_sent(far_s.at[k], far_ss.at[k])
+        all_sent(fin_s.at[k], fin_ss.at[k])
+    for n in range(6):
+        all_sent(term_in[n], f1_s.at[n])
+        all_sent(half_in[n], f2_s.at[n])
+    for n in (0, 1, 3):
+        all_sent(arrays[n].at[place, c, pl.ds(0, 3)], ya_s.at[min(n, 2)])
     for n in (0, 1):
-        for k in range(9):
-            ring(n, k).wait_send()
+        all_sent(arrays[n].at[pl.ds(0, 7), c], rg_s.at[n, 0])
+        all_sent(arrays[n].at[:, c], rg_s.at[n, 1])
     for n in (2, 3):
-        for r in range(8):
-            if r > 0:
-                gd(n, r).wait_send()
-            gp(n, r).wait_send()
+        all_sent(arrays[n].at[pl.ds(0, 7), c], gd_s.at[n - 2])
+        all_sent(arrays[n].at[:, c], gp_s.at[n - 2])
 
 
 def fused_layer(*args):
@@ -1014,11 +992,11 @@
         vmem(PIECE, D), vmem(PIECE, D),
         vmem(8, 8, 128, dtype=F32), vmem(7, 8, 128, dtype=F32), vmem(8, 128, dtype=F32), vmem(7, 8, 128, dtype=F32),
         vmem(8, 128, dtype=F32), vmem(8, 128, dtype=F32),
-        dma(9), dma(5), dma(5), dma(8), dma(8), dma(4, 3, 4), dma(4, 3, 4), dma(4, 4, 4), dma(4, 4, 4), dma(4, 4), dma(4, 4),
-        dma(8), dma(8), dma(8), dma(8), dma(8), dma(8), dma(4, 10), dma(4, 10),
-        dma(4, 4), dma(4, 4), dma(4, 2), dma(4, 2), dma(4, 2, 2), dma(4, 2, 2),
-        dma(6, 4), dma(6, 4), dma(6, 4), dma(6, 4), dma(3, 4), dma(3, 4), dma(2, 9), dma(2, 9), dma(4, 8), dma(4, 8), dma(4, 8), dma(4, 8),
-        dma(7), dma(7), dma(7), dma(7), dma(1), dma(1),
+        dma(6), dma(5), dma(5), dma(1), dma(1), dma(4), dma(4, 3), dma(4), dma(4, 3), dma(4), dma(4),
+        dma(1), dma(1), dma(1), dma(1), dma(1), dma(1), dma(4), dma(4, 7),
+        dma(4), dma(4, 4), dma(4), dma(4), dma(4), dma(4),
+        dma(6), dma(6), dma(6), dma(6), dma(3), dma(3), dma(2, 2), dma(2, 4), dma(2), dma(4), dma(2), dma(2),
+        dma(1), dma(1), dma(1), dma(1), dma(1), dma(1),
     ]
     anywhere = pl.BlockSpec(memory_space=pl.ANY)
     inside = pl.BlockSpec(memory_space=pltpu.VMEM)

time: 126 us -> 120 us (0.952)
  Pallas kernels: 125 us -> 119 us
    pallas_call x1, Pallas kernels: 122 us -> 116 us  [fused_layer(): pl.pallas_call(layer_kernel, out_shape=(out(PIECE, D), out(PIECE, D), out...]
where the time goes in v6:
time: 120 us
  Pallas kernels  119 us (99%)
    pallas_call x1, Pallas kernels, fused_layer(): pl.pallas_call(layer_kernel, out_shape=(out(PIECE, D), out(PIECE, D), out...  116 us
    pallas_call x1, Pallas kernels, spread(): pl.pallas_call(spread_kernel, out_shape=(out(PIECE, D, dtype=BF16), out(P...  3.56 us

profile of v6, /device:TPU:1, one launch (start us, length us, event | category | flops | bytes accessed | tf_op | source)
XLA Modules:
  0.0 120.1 jit_solution(4357351678293594350)
XLA Ops:
  0.7 115.8 %layer.1 = (bf16[128,1024]{1,0:T(8,128)(2,1)S(1)}, bf16[128,1024]{1,0:T(8,128)(2,1)S(1)}, bf16[8,2,4,16,768]{4,3,2,1,0:T(8,128)(2,1)S(1)}, bf16[8,2,4,48,128]{4,...) custom-call(bf16[128,1024]{1,0:T(8,128)(2,1)} %bitcast.14, ...), custom_call_target="tpu_custom_call" | custom-call | tf_op jit(solution)/shard_map/layer/pallas_call | solution.py:1007
  116.4 3.6 %spread.1 = (bf16[128,1024]{1,0:T(8,128)(2,1)}, f32[128,1024]{1,0:T(8,128)}, f32[1,128]{1,0:T(1,128)}, f32[128,1024]{1,0:T(8,128)}, f32[128,1024]{1,0:T(8,128)},...) custom-call(bf16[128,1024]{1,0:T(8,128)(2,1)S(1)} %get-tuple-element, ...), custom_call_target="tpu_custom_call" | custom-call | tf_op jit(solution)/shard_map/spread/pallas_call | solution.py:1084

commit v7 on v6

--- a/solution.py
+++ b/solution.py
@@ -526,10 +526,10 @@
     attend(0)
     attend(1)
     w_xstart(1)
-    ag_near(cot_all, 1)
     attend(2)
     wo_pass_x()
     attend(3)
+    ag_near(cot_all, 1)
     ag_pass(cot_all, 1)
     wo_pass_finish()
     all_in(mixed_own.at[:, pl.ds(0, 896)], mx_r.at[0])

time: 120 us -> 119 us (level)
  no operation moved by 1% of the time
where the time goes in v7:
time: 119 us
  Pallas kernels  118 us (99%)
    pallas_call x1, Pallas kernels, fused_layer(): pl.pallas_call(layer_kernel, out_shape=(out(PIECE, D), out(PIECE, D), out...  115 us
    pallas_call x1, Pallas kernels, spread(): pl.pallas_call(spread_kernel, out_shape=(out(PIECE, D, dtype=BF16), out(P...  3.56 us

profile of v7, /device:TPU:1, one launch (start us, length us, event | category | flops | bytes accessed | tf_op | source)
XLA Modules:
  0.0 119.0 jit_solution(4820281548850213466)
XLA Ops:
  0.7 114.7 %layer.1 = (bf16[128,1024]{1,0:T(8,128)(2,1)S(1)}, bf16[128,1024]{1,0:T(8,128)(2,1)S(1)}, bf16[8,2,4,16,768]{4,3,2,1,0:T(8,128)(2,1)S(1)}, bf16[8,2,4,48,128]{4,...) custom-call(bf16[128,1024]{1,0:T(8,128)(2,1)} %bitcast.14, ...), custom_call_target="tpu_custom_call" | custom-call | tf_op jit(solution)/shard_map/layer/pallas_call | solution.py:1007
  115.3 3.6 %spread.1 = (bf16[128,1024]{1,0:T(8,128)(2,1)}, f32[128,1024]{1,0:T(8,128)}, f32[1,128]{1,0:T(1,128)}, f32[128,1024]{1,0:T(8,128)}, f32[128,1024]{1,0:T(8,128)},...) custom-call(bf16[128,1024]{1,0:T(8,128)(2,1)S(1)} %get-tuple-element, ...), custom_call_target="tpu_custom_call" | custom-call | tf_op jit(solution)/shard_map/spread/pallas_call | solution.py:1084

commit v8 on v7

--- a/solution.py
+++ b/solution.py
@@ -221,17 +221,17 @@
         else:
             src = wo_in.at[at(c * 64 + z * 16, 16, 16)]
         dst = w_quarter(n, shard(r) if recv else f, z, p)
-        return remote(src, dst, wy_s.at[n], wy_r.at[n, r - 1], dev(x, y + r, z, c))
+        return remote(src, dst, wy_s.at[0], wy_r.at[r - 1 if n == 0 else n + 2], dev(x, y + r, z, c))
 
     def w_z(n, r, dz, recv=False):
         src = w_quarter(n, shard(r), z)
         dst = w_quarter(n, shard(r), (z + 4 - dz) % 4) if recv else src
-        return remote(src, dst, wz_s.at[n], wz_r.at[n, r - 1], dev(x, y, z + dz, c))
+        return remote(src, dst, wz_s.at[0], wz_r.at[r - 1 if n == 0 else n + 2], dev(x, y, z + dz, c))
 
     def w_x(n, r, recv=False):
         src = w_rows(n, shard(r))
         dst = w_rows(n, ((y + 4 - r) % 4) * 2 + 1 - xl) if recv else src
-        return remote(src, dst, wx_s.at[n], wx_r.at[n], x_to)
+        return remote(src, dst, wx_s.at[0], wx_r.at[n], x_to)
 
     def quarters(n, count):
         if n == 2:
@@ -254,14 +254,20 @@
         w_x(n, 0).start()
 
     def w_zstart(n):
+        if n > 0:
+            all_in(quarters(n, 3), wy_r.at[n + 2])
         for r in (1, 3, 2):
-            all_in(w_quarter(n, shard(r), z), wy_r.at[n, r - 1])
+            if n == 0:
+                all_in(w_quarter(n, shard(r), z), wy_r.at[r - 1])
             for dz in (1, 3, 2):
                 w_z(n, r, dz).start()
 
     def w_xstart(n):
+        if n > 0:
+            all_in(quarters(n, 9), wz_r.at[n + 2])
         for r in (1, 3, 2):
-            all_in(quarters(n, 3), wz_r.at[n, r - 1])
+            if n == 0:
+                all_in(quarters(n, 3), wz_r.at[r - 1])
             w_x(n, r).start()
             if n == 3:
                 wo_pass(2 * ((4 - r) % 4)).start()
@@ -378,14 +384,14 @@
 
     def c_sib(k, a):
         src = held(k).at[a, rows((1 - c) * PIECE, PIECE)]
-        return remote(src, sib.at[k, a], sib_ss.at[k], sib_rs.at[k, a], sibling)
+        return remote(src, sib.at[k, a], sib_ss.at[k - 1], sib_rs.at[k - 1, a], sibling)
 
     def c_far(k, n):
-        return remote(far_s.at[k, pl.ds(64 * n, 64)], far_r.at[k, n], far_ss.at[k], far_rs.at[k], y_up if n == 0 else y_dn)
+        return remote(far_s.at[k, pl.ds(64 * n, 64)], far_r.at[k, n], far_ss.at[k - 1], far_rs.at[k - 1], y_up if n == 0 else y_dn)
 
     def c_fin(k, n, h):
         cut = pl.ds(64 * h, 64)
-        return remote(fin_s.at[k, n, cut], fin_r.at[k, n, cut], fin_ss.at[k], fin_rs.at[k], y_up if n == 0 else y_dn)
+        return remote(fin_s.at[k, n, cut], fin_r.at[k, n, cut], fin_ss.at[k - 1], fin_rs.at[k - 1], y_up if n == 0 else y_dn)
 
     def rs_put(k, a, value):
         held(k)[a] = value.astype(BF16)
@@ -405,7 +411,7 @@
         c_fin(k, n, 1 - n).start()
 
     def rs_mid(k):
-        all_in(far_r.at[k], far_rs.at[k])
+        all_in(far_r.at[k], far_rs.at[k - 1])
         for n in (0, 1):
             cut = pl.ds(64 * n, 64)
             fin_s[k, n, cut] = (fin_s[k, n, cut].astype(F32) + far_r[k, n].astype(F32)).astype(BF16)
@@ -413,7 +419,7 @@
 
     def rs_finish(k):
         total = rs_pair(k, y)
-        all_in(fin_r.at[k], fin_rs.at[k])
+        all_in(fin_r.at[k], fin_rs.at[k - 1])
         return total + fin_r[k, 0].astype(F32) + fin_r[k, 1].astype(F32)
 
     w_zstart(0)
@@ -583,14 +589,14 @@
             src, to = terms[n].at[(x + r) % 4], dev(x + r, y, z, c)
         else:
             src, to = terms[n].at[:, (z + r) % 4], dev(x, y, z + r, c)
-        return remote(src, term_in[n].at[r - 1], f1_s.at[n], f1_r.at[n], to)
+        return remote(src, term_in[n].at[r - 1], f1_s.at[0], f1_r.at[n], to)
 
     def second(n, r):
         if n in (0, 3, 5):
             src, to = halfway[n].at[(z + r) % 4], dev(x, y, z + r, c)
         else:
             src, to = halfway[n].at[(x + r) % 4], dev(x + r, y, z, c)
-        return remote(src, half_in[n].at[r - 1], f2_s.at[n], f2_r.at[n], to)
+        return remote(src, half_in[n].at[r - 1], f2_s.at[0], f2_r.at[n], to)
 
     def first_start(n):
         for r in (1, 3, 2):
@@ -701,7 +707,7 @@
     first_sum(0)
     all_in(g_mixed.at[pl.ds(0, 896)], um_r.at[0])
     all_sent(mixed_grad.at[:, pl.ds(0, 896)], um_s.at[0])
-    all_sent(sib.at[1], sib_ss.at[1])
+    all_sent(sib.at[1], sib_ss.at[0])
     ag_start(branch_all, 3)
 
     def along_y(n, r, recv=False):
@@ -940,21 +946,19 @@
     for n in (3, 2):
         spread_finish(n)
 
-    for n in range(4):
-        all_sent(quarters(n, 3), wy_s.at[n])
-        all_sent(quarters(n, 9), wz_s.at[n])
-        all_sent(blocks(n, 4), wx_s.at[n])
+    all_sent(wo_all.at[pl.ds(0, 3 * 64)], wy_s.at[0])
+    all_sent(wo_all.at[pl.ds(0, 9 * 64)], wz_s.at[0])
+    all_sent(wo_all, wx_s.at[0])
     all_sent(wo_all.at[pl.ds(0, 448)], wp_s.at[0])
     for k, buf in enumerate((normed_all, cot_all, mlp_all, branch_all)):
         all_sent(buf.at[pl.ds(0, 896)], ag_s.at[k])
     for k in range(1, 4):
         if k > 1:
-            all_sent(sib.at[k], sib_ss.at[k])
-        all_sent(far_s.at[k], far_ss.at[k])
-        all_sent(fin_s.at[k], fin_ss.at[k])
-    for n in range(6):
-        all_sent(term_in[n], f1_s.at[n])
-        all_sent(half_in[n], f2_s.at[n])
+            all_sent(sib.at[k], sib_ss.at[k - 1])
+        all_sent(far_s.at[k], far_ss.at[k - 1])
+        all_sent(fin_s.at[k], fin_ss.at[k - 1])
+    all_sent(p_t.at[:, pl.ds(0, 624)], f1_s.at[0])
+    all_sent(p_t.at[0, pl.ds(0, 624)], f2_s.at[0])
     for n in (0, 1, 3):
         all_sent(arrays[n].at[place, c, pl.ds(0, 3)], ya_s.at[min(n, 2)])
     for n in (0, 1):
@@ -992,10 +996,10 @@
         vmem(PIECE, D), vmem(PIECE, D),
         vmem(8, 8, 128, dtype=F32), vmem(7, 8, 128, dtype=F32), vmem(8, 128, dtype=F32), vmem(7, 8, 128, dtype=F32),
         vmem(8, 128, dtype=F32), vmem(8, 128, dtype=F32),
-        dma(6), dma(5), dma(5), dma(1), dma(1), dma(4), dma(4, 3), dma(4), dma(4, 3), dma(4), dma(4),
+        dma(6), dma(5), dma(5), dma(1), dma(1), dma(1), dma(6), dma(1), dma(6), dma(1), dma(4),
         dma(1), dma(1), dma(1), dma(1), dma(1), dma(1), dma(4), dma(4, 7),
-        dma(4), dma(4, 4), dma(4), dma(4), dma(4), dma(4),
-        dma(6), dma(6), dma(6), dma(6), dma(3), dma(3), dma(2, 2), dma(2, 4), dma(2), dma(4), dma(2), dma(2),
+        dma(3), dma(3, 4), dma(3), dma(3), dma(3), dma(3),
+        dma(1), dma(6), dma(1), dma(6), dma(3), dma(3), dma(2, 2), dma(2, 4), dma(2), dma(4), dma(2), dma(2),
         dma(1), dma(1), dma(1), dma(1), dma(1), dma(1),
     ]
     anywhere = pl.BlockSpec(memory_space=pl.ANY)

time: 119 us -> 119 us (level)
  no operation moved by 1% of the time
where the time goes in v8:
time: 119 us; the launch traced here: 118 us
  Pallas kernels  118 us (99%)
    pallas_call x1, Pallas kernels, fused_layer(): pl.pallas_call(layer_kernel, out_shape=(out(PIECE, D), out(PIECE, D), out...  114 us
    pallas_call x1, Pallas kernels, spread(): pl.pallas_call(spread_kernel, out_shape=(out(PIECE, D, dtype=BF16), out(P...  3.56 us

profile of v8, /device:TPU:1, one launch (start us, length us, event | category | flops | bytes accessed | tf_op | source)
XLA Modules:
  0.0 118.5 jit_solution(8470008273396520208)
XLA Ops:
  0.7 114.1 %layer.1 = (bf16[128,1024]{1,0:T(8,128)(2,1)S(1)}, bf16[128,1024]{1,0:T(8,128)(2,1)S(1)}, bf16[8,2,4,16,768]{4,3,2,1,0:T(8,128)(2,1)S(1)}, bf16[8,2,4,48,128]{4,...) custom-call(bf16[128,1024]{1,0:T(8,128)(2,1)} %bitcast.14, ...), custom_call_target="tpu_custom_call" | custom-call | tf_op jit(solution)/shard_map/layer/pallas_call | solution.py:1011
  114.8 3.6 %spread.1 = (bf16[128,1024]{1,0:T(8,128)(2,1)}, f32[128,1024]{1,0:T(8,128)}, f32[1,128]{1,0:T(1,128)}, f32[128,1024]{1,0:T(8,128)}, f32[128,1024]{1,0:T(8,128)},...) custom-call(bf16[128,1024]{1,0:T(8,128)(2,1)S(1)} %get-tuple-element, ...), custom_call_target="tpu_custom_call" | custom-call | tf_op jit(solution)/shard_map/spread/pallas_call | solution.py:1088
